TPU v7x, 32 devices: a whole 2x2x4 slice. The times are simulated.
32 devices in a mesh: dp: 16 (over z, y, x), mp: 2 (over core).
Axes of the slice: x: 2, y: 2, z: 4, core: 2. Of those that a mesh axis runs over, the one named last changes fastest.
Arguments:
- word_inputs: bfloat16 [14336, 768], P('dp'), may hold values from -6 to 6
- entity_base: bfloat16 [2048, 768], P('dp'), may hold values from -6 to 6
- entity_ids: int32 [2048], P('dp'), may hold values from 0 to 126975
- buckets: int32 [16, 2, 16, 8], P('dp', 'mp'), may hold values from -1 to 127, as said below
- mask_positions: int32 [16, 16], P('dp'), may hold values from 0 to 127, as said below
- targets: int32 [16, 16], replicated, may hold values from 0 to 126975
- word_cotangent: bfloat16 [14336, 768], P('dp'), may hold values from -6 to 6
- attention_in: float32 [2, 6, 768, 768], P(None, None, 'dp', 'mp'), may hold values from -0.21875 to 0.21875
- attention_in_first: float32 [2, 6, 768, 768], P(None, None, 'dp', 'mp'), may hold values from -24 to 24
- attention_in_second: float32 [2, 6, 768, 768], P(None, None, 'dp', 'mp'), may hold values from 1.47456 to 5.89824
- attention_out: float32 [2, 768, 768], P(None, 'mp', 'dp'), may hold values from -4 to 4
- attention_out_first: float32 [2, 768, 768], P(None, 'mp', 'dp'), may hold values from -3 to 3
- attention_out_second: float32 [2, 768, 768], P(None, 'mp', 'dp'), may hold values from 0.0196608 to 0.0802816
- feed_up: float32 [2, 768, 3072], P(None, 'dp', 'mp'), may hold values from -0.21875 to 0.21875
- feed_up_first: float32 [2, 768, 3072], P(None, 'dp', 'mp'), may hold values from -16 to 16
- feed_up_second: float32 [2, 768, 3072], P(None, 'dp', 'mp'), may hold values from 0.65536 to 2.62144
- feed_down: float32 [2, 3072, 768], P(None, 'mp', 'dp'), may hold values from -0.109375 to 0.109375
- feed_down_first: float32 [2, 3072, 768], P(None, 'mp', 'dp'), may hold values from -40 to 40
- feed_down_second: float32 [2, 3072, 768], P(None, 'mp', 'dp'), may hold values from 3.2768 to 13.1072
- norm_params: float32 [2, 4, 768], P(None, None, 'dp'), may hold values from -0.5 to 1.5
- norm_params_first: float32 [2, 4, 768], P(None, None, 'dp'), may hold values from -64 to 64
- norm_params_second: float32 [2, 4, 768], P(None, None, 'dp'), may hold values from 8.02816 to 32.11264
- entity_proj: float32 [256, 768], P('dp'), may hold values from -2 to 2
- entity_proj_first: float32 [256, 768], P('dp'), may hold values from -1.5 to 1.5
- entity_proj_second: float32 [256, 768], P('dp'), may hold values from 0.00512 to 0.02048
- head_proj: float32 [768, 256], P('dp'), may hold values from -0.21875 to 0.21875
- head_proj_first: float32 [768, 256], P('dp'), may hold values from -0.00390625 to 0.00390625
- head_proj_second: float32 [768, 256], P('dp'), may hold values from 3.90625e-08 to 1.5625e-07
- entity_table: float32 [126976, 256], P(('dp', 'mp')), may hold values from -0.875 to 0.875
- entity_table_first: float32 [126976, 256], P(('dp', 'mp')), may hold values from -1 to 1
- entity_table_second: float32 [126976, 256], P(('dp', 'mp')), may hold values from 0 to 1, as said below
Outputs:
- loss_value: float32 [256], replicated
- word_grads: float32 [14336, 768], P('dp')
- attention_in_first_new: float32 [2, 6, 768, 768], P(None, None, 'dp', 'mp')
- attention_in_second_new: float32 [2, 6, 768, 768], P(None, None, 'dp', 'mp')
- attention_in_new: float32 [2, 6, 768, 768], P(None, None, 'dp', 'mp')
- attention_out_first_new: float32 [2, 768, 768], P(None, 'mp', 'dp')
- attention_out_second_new: float32 [2, 768, 768], P(None, 'mp', 'dp')
- attention_out_new: float32 [2, 768, 768], P(None, 'mp', 'dp')
- feed_up_first_new: float32 [2, 768, 3072], P(None, 'dp', 'mp')
- feed_up_second_new: float32 [2, 768, 3072], P(None, 'dp', 'mp')
- feed_up_new: float32 [2, 768, 3072], P(None, 'dp', 'mp')
- feed_down_first_new: float32 [2, 3072, 768], P(None, 'mp', 'dp')
- feed_down_second_new: float32 [2, 3072, 768], P(None, 'mp', 'dp')
- feed_down_new: float32 [2, 3072, 768], P(None, 'mp', 'dp')
- norm_params_first_new: float32 [2, 4, 768], P(None, None, 'dp')
- norm_params_second_new: float32 [2, 4, 768], P(None, None, 'dp')
- norm_params_new: float32 [2, 4, 768], P(None, None, 'dp')
- entity_proj_first_new: float32 [256, 768], P('dp')
- entity_proj_second_new: float32 [256, 768], P('dp')
- entity_proj_new: float32 [256, 768], P('dp')
- head_proj_first_new: float32 [768, 256], P('dp')
- head_proj_second_new: float32 [768, 256], P('dp')
- head_proj_new: float32 [768, 256], P('dp')
- entity_table_first_new: float32 [126976, 256], P(('dp', 'mp'))
- entity_table_second_new: float32 [126976, 256], P(('dp', 'mp'))
- entity_table_new: float32 [126976, 256], P(('dp', 'mp'))
Inputs may be any that keep to these rules, and one draw needn't show every extreme that they name: buckets[i, j, k, c] is -1 or an index into the 128 entity slots of dp index i; each such slot is named exactly once in buckets[i], at some j, k with its entity id // 3968 equal to 2 * k + j, so that the row it reads is its entity id. `mask_positions`: the 16 positions of a sequence are distinct. `entity_table_second`: positive.
All inputs are finite; a program needn't handle non-finite values.
Results may differ from a plain program's by a relative error of at most 0.03.
Values may be sent and summed in bfloat16 or wider, within the bound.
A program may use at most 448 MiB of HBM per device.

v0:
```python
import jax
import jax.numpy as jnp
from jax import lax
from jax.sharding import PartitionSpec as P

D = 768
HEAD_DIM = 64
WORDS = 896
ENT_LEN = 128
MASK_ENT = 16
LAYERS = 2
STEP = 10
SEQ_DEV = 1


norm_eps = 1e-05
beta_first = 0.9
beta_second = 0.999
adam_eps = 1e-12
weight_decay = 0.01
kind_rates = (0.05, 1.0, 0.05, 0.027, 0.75, 0.5, 0.05, 0.2)


def joined(x, axis, combine):
    everything = jax.tree.map(lambda part: lax.all_gather(part, axis), x)
    leading = jax.tree.map(lambda part: part[0], everything)

    def lap(k, so_far):
        return combine(so_far, jax.tree.map(lambda part: part[k], everything))

    return lax.fori_loop(1, lax.axis_size(axis), lap, leading)


def layer_norm(values, gain_row, shift_row):
    centered = values - jnp.mean(values, axis=-1, keepdims=True)
    spread = jnp.mean(centered * centered, axis=-1, keepdims=True)
    return centered * lax.rsqrt(spread + norm_eps) * gain_row + shift_row


def gelu_exact(values):
    return jax.nn.gelu(values, approximate=False)


def adam_update(master, first_moment, second_moment, gradient, kind_rate):
    first_new = beta_first * first_moment + (1.0 - beta_first) * gradient
    second_new = beta_second * second_moment + (1.0 - beta_second) * gradient * gradient
    first_hat = first_new / (1.0 - beta_first**STEP)
    second_hat = second_new / (1.0 - beta_second**STEP)
    master_new = master - kind_rate * (
        first_hat / (jnp.sqrt(second_hat) + adam_eps) + weight_decay * master
    )
    return (first_new, second_new, master_new)


def project(fetched_row_values, weight_matrix_entry):
    return jnp.einsum(
        "mvw,wu->mvu", fetched_row_values, weight_matrix_entry, preferred_element_type=jnp.float32
    )


def project_back(row_gradient_block, weight_matrix_entry):
    return jnp.einsum(
        "tic,vc->tiv", row_gradient_block, weight_matrix_entry, preferred_element_type=jnp.float32
    )


def weight_grad(layer_input_list, row_gradient_block):
    return jnp.einsum(
        "hmq,hmw->qw", layer_input_list, row_gradient_block, preferred_element_type=jnp.float32
    )


def split_heads(values):
    return values.reshape(values.shape[0], values.shape[1], values.shape[2] // HEAD_DIM, HEAD_DIM)


def merge_heads(partial_sum):
    return lax.psum(partial_sum.astype(jnp.bfloat16), "mp").astype(jnp.float32)


def merge_inputs(partial_sum):
    return lax.psum(partial_sum.astype(jnp.bfloat16), "mp").astype(jnp.float32)


def seq_scores(query_word, query_entity, key_rows):
    score_word = jnp.einsum(
        "qhd,khd->hqk", query_word, key_rows[:WORDS], preferred_element_type=jnp.float32
    )
    score_entity = jnp.einsum(
        "qhd,khd->hqk", query_entity, key_rows[WORDS:], preferred_element_type=jnp.float32
    )
    return jnp.concatenate([score_word, score_entity], axis=-1) * 0.125


def attend_forward(seq_item):
    query_word, query_entity, key_rows, value_rows = seq_item
    scores = seq_scores(query_word, query_entity, key_rows)
    peak_value = jnp.max(scores, axis=-1, keepdims=True)
    exp_scores = jnp.exp(scores - peak_value)
    exp_total = jnp.sum(exp_scores, axis=-1, keepdims=True)
    prob_low = (exp_scores / exp_total).astype(jnp.bfloat16)
    mixed_heads = jnp.einsum(
        "hqk,khd->qhd", prob_low, value_rows, preferred_element_type=jnp.float32
    )
    return (mixed_heads, (peak_value + jnp.log(exp_total))[..., 0])


def attend_backward(seq_item):
    query_word, query_entity, key_rows, value_rows, log_norm, grad_mixed = seq_item
    scores = seq_scores(query_word, query_entity, key_rows)
    prob_rows = jnp.exp(scores - log_norm[..., None])
    grad_value = jnp.einsum(
        "hqk,qhd->khd",
        prob_rows.astype(jnp.bfloat16),
        grad_mixed,
        preferred_element_type=jnp.float32,
    )
    grad_probs = jnp.einsum(
        "qhd,khd->hqk", grad_mixed, value_rows, preferred_element_type=jnp.float32
    )
    inner_sum = jnp.sum(prob_rows * grad_probs, axis=-1, keepdims=True)
    grad_scores = (prob_rows * (grad_probs - inner_sum) * 0.125).astype(jnp.bfloat16)
    score_word = grad_scores[..., :WORDS]
    score_entity = grad_scores[..., WORDS:]
    grad_qw = jnp.einsum(
        "hqk,khd->qhd", score_word, key_rows[:WORDS], preferred_element_type=jnp.float32
    )
    grad_qe = jnp.einsum(
        "hqk,khd->qhd", score_entity, key_rows[WORDS:], preferred_element_type=jnp.float32
    )
    grad_key = jnp.concatenate(
        [
            jnp.einsum("hqk,qhd->khd", score_word, query_word, preferred_element_type=jnp.float32),
            jnp.einsum(
                "hqk,qhd->khd", score_entity, query_entity, preferred_element_type=jnp.float32
            ),
        ],
        axis=0,
    )
    return (grad_qw, grad_qe, grad_key, grad_value)


def layer_forward(hidden, attn_mats, out_mat, up_mat, down_mat, gain_rows):
    hidden_low = hidden.astype(jnp.bfloat16)
    words_low = hidden_low[:, :WORDS]
    ents_low = hidden_low[:, WORDS:]
    query_word = jnp.concatenate(
        [project(words_low, attn_mats[0]), project(ents_low, attn_mats[2])], axis=1
    ).astype(jnp.bfloat16)
    query_entity = jnp.concatenate(
        [project(words_low, attn_mats[1]), project(ents_low, attn_mats[3])], axis=1
    ).astype(jnp.bfloat16)
    key_rows = project(hidden_low, attn_mats[4]).astype(jnp.bfloat16)
    value_rows = project(hidden_low, attn_mats[5]).astype(jnp.bfloat16)
    mixed_heads, log_norm = lax.map(
        attend_forward,
        (
            split_heads(query_word),
            split_heads(query_entity),
            split_heads(key_rows),
            split_heads(value_rows),
        ),
    )
    mixed_low = mixed_heads.reshape(key_rows.shape).astype(jnp.bfloat16)
    attended = merge_heads(project(mixed_low, out_mat))
    first_out = layer_norm(hidden + attended, gain_rows[0], gain_rows[1])
    first_low = first_out.astype(jnp.bfloat16)
    inner_pre = project(first_low, up_mat)
    inner_low = gelu_exact(inner_pre).astype(jnp.bfloat16)
    outer_out = merge_heads(project(inner_low, down_mat))
    result = layer_norm(first_out + outer_out, gain_rows[2], gain_rows[3])
    saved_acts = (
        hidden,
        hidden_low,
        query_word,
        query_entity,
        key_rows,
        value_rows,
        log_norm,
        mixed_low,
        attended,
        first_out,
        first_low,
        inner_pre,
        inner_low,
        outer_out,
    )
    return (result, saved_acts)


def layer_backward(grad_out, saved_acts, attn_mats, out_mat, up_mat, down_mat, gain_rows):
    (
        hidden,
        hidden_low,
        query_word,
        query_entity,
        key_rows,
        value_rows,
        log_norm,
        mixed_low,
        attended,
        first_out,
        first_low,
        inner_pre,
        inner_low,
        outer_out,
    ) = saved_acts
    second_back = jax.vjp(layer_norm, first_out + outer_out, gain_rows[2], gain_rows[3])[1]
    grad_second, grad_gain_late, grad_shift_late = second_back(grad_out)
    grad_outer = grad_second.astype(jnp.bfloat16)
    grad_down = weight_grad(inner_low, grad_outer)
    grad_inner = project_back(grad_outer, down_mat)
    grad_pre = jax.vjp(gelu_exact, inner_pre)[1](grad_inner)[0].astype(jnp.bfloat16)
    grad_up = weight_grad(first_low, grad_pre)
    grad_first = grad_second + merge_inputs(project_back(grad_pre, up_mat))
    first_back = jax.vjp(layer_norm, hidden + attended, gain_rows[0], gain_rows[1])[1]
    grad_first_in, grad_gain_early, grad_shift_early = first_back(grad_first)
    grad_attended = grad_first_in.astype(jnp.bfloat16)
    grad_out_mat = weight_grad(mixed_low, grad_attended)
    grad_mixed = project_back(grad_attended, out_mat).astype(jnp.bfloat16)
    grad_qw, grad_qe, grad_key, grad_value = lax.map(
        attend_backward,
        (
            split_heads(query_word),
            split_heads(query_entity),
            split_heads(key_rows),
            split_heads(value_rows),
            log_norm,
            split_heads(grad_mixed),
        ),
    )
    flat_shape = key_rows.shape
    grad_qw = grad_qw.reshape(flat_shape).astype(jnp.bfloat16)
    grad_qe = grad_qe.reshape(flat_shape).astype(jnp.bfloat16)
    grad_key = grad_key.reshape(flat_shape).astype(jnp.bfloat16)
    grad_value = grad_value.reshape(flat_shape).astype(jnp.bfloat16)
    words_low = hidden_low[:, :WORDS]
    ents_low = hidden_low[:, WORDS:]
    grad_mats = jnp.stack(
        [
            weight_grad(words_low, grad_qw[:, :WORDS]),
            weight_grad(words_low, grad_qe[:, :WORDS]),
            weight_grad(ents_low, grad_qw[:, WORDS:]),
            weight_grad(ents_low, grad_qe[:, WORDS:]),
            weight_grad(hidden_low, grad_key),
            weight_grad(hidden_low, grad_value),
        ]
    )
    part_words = project_back(grad_qw[:, :WORDS], attn_mats[0]) + project_back(
        grad_qe[:, :WORDS], attn_mats[1]
    )
    part_ents = project_back(grad_qw[:, WORDS:], attn_mats[2]) + project_back(
        grad_qe[:, WORDS:], attn_mats[3]
    )
    part_sum = (
        jnp.concatenate([part_words, part_ents], axis=1)
        + project_back(grad_key, attn_mats[4])
        + project_back(grad_value, attn_mats[5])
    )
    grad_hidden = grad_first_in + merge_inputs(part_sum)
    grad_norms = jnp.stack([grad_gain_early, grad_shift_early, grad_gain_late, grad_shift_late])
    return (grad_hidden, (grad_mats, grad_out_mat, grad_up, grad_down, grad_norms))


def combine_partition(left_side, right_side):
    peak_left, total_left, picked_left = left_side
    peak_right, total_right, picked_right = right_side
    peak_both = jnp.maximum(peak_left, peak_right)
    total_both = total_left * jnp.exp(peak_left - peak_both) + total_right * jnp.exp(
        peak_right - peak_both
    )
    return (peak_both, total_both, picked_left + picked_right)


def on_device(
    word_inputs,
    entity_base,
    entity_ids,
    buckets,
    mask_positions,
    targets,
    word_cotangent,
    attention_in,
    attention_in_first,
    attention_in_second,
    attention_out,
    attention_out_first,
    attention_out_second,
    feed_up,
    feed_up_first,
    feed_up_second,
    feed_down,
    feed_down_first,
    feed_down_second,
    norm_params,
    norm_params_first,
    norm_params_second,
    entity_proj,
    entity_proj_first,
    entity_proj_second,
    head_proj,
    head_proj_first,
    head_proj_second,
    entity_table,
    entity_table_first,
    entity_table_second,
):
    gathered = (
        lax.all_gather(attention_in.astype(jnp.bfloat16), "dp", axis=2, tiled=True),
        lax.all_gather(attention_out.astype(jnp.bfloat16), "dp", axis=2, tiled=True),
        lax.all_gather(feed_up.astype(jnp.bfloat16), "dp", axis=1, tiled=True),
        lax.all_gather(feed_down.astype(jnp.bfloat16), "dp", axis=2, tiled=True),
        lax.all_gather(norm_params.astype(jnp.bfloat16), "dp", axis=2, tiled=True),
        lax.all_gather(entity_proj.astype(jnp.bfloat16), "dp", axis=0, tiled=True),
        lax.all_gather(head_proj.astype(jnp.bfloat16), "dp", axis=0, tiled=True),
    )
    attn_low, out_low, up_low, down_low, norm_low, proj_low, head_low = gathered
    gain_all = norm_low.astype(jnp.float32)
    slot_total = entity_ids.shape[0]
    shard_rows = entity_table.shape[0]
    bucket_rows = buckets.reshape(buckets.shape[2], buckets.shape[3])
    filled = bucket_rows >= 0
    safe_slot = jnp.maximum(bucket_rows, 0)
    request = jnp.where(filled, entity_ids[safe_slot] % shard_rows, -1)
    received = lax.all_to_all(request, "dp", split_axis=0, concat_axis=0, tiled=True)
    shard_base = lax.axis_index(("dp", "mp")) * shard_rows
    owned_mask = received >= 0
    safe_row = jnp.clip(received, 0, shard_rows - 1)
    table_low = entity_table.astype(jnp.bfloat16)
    replies = jnp.where(owned_mask[:, :, None], table_low[safe_row], jnp.zeros((), jnp.bfloat16))
    replied_rows_result = lax.all_to_all(replies, "dp", split_axis=0, concat_axis=0, tiled=True)
    row_placement_plan = (
        bucket_rows[:, :, None] == jnp.arange(slot_total, dtype=jnp.int32)[None, None, :]
    ).astype(jnp.bfloat16)
    local_shard_rows = jnp.einsum(
        "wvt,wvi->ti", row_placement_plan, replied_rows_result, preferred_element_type=jnp.float32
    )
    paired = lax.psum(local_shard_rows.astype(jnp.bfloat16), "mp").astype(jnp.float32)
    masked_slots = (
        jnp.arange(SEQ_DEV, dtype=jnp.int32)[:, None] * ENT_LEN + mask_positions
    ).reshape(-1)
    keep_weight = 1.0 - jnp.any(
        jnp.arange(slot_total, dtype=jnp.int32)[:, None] == masked_slots[None, :], axis=1
    ).astype(jnp.float32)
    entity_rows = (paired * keep_weight[:, None]).astype(jnp.bfloat16)
    entity_inputs = entity_base.astype(jnp.float32) + jnp.dot(
        entity_rows, proj_low, preferred_element_type=jnp.float32
    )
    hidden = jnp.concatenate(
        [
            word_inputs.astype(jnp.float32).reshape(SEQ_DEV, WORDS, D),
            entity_inputs.reshape(SEQ_DEV, ENT_LEN, D),
        ],
        axis=1,
    )
    saved_layers = []
    for layer_index in range(LAYERS):
        hidden, saved_acts = layer_forward(
            hidden,
            attn_low[layer_index],
            out_low[layer_index],
            up_low[layer_index],
            down_low[layer_index],
            gain_all[layer_index],
        )
        saved_layers.append(saved_acts)
    seq_index = jnp.arange(SEQ_DEV, dtype=jnp.int32)[:, None]
    masked_rows = WORDS + mask_positions
    masked_low = hidden[seq_index, masked_rows].reshape(SEQ_DEV * MASK_ENT, D).astype(jnp.bfloat16)
    head_pre = jnp.dot(masked_low, head_low, preferred_element_type=jnp.float32)
    states_low = gelu_exact(head_pre).astype(jnp.bfloat16)
    all_states = lax.all_gather(states_low, "dp", axis=0, tiled=True)
    logits = lax.dot_general(
        all_states, table_low, (((1,), (1,)), ((), ())), preferred_element_type=jnp.float32
    )
    flat_targets = targets.reshape(-1)
    target_hits = (
        jnp.arange(shard_rows, dtype=jnp.int32)[None, :] == (flat_targets - shard_base)[:, None]
    )
    peak_value = jnp.max(logits, axis=1)
    exp_total = jnp.sum(jnp.exp(logits - peak_value[:, None]), axis=1)
    picked = jnp.sum(jnp.where(target_hits, logits, 0.0), axis=1)
    peak_all, total_all, picked_all = joined(
        (peak_value, exp_total, picked), ("dp", "mp"), combine_partition
    )
    log_norm = peak_all + jnp.log(total_all)
    row_losses = log_norm - picked_all
    prob_rows = jnp.exp(logits - log_norm[:, None])
    grad_logits = ((prob_rows - target_hits.astype(jnp.float32)) / flat_targets.shape[0]).astype(
        jnp.bfloat16
    )
    grad_table = lax.dot_general(
        grad_logits, all_states, (((0,), (0,)), ((), ())), preferred_element_type=jnp.float32
    )
    grad_share = lax.psum_scatter(
        jnp.dot(grad_logits, table_low, preferred_element_type=jnp.float32),
        ("dp", "mp"),
        scatter_dimension=0,
        tiled=True,
    )
    grad_states = lax.all_gather(grad_share, "mp", axis=0, tiled=True)
    grad_head_pre = jax.vjp(gelu_exact, head_pre)[1](grad_states)[0].astype(jnp.bfloat16)
    grad_head = lax.dot_general(
        masked_low, grad_head_pre, (((0,), (0,)), ((), ())), preferred_element_type=jnp.float32
    )
    grad_masked = lax.dot_general(
        grad_head_pre, head_low, (((1,), (1,)), ((), ())), preferred_element_type=jnp.float32
    )
    grad_hidden = jnp.concatenate(
        [
            word_cotangent.astype(jnp.float32).reshape(SEQ_DEV, WORDS, D),
            jnp.zeros((SEQ_DEV, ENT_LEN, D), jnp.float32),
        ],
        axis=1,
    )
    grad_hidden = grad_hidden.at[seq_index, masked_rows].add(
        grad_masked.reshape(SEQ_DEV, MASK_ENT, D)
    )
    kept_grads = []
    for layer_index in reversed(range(LAYERS)):
        grad_hidden, layer_grads = layer_backward(
            grad_hidden,
            saved_layers[layer_index],
            attn_low[layer_index],
            out_low[layer_index],
            up_low[layer_index],
            down_low[layer_index],
            gain_all[layer_index],
        )
        if layer_index == 0:
            word_grads = grad_hidden[:, :WORDS].reshape(SEQ_DEV * WORDS, D)
            grad_entity = grad_hidden[:, WORDS:].reshape(slot_total, D).astype(jnp.bfloat16)
            grad_proj = lax.dot_general(
                entity_rows,
                grad_entity,
                (((0,), (0,)), ((), ())),
                preferred_element_type=jnp.float32,
            )
            row_gradient_block = (
                lax.dot_general(
                    grad_entity,
                    proj_low,
                    (((1,), (1,)), ((), ())),
                    preferred_element_type=jnp.float32,
                )
                * keep_weight[:, None]
            )
            outgoing = jnp.where(filled[:, :, None], row_gradient_block[safe_slot], 0.0)
            incoming = lax.all_to_all(
                outgoing.astype(jnp.bfloat16), "dp", split_axis=0, concat_axis=0, tiled=True
            ).astype(outgoing.dtype)
            grad_table = grad_table.at[safe_row].add(
                jnp.where(owned_mask[:, :, None], incoming, 0.0)
            )
        kept_grads.insert(0, layer_grads)
    stacked = tuple(
        (
            jnp.stack([kept_grads[layer_index][member_index] for layer_index in range(LAYERS)])
            for member_index in range(5)
        )
    )
    summed = (
        lax.psum_scatter(stacked[0], "dp", scatter_dimension=2, tiled=True),
        lax.psum_scatter(stacked[1], "dp", scatter_dimension=2, tiled=True),
        lax.psum_scatter(stacked[2], "dp", scatter_dimension=1, tiled=True),
        lax.psum_scatter(stacked[3], "dp", scatter_dimension=2, tiled=True),
        lax.psum_scatter(stacked[4], "dp", scatter_dimension=2, tiled=True),
        lax.psum_scatter(grad_proj, "dp", scatter_dimension=0, tiled=True),
        lax.psum_scatter(grad_head, "dp", scatter_dimension=0, tiled=True),
    )
    reduced = summed[:5]
    reduced_proj = summed[5]
    reduced_head = summed[6]
    attn_new = adam_update(
        attention_in, attention_in_first, attention_in_second, reduced[0], kind_rates[0]
    )
    out_new = adam_update(
        attention_out, attention_out_first, attention_out_second, reduced[1], kind_rates[1]
    )
    up_new = adam_update(feed_up, feed_up_first, feed_up_second, reduced[2], kind_rates[2])
    down_new = adam_update(feed_down, feed_down_first, feed_down_second, reduced[3], kind_rates[3])
    norm_new = adam_update(
        norm_params, norm_params_first, norm_params_second, reduced[4], kind_rates[4]
    )
    proj_new = adam_update(
        entity_proj, entity_proj_first, entity_proj_second, reduced_proj, kind_rates[5]
    )
    head_new = adam_update(
        head_proj, head_proj_first, head_proj_second, reduced_head, kind_rates[6]
    )
    table_new = adam_update(
        entity_table, entity_table_first, entity_table_second, grad_table, kind_rates[7]
    )
    return (
        row_losses,
        word_grads,
        attn_new[0],
        attn_new[1],
        attn_new[2],
        out_new[0],
        out_new[1],
        out_new[2],
        up_new[0],
        up_new[1],
        up_new[2],
        down_new[0],
        down_new[1],
        down_new[2],
        norm_new[0],
        norm_new[1],
        norm_new[2],
        proj_new[0],
        proj_new[1],
        proj_new[2],
        head_new[0],
        head_new[1],
        head_new[2],
        table_new[0],
        table_new[1],
        table_new[2],
    )


def solution(mesh):
    in_specs = (
        P("dp", None),
        P("dp", None),
        P("dp"),
        P("dp", "mp", None, None),
        P("dp", None),
        P(),
        P("dp", None),
        P(None, None, "dp", "mp"),
        P(None, None, "dp", "mp"),
        P(None, None, "dp", "mp"),
        P(None, "mp", "dp"),
        P(None, "mp", "dp"),
        P(None, "mp", "dp"),
        P(None, "dp", "mp"),
        P(None, "dp", "mp"),
        P(None, "dp", "mp"),
        P(None, "mp", "dp"),
        P(None, "mp", "dp"),
        P(None, "mp", "dp"),
        P(None, None, "dp"),
        P(None, None, "dp"),
        P(None, None, "dp"),
        P("dp", None),
        P("dp", None),
        P("dp", None),
        P("dp", None),
        P("dp", None),
        P("dp", None),
        P(("dp", "mp"), None),
        P(("dp", "mp"), None),
        P(("dp", "mp"), None),
    )
    out_specs = (
        P(),
        P("dp", None),
        P(None, None, "dp", "mp"),
        P(None, None, "dp", "mp"),
        P(None, None, "dp", "mp"),
        P(None, "mp", "dp"),
        P(None, "mp", "dp"),
        P(None, "mp", "dp"),
        P(None, "dp", "mp"),
        P(None, "dp", "mp"),
        P(None, "dp", "mp"),
        P(None, "mp", "dp"),
        P(None, "mp", "dp"),
        P(None, "mp", "dp"),
        P(None, None, "dp"),
        P(None, None, "dp"),
        P(None, None, "dp"),
        P("dp", None),
        P("dp", None),
        P("dp", None),
        P("dp", None),
        P("dp", None),
        P("dp", None),
        P(("dp", "mp"), None),
        P(("dp", "mp"), None),
        P(("dp", "mp"), None),
    )
    return jax.shard_map(
        on_device, mesh=mesh, in_specs=in_specs, out_specs=out_specs, check_vma=False
    )
```

profile of v0, /device:TPU:0, one launch (start us, length us, event | category | flops | bytes accessed | tf_op | source)
XLA Modules:
  0.0 2365.6 jit_solution(3553898274114699065)
XLA Ops:
  41.3 40.1 %all_gather.45 = bf16[256,768]{1,0:T(8,128)(2,1)S(1)} all-gather(bf16[16,768]{1,0:T(8,128)(2,1)S(1)} %convert_element_type.418), channel_id=1, replica_groups=mesh['dp'=16,'mp'=2] {'dp'}, dimensions={0}, use_global_device_ids=true | all-gather | bytes 417792 | tf_op jit(solution)/shard_map/all_gather | solution.py:314
  86.6 55.9 %all-gather.11.cloned.1.call-done = bf16[2,6,768,384]{3,2,1,0:T(8,128)(2,1)} async-done(((bf16[2,6,48,384]{3,2,1,0:T(8,128)(2,1)}), bf16[2,6,768,384]{3,2,1,0:T(8,128)(2,1)}) %all-gather.11.cloned.1.call-update) | async-done | bytes 7077904 | tf_op jit(solution)/shard_map/all_gather | solution.py:309
  205.4 42.0 %all_gather.48 = bf16[2,4,768]{1,0,2:T(2,128)(2,1)S(1)} all-gather(bf16[2,4,48]{1,0,2:T(2,128)(2,1)S(1)} %copy.303), channel_id=1, replica_groups=mesh['dp'=16,'mp'=2] {'dp'}, dimensions={2}, use_global_device_ids=true | all-gather | bytes 13056 | tf_op jit(solution)/shard_map/all_gather | solution.py:313
  247.7 21.2 slice_reduce_fusion.1
  272.1 15.6 all-gather.15.cloned.1.call-done
  287.7 20.2 multiply_convert_fusion.3
  307.9 62.0 %all-gather.17.cloned.1.call-done = bf16[2,1536,768]{1,2,0:T(8,128)(2,1)} async-done(((bf16[2,1536,48]{1,2,0:T(8,128)(2,1)}), bf16[2,1536,768]{1,2,0:T(8,128)(2,1)}) %all-gather.17.cloned.1.call-update) | async-done | bytes 4718608 | tf_op jit(solution)/shard_map/all_gather | solution.py:312
  381.0 14.7 all-reduce.20.cloned.1.call-done
  427.5 11.8 fusion.130
  442.9 21.7 all-reduce.22.cloned.1.call-done
  467.9 20.3 multiply_convert_fusion.2
  494.6 43.2 %all_gather.51 = bf16[768,256]{1,0:T(8,128)(2,1)S(1)} all-gather(bf16[48,256]{1,0:T(8,128)(2,1)S(1)} %convert_element_type.459), channel_id=1, replica_groups=mesh['dp'=16,'mp'=2] {'dp'}, dimensions={0}, use_global_device_ids=true | all-gather | bytes 417792 | tf_op jit(solution)/shard_map/all_gather | solution.py:315
  547.7 36.3 %all_gather.52 = bf16[256,256]{1,0:T(8,128)(2,1)S(1)} all-gather(bf16[16,256]{1,0:T(8,128)(2,1)S(1)} %get-tuple-element.518), channel_id=1, replica_groups=mesh['dp'=16,'mp'=2] {'dp'}, dimensions={0}, use_global_device_ids=true | all-gather | bytes 139264 | tf_op jit(solution)/shard_map/all_gather | solution.py:372
  590.4 38.4 %all-gather.4 = f32[32,1,256]{2,1,0:T(1,128)S(1)} all-gather(f32[1,1,256]{2,1,0:T(1,128)S(1)} %bitcast.593), channel_id=3, replica_groups=mesh['dp'=16,'mp'=2] {'dp','mp'}, dimensions={0}, use_global_device_ids=true | all-gather | bytes 33792 | tf_op jit(solution)/shard_map/all_gather | solution.py:25
  630.0 36.6 %all-gather.5 = f32[32,1,256]{2,1,0:T(1,128)S(1)} all-gather(f32[1,1,256]{2,1,0:T(1,128)S(1)} %bitcast.592), channel_id=4, replica_groups=mesh['dp'=16,'mp'=2] {'dp','mp'}, dimensions={0}, use_global_device_ids=true | all-gather | bytes 33792 | tf_op jit(solution)/shard_map/all_gather | solution.py:25
  667.8 38.0 %all-gather.3 = f32[32,1,256]{2,1,0:T(1,128)S(1)} all-gather(f32[1,1,256]{2,1,0:T(1,128)S(1)} %bitcast.591), channel_id=2, replica_groups=mesh['dp'=16,'mp'=2] {'dp','mp'}, dimensions={0}, use_global_device_ids=true | all-gather | bytes 33792 | tf_op jit(solution)/shard_map/all_gather | solution.py:25
  707.0 122.7 %while.12 = (s32[]{:T(128)}, f32[256]{0:T(256)}, f32[256]{0:T(256)}, f32[256]{0:T(256)}, f32[32,256]{1,0:T(8,128)}, /*index=5*/f32[32,256]{1,0:T(8,128)}, f32[32,256]{1,0:T(8,128)}, s32[]{:T(128)}, s32[]{:T(128)}, s32[]{:T(128)}) while((s32[]{:T(128)}, f32[256]{0:T(256)}, f32[256]{0:T(256)}, f32[256]{0:T(256)}, f32[32,256]{1,0:T(8,128)}, ...), condition=%wide.region_22.23_spmd, body=%wide.region_21.22_spmd.sunk | while | flops 1797 | bytes 15503 | solution.py:31
  840.6 126.4 %reduce-scatter.9.cloned.1.call-done = f32[8,256]{1,0:T(8,128)} async-done(((f32[256,256]{1,0:T(8,128)}), f32[8,256]{1,0:T(8,128)}) %reduce-scatter.9.cloned.1.call-update) | async-done | bytes 8208 | tf_op jit(solution)/shard_map/reduce_scatter | solution.py:395
  996.2 16.2 all-reduce.26.cloned.1.call-done
  1023.3 11.6 fusion.122
  1034.9 28.1 %multiply_convert_fusion.1 = bf16[6,1024,1024]{1,2,0:T(8,128)(2,1)} fusion(f32[6,1024]{1,0:T(8,128)S(1)} %log_add_fusion.1, bf16[1024,6,64]{0,2,1:T(8,128)(2,1)} %bitcast.614, bf16[1024,6,64]{0,2,1:T(8,128)(2,1)} %bitcast.610, f32[6,1024,128]{1,2,0:T(8,128)} %copy-done.13, f32[6,1024,896]{1,2,0:T(8,128)} %copy-done.3), kind=kOutput, calls=%fused_computation.18 | convolution fusion | flops 1679825920 | bytes 39346176 | tf_op jit(solution)/shard_map/while/body/eval_jaxpr/sub | solution.py:122
  1087.9 21.7 all-reduce.28.cloned.1.call-done
  1129.5 21.6 all-reduce.30.cloned.1.call-done
  1160.5 11.6 fusion.125
  1172.1 28.1 %multiply_convert_fusion = bf16[6,1024,1024]{1,2,0:T(8,128)(2,1)} fusion(f32[6,1024]{1,0:T(8,128)S(1)} %log_add_fusion, bf16[1024,6,64]{0,2,1:T(8,128)(2,1)} %bitcast.612, bf16[1024,6,64]{0,2,1:T(8,128)(2,1)} %bitcast.606, f32[6,1024,128]{1,2,0:T(8,128)} %copy-done.12, f32[6,1024,896]{1,2,0:T(8,128)} %copy-done.2), kind=kOutput, calls=%fused_computation.14 | convolution fusion | flops 1679825920 | bytes 39346176 | tf_op jit(solution)/shard_map/while/body/eval_jaxpr/sub | solution.py:122
  1264.9 14.9 copy.323
  1338.8 16.2 reduce-scatter.17.cloned.1.call-done
  1356.4 125.1 %reduce-scatter.19.cloned.1.call-done = f32[48,8]{1,0:T(8,128)} async-done(((f32[768,8]{1,0:T(8,128)}), f32[48,8]{1,0:T(8,128)}) %reduce-scatter.19.cloned.1.call-update) | async-done | bytes 1552
  1515.3 92.5 %reduce-scatter.15.cloned.1.call-done = f32[16,768]{1,0:T(8,128)} async-done(((f32[256,768]{1,0:T(8,128)}), f32[16,768]{1,0:T(8,128)}) %reduce-scatter.15.cloned.1.call-update) | async-done | bytes 49168 | tf_op jit(solution)/shard_map/reduce_scatter | solution.py:468
  1609.3 342.8 %all-reduce.34.cloned.1.call-done = (f32[2,384,768]{1,0,2:T(2,128)}, f32[2,1536,768]{1,0,2:T(2,128)}) async-done(((f32[2,384,768]{1,0,2:T(2,128)}, f32[2,1536,768]{1,0,2:T(2,128)}), (f32[2,384,768]{1,0,2:T(2,128)}, f32[2,1536,768]{1,0,2:T(2,128)})) %all-reduce.34.cloned.1.call-update) | async-done | bytes 11796496
  1957.8 170.3 %reduce-scatter.13.cloned.1.call-done = f32[2,48,1536]{2,1,0:T(8,128)} async-done(((f32[2,768,1536]{2,1,0:T(8,128)}), f32[2,48,1536]{2,1,0:T(8,128)}) %reduce-scatter.13.cloned.1.call-update) | async-done | bytes 589840 | tf_op jit(solution)/shard_map/reduce_scatter | solution.py:465
  2131.1 223.4 %reduce-scatter.11.cloned.1.call-done = f32[2,6,48,384]{3,2,1,0:T(8,128)} async-done(((f32[2,6,768,384]{3,2,1,0:T(8,128)}), f32[2,6,48,384]{3,2,1,0:T(8,128)}) %reduce-scatter.11.cloned.1.call-update) | async-done | bytes 884752 | tf_op jit(solution)/shard_map/reduce_scatter | solution.py:463
  (789 shorter events, 577.9 us)
Async XLA Ops:
  11.1 15.5 all-to-all-start
  19.4 63.6 %all-reduce.16.cloned.1.call-start = ((), (), s32[]{:S(2)}) async-start(), calls=%async_computation.9 | async-start | bytes 131072 | tf_op jit(solution)/shard_map/psum | solution.py:338
  39.5 103.0 %all-gather.11.cloned.1.call-start = ((), (), s32[]{:S(2)}) async-start(), calls=%async_computation.10 | async-start | bytes 7520256 | tf_op jit(solution)/shard_map/all_gather | solution.py:309
  40.4 159.7 %all-gather.13.cloned.1.call-start = ((), (), s32[]{:S(2)}) async-start(), calls=%async_computation.11 | async-start | bytes 1253376 | tf_op jit(solution)/shard_map/all_gather | solution.py:310
  41.1 227.8 %all-reduce.18.cloned.1.call-start = ((), (), s32[]{:S(2)}) async-start(), calls=%async_computation.12 | async-start | bytes 3145728 | tf_op jit(solution)/shard_map/psum | solution.py:78
  203.6 84.1 %all-gather.15.cloned.1.call-start = ((), (), s32[]{:S(2)}) async-start(), calls=%async_computation.13 | async-start | bytes 5013504 | tf_op jit(solution)/shard_map/all_gather | solution.py:311
  204.4 165.5 %all-gather.17.cloned.1.call-start = ((), (), s32[]{:S(2)}) async-start(), calls=%async_computation.14 | async-start | bytes 5013504 | tf_op jit(solution)/shard_map/all_gather | solution.py:312
  205.2 190.4 %all-reduce.20.cloned.1.call-start = ((), (), s32[]{:S(2)}) async-start(), calls=%async_computation.15 | async-start | bytes 3145728 | tf_op jit(solution)/shard_map/psum | solution.py:78
  376.4 88.2 %all-reduce.22.cloned.1.call-start = ((), (), s32[]{:S(2)}) async-start(), calls=%async_computation.16 | async-start | bytes 3145728 | tf_op jit(solution)/shard_map/psum | solution.py:78
  442.8 95.4 %all-reduce.24.cloned.1.call-start = ((), (), s32[]{:S(2)}) async-start(), calls=%async_computation.17 | async-start | bytes 3145728 | tf_op jit(solution)/shard_map/psum | solution.py:78
  467.2 550.1 %copy-start.113 = (f32[1024]{0:T(1024)}, f32[1024]{0:T(1024)S(1)}, u32[]{:S(2)}) copy-start(f32[1024]{0:T(1024)S(1)} %broadcast_multiply_fusion.1) | copy-start | bytes 12292
  493.8 473.2 %reduce-scatter.9.cloned.1.call-start = ((), (), s32[]{:S(2)}) async-start(), calls=%async_computation.18 | async-start | bytes 270336 | tf_op jit(solution)/shard_map/reduce_scatter | solution.py:395
  837.4 175.1 %all-reduce.26.cloned.1.call-start = ((), (), s32[]{:S(2)}) async-start(), calls=%async_computation.19 | async-start | bytes 3145728 | tf_op jit(solution)/shard_map/psum | solution.py:82
  995.9 113.7 %all-reduce.28.cloned.1.call-start = ((), (), s32[]{:S(2)}) async-start(), calls=%async_computation.20 | async-start | bytes 3145728 | tf_op jit(solution)/shard_map/psum | solution.py:82
  1087.8 63.3 %all-reduce.30.cloned.1.call-start = ((), (), s32[]{:S(2)}) async-start(), calls=%async_computation.21 | async-start | bytes 3145728 | tf_op jit(solution)/shard_map/psum | solution.py:82
  1129.4 117.4 %all-reduce.32.cloned.1.call-start = ((), (), s32[]{:S(2)}) async-start(), calls=%async_computation.22 | async-start | bytes 3145728 | tf_op jit(solution)/shard_map/psum | solution.py:82
  1225.0 130.0 %reduce-scatter.17.cloned.1.call-start = ((), (), s32[]{:S(2)}) async-start(), calls=%async_computation.26 | async-start | bytes 835584 | tf_op jit(solution)/shard_map/reduce_scatter | solution.py:469
  1226.3 255.2 %reduce-scatter.19.cloned.1.call-start = ((), (), s32[]{:S(2)}) async-start(), calls=%async_computation.27 | async-start | bytes 417792
  1242.4 365.3 %reduce-scatter.15.cloned.1.call-start = ((), (), s32[]{:S(2)}) async-start(), calls=%async_computation.25 | async-start | bytes 835584 | tf_op jit(solution)/shard_map/reduce_scatter | solution.py:468
  1252.4 699.6 %all-reduce.34.cloned.1.call-start = ((), (), s32[]{:S(2)}) async-start(), calls=%async_computation.28 | async-start | bytes 23592960
  1289.9 838.2 %reduce-scatter.13.cloned.1.call-start = ((), (), s32[]{:S(2)}) async-start(), calls=%async_computation.24 | async-start | bytes 10027008 | tf_op jit(solution)/shard_map/reduce_scatter | solution.py:465
  1304.3 1050.2 %reduce-scatter.11.cloned.1.call-start = ((), (), s32[]{:S(2)}) async-start(), calls=%async_computation.23 | async-start | bytes 15040512 | tf_op jit(solution)/shard_map/reduce_scatter | solution.py:463
  1485.9 12.2 all-to-all-start.2
  1503.9 450.2 %copy-start.86 = (f32[2,384,48]{1,2,0:T(8,128)S(1)}, f32[2,384,48]{1,2,0:T(8,128)}, u32[]{:S(2)}) copy-start(f32[2,384,48]{1,2,0:T(8,128)} %param.43) | copy-start | bytes 442372
  1503.9 450.2 %copy-start.106 = (f32[2,384,48]{1,2,0:T(8,128)S(1)}, f32[2,384,48]{1,2,0:T(8,128)}, u32[]{:S(2)}) copy-start(f32[2,384,48]{1,2,0:T(8,128)} %param.45) | copy-start | bytes 442372
  1504.0 450.2 %copy-start.107 = (f32[2,384,48]{1,2,0:T(8,128)S(1)}, f32[2,384,48]{1,2,0:T(8,128)}, u32[]{:S(2)}) copy-start(f32[2,384,48]{1,2,0:T(8,128)} %param.44) | copy-start | bytes 442372
  1515.3 439.7 %copy-start.57 = (f32[2,1536,48]{1,2,0:T(8,128)S(1)}, f32[2,1536,48]{1,2,0:T(8,128)}, u32[]{:S(2)}) copy-start(f32[2,1536,48]{1,2,0:T(8,128)} %param.49) | copy-start | bytes 1769476
  1515.3 439.7 %copy-start.87 = (f32[2,1536,48]{1,2,0:T(8,128)S(1)}, f32[2,1536,48]{1,2,0:T(8,128)}, u32[]{:S(2)}) copy-start(f32[2,1536,48]{1,2,0:T(8,128)} %param.51) | copy-start | bytes 1769476
  1953.0 175.2 %copy-start.59 = (f32[2,48,1536]{2,1,0:T(8,128)S(1)}, f32[2,48,1536]{2,1,0:T(8,128)}, u32[]{:S(2)}) copy-start(f32[2,48,1536]{2,1,0:T(8,128)} %param.46) | copy-start | bytes 1769476
  1955.0 399.5 %copy-start.39 = (f32[2,6,48,384]{3,2,1,0:T(8,128)S(1)}, f32[2,6,48,384]{3,2,1,0:T(8,128)}, u32[]{:S(2)}) copy-start(f32[2,6,48,384]{3,2,1,0:T(8,128)} %param.40) | copy-start | bytes 2654212
  1955.0 399.5 %copy-start.72 = (f32[2,6,48,384]{3,2,1,0:T(8,128)S(1)}, f32[2,6,48,384]{3,2,1,0:T(8,128)}, u32[]{:S(2)}) copy-start(f32[2,6,48,384]{3,2,1,0:T(8,128)} %param.42) | copy-start | bytes 2654212
  2128.1 229.8 %copy-start.1 = (s32[128]{0:T(128)S(1)}, s32[128]{0:T(128)}, u32[]{:S(2)}) copy-start(s32[128]{0:T(128)} %param.35) | copy-start | bytes 1540
  (185 other events, 3115.5 us)
Sparse Core Ops, SparseCore 0:
  39.6 14.3 all-reduce.15
  203.7 19.1 all-reduce.17
  376.5 19.0 all-reduce.19
  443.0 21.5 all-reduce.21
  493.9 21.5 all-reduce.23
  837.5 129.5 reduce-scatter.8
  996.0 16.3 all-reduce.25
  1088.0 21.5 all-reduce.27
  1129.5 21.5 all-reduce.29
  1225.1 21.5 all-reduce.31
Sparse Core Ops, SparseCore 1:
  43.2 99.2 all-gather.10
  145.6 54.4 all-gather.12
  207.7 79.9 all-gather.14
  291.3 78.5 all-gather.16
  1231.2 123.7 reduce-scatter.16
  1360.9 120.5 reduce-scatter.18
  1486.0 121.7 reduce-scatter.14
  1614.1 337.9 all-reduce.33
  1958.5 169.5 reduce-scatter.12
  2133.9 220.5 reduce-scatter.10
where the time goes:
time: 2380 us; the launch traced here: 2370 us
  waiting for transfers between devices  1340 us (56%)
  matrix products  330 us (14%)
  blocking collectives  287 us (12%)
  other arithmetic  218 us (9%)
  local copies, waits for them, and re-layouts  153 us (6%)
    unnamed x22, waiting for transfers between devices  468 us
    reduce_scatter x1, waiting for transfers between devices, on_device(): lax.psum_scatter(stacked[0], 'dp', scatter_dimension=2, tiled=True)  223 us
    reduce_scatter x1, waiting for transfers between devices, on_device(): lax.psum_scatter(stacked[2], 'dp', scatter_dimension=1, tiled=True)  170 us
    reduce_scatter x1, waiting for transfers between devices, on_device(): lax.psum_scatter(jnp.dot(grad_logits, table_low, preferred_element_type=j...  126 us
    all_gather x3, blocking collectives, joined(): everything = jax.tree.map(lambda part: lax.all_gather(part, axis), x)  113 us
    reduce_scatter x1, waiting for transfers between devices, on_device(): lax.psum_scatter(grad_proj, 'dp', scatter_dimension=0, tiled=True)  92.5 us
    dot_general x18, matrix products, project(): jnp.einsum('mvw,wu->mvu', fetched_row_values, weight_matrix_entry, prefer...  77.9 us
    psum x4, waiting for transfers between devices, merge_inputs(): return lax.psum(partial_sum.astype(jnp.bfloat16), 'mp').astype(jnp.float32)  63.8 us
  transfers between devices with their start and end apart: 22, of which 19 were waited for; matrix products, arithmetic and copies ran while one was open for 11% of the time, Pallas kernels for 0%

commit v1 on v0

--- a/solution.py
+++ b/solution.py
@@ -1,6 +1,10 @@
+import functools
+
 import jax
 import jax.numpy as jnp
 from jax import lax
+from jax.experimental import pallas as pl
+from jax.experimental.pallas import tpu as pltpu
 from jax.sharding import PartitionSpec as P
 
 D = 768
@@ -21,14 +25,301 @@
 kind_rates = (0.05, 1.0, 0.05, 0.027, 0.75, 0.5, 0.05, 0.2)
 
 
-def joined(x, axis, combine):
-    everything = jax.tree.map(lambda part: lax.all_gather(part, axis), x)
-    leading = jax.tree.map(lambda part: part[0], everything)
-
-    def lap(k, so_far):
-        return combine(so_far, jax.tree.map(lambda part: part[k], everything))
-
-    return lax.fori_loop(1, lax.axis_size(axis), lap, leading)
+MESH = pl.DeviceIdType.MESH
+ANY = pl.BlockSpec(memory_space=pl.ANY)
+VMEM = pl.BlockSpec(memory_space=pltpu.VMEM)
+VMEM_BYTES = 60 * 2**20
+
+
+def chip_grid(n_dp):
+    return {16: (4, 2, 2), 64: (4, 4, 4)}.get(n_dp, (n_dp, 1, 1))
+
+
+def place(dims):
+    index = lax.axis_index("dp")
+    return index // (dims[1] * dims[2]), index // dims[2] % dims[1], index % dims[2]
+
+
+def axis_peers(dims, axis):
+    here = place(dims)
+    core = lax.axis_index("mp")
+    peers = []
+    for step in range(1, dims[axis]):
+        spot = list(here)
+        spot[axis] = lax.rem(here[axis] + step, dims[axis])
+        peers.append((spot[axis], (spot[0] * dims[1] * dims[2] + spot[1] * dims[2] + spot[2], core)))
+    return peers
+
+
+def greet(targets):
+    barrier = pltpu.get_barrier_semaphore()
+    for target in targets:
+        pl.semaphore_signal(barrier, inc=1, device_id=target, device_id_type=MESH)
+    pl.semaphore_wait(barrier, len(targets))
+
+
+def send(src, dst, send_sem, recv_sem, target):
+    copy = pltpu.make_async_remote_copy(
+        src_ref=src,
+        dst_ref=dst,
+        send_sem=send_sem,
+        recv_sem=recv_sem,
+        device_id=target,
+        device_id_type=MESH,
+    )
+    copy.start()
+    return copy
+
+
+def gather_body(dims, chunks, count, *refs):
+    shards, wholes = refs[:count], refs[count : 2 * count]
+    send_sem, recv_sem, local_sem = refs[2 * count :]
+    z, y, x = place(dims)
+    peers = [axis_peers(dims, axis) for axis in range(3)]
+    greet([target for group in peers for _, target in group])
+    pending = {}
+
+    def start(stage, c):
+        which, first, size, y_first = chunks[c]
+        rows = pl.ds(first, size)
+        whole = wholes[which]
+        copies = []
+        if stage == 0:
+            src, dst, group = shards[which].at[rows], whole.at[rows, z, y, x], peers[0]
+            own = pltpu.make_async_copy(src, dst, local_sem.at[c])
+            own.start()
+            copies.append(own)
+        elif stage == 1:
+            src = whole.at[rows, :, y, x]
+            dst, group = src, peers[1 if y_first else 2]
+        else:
+            src = whole.at[rows, :, :, x] if y_first else whole.at[rows, :, y]
+            dst, group = src, peers[2 if y_first else 1]
+        base = (0, dims[0], dims[0] + max(dims[1:]))[stage]
+        for slot, (_, target) in enumerate(group):
+            copies.append(
+                send(src, dst, send_sem.at[c, base + slot], recv_sem.at[c, base + slot], target)
+            )
+        pending[stage, c] = copies
+
+    def finish(stage, c):
+        for copy in pending.pop((stage, c)):
+            copy.wait()
+
+    total = len(chunks)
+    start(0, 0)
+    for step in range(total + 2):
+        if step + 1 < total:
+            start(0, step + 1)
+        if step < total:
+            finish(0, step)
+            start(1, step)
+        if 0 <= step - 1 < total:
+            finish(1, step - 1)
+            start(2, step - 1)
+        if 0 <= step - 2 < total:
+            finish(2, step - 2)
+
+
+def gather_weights(dims, shards, chunks, collective_id):
+    count = len(shards)
+    copies = dims[0] + 2 * max(dims[1:])
+    return pl.pallas_call(
+        functools.partial(gather_body, dims, chunks, count),
+        out_shape=[
+            jax.ShapeDtypeStruct((s.shape[0], *dims, *s.shape[1:]), s.dtype) for s in shards
+        ],
+        in_specs=[ANY] * count,
+        out_specs=[ANY] * count,
+        scratch_shapes=[
+            pltpu.SemaphoreType.DMA((len(chunks), copies)),
+            pltpu.SemaphoreType.DMA((len(chunks), copies)),
+            pltpu.SemaphoreType.DMA((len(chunks),)),
+        ],
+        compiler_params=pltpu.CompilerParams(
+            collective_id=collective_id, has_side_effects=True, vmem_limit_bytes=2**20
+        ),
+    )(*shards)
+
+
+def sum_body(dims, flags, *refs):
+    count = len(flags)
+    parts, totals = refs[:count], refs[count : 2 * count]
+    buffers = refs[2 * count : 6 * count]
+    send_sem, recv_sem, local_sem = refs[6 * count :]
+    z, y, x = place(dims)
+    peers = [axis_peers(dims, axis) for axis in range(3)]
+    greet([target for group in peers for _, target in group])
+    pending = {}
+
+    def start(stage, c):
+        y_first = flags[c]
+        own, first, second, third = buffers[4 * c : 4 * c + 4]
+        copies = []
+        base = (0, max(dims[1:]), 2 * max(dims[1:]))[stage]
+        if stage == 0:
+            mine = parts[c].at[:, y] if y_first else parts[c].at[:, :, x]
+            local = pltpu.make_async_copy(mine, own, local_sem.at[c])
+            local.start()
+            copies.append(local)
+        group = peers[((1, 2, 0) if y_first else (2, 1, 0))[stage]]
+        for slot, (spot, target) in enumerate(group):
+            if stage == 0:
+                src = parts[c].at[:, spot] if y_first else parts[c].at[:, :, spot]
+                dst = first.at[slot]
+            elif stage == 1:
+                src, dst = own.at[:, spot], second.at[slot]
+            else:
+                src, dst = own.at[spot, x if y_first else y], third.at[slot]
+            copies.append(
+                send(src, dst, send_sem.at[c, base + slot], recv_sem.at[c, base + slot], target)
+            )
+        pending[stage, c] = copies
+
+    def finish(stage, c):
+        y_first = flags[c]
+        own, first, second, third = buffers[4 * c : 4 * c + 4]
+        for copy in pending.pop((stage, c)):
+            copy.wait()
+        across = dims[2] if y_first else dims[1]
+        line = x if y_first else y
+        count_peers = len(peers[((1, 2, 0) if y_first else (2, 1, 0))[stage]])
+        if stage == 0 and count_peers:
+
+            def add_first(i, carry):
+                value = own[i // across, i % across].astype(jnp.float32)
+                for slot in range(count_peers):
+                    value += first[slot, i // across, i % across].astype(jnp.float32)
+                own[i // across, i % across] = value.astype(own.dtype)
+                return carry
+
+            lax.fori_loop(0, dims[0] * across, add_first, 0)
+        if stage == 1 and count_peers:
+
+            def add_second(i, carry):
+                value = own[i, line].astype(jnp.float32)
+                for slot in range(count_peers):
+                    value += second[slot, i].astype(jnp.float32)
+                own[i, line] = value.astype(own.dtype)
+                return carry
+
+            lax.fori_loop(0, dims[0], add_second, 0)
+        if stage == 2:
+            value = own[z, line].astype(jnp.float32)
+            for slot in range(count_peers):
+                value += third[slot].astype(jnp.float32)
+            totals[c][...] = value
+
+    total = len(flags)
+    ahead = 2
+    for c in range(min(ahead, total)):
+        start(0, c)
+    for step in range(total + 2 * ahead):
+        if step + ahead < total:
+            start(0, step + ahead)
+        if step < total:
+            finish(0, step)
+            start(1, step)
+        if 0 <= step - ahead < total:
+            finish(1, step - ahead)
+            start(2, step - ahead)
+        if 0 <= step - 2 * ahead < total:
+            finish(2, step - 2 * ahead)
+
+
+def sum_gradients(dims, parts, flags, collective_id):
+    count = len(parts)
+    scratch = []
+    for part, y_first in zip(parts, flags):
+        block = part.shape[3:]
+        own = (dims[0], dims[2] if y_first else dims[1])
+        turns = (dims[1], dims[2]) if y_first else (dims[2], dims[1])
+        scratch += [
+            pltpu.VMEM((*own, *block), part.dtype),
+            pltpu.VMEM((max(turns[0] - 1, 1), *own, *block), part.dtype),
+            pltpu.VMEM((max(turns[1] - 1, 1), dims[0], *block), part.dtype),
+            pltpu.VMEM((max(dims[0] - 1, 1), *block), part.dtype),
+        ]
+    copies = dims[0] + 2 * max(dims[1:])
+    return pl.pallas_call(
+        functools.partial(sum_body, dims, flags),
+        out_shape=[jax.ShapeDtypeStruct(part.shape[3:], jnp.float32) for part in parts],
+        in_specs=[ANY] * count,
+        out_specs=[VMEM] * count,
+        scratch_shapes=scratch
+        + [
+            pltpu.SemaphoreType.DMA((count, copies)),
+            pltpu.SemaphoreType.DMA((count, copies)),
+            pltpu.SemaphoreType.DMA((count,)),
+        ],
+        compiler_params=pltpu.CompilerParams(
+            collective_id=collective_id, has_side_effects=True, vmem_limit_bytes=VMEM_BYTES
+        ),
+    )(*parts)
+
+
+def spread_body(count, wide, swap, data, result, send_sem, recv_sem, local_sem):
+    pair = lax.axis_size("mp")
+    index = lax.axis_index("dp") * pair + lax.axis_index("mp") if wide else lax.axis_index("dp")
+
+    def target_of(step):
+        other = lax.rem(index + step, count)
+        if wide:
+            return other, (other // pair, lax.rem(other, pair))
+        return other, (other, lax.axis_index("mp"))
+
+    barrier = pltpu.get_barrier_semaphore()
+
+    def hello(step, carry):
+        pl.semaphore_signal(barrier, inc=1, device_id=target_of(step)[1], device_id_type=MESH)
+        return carry
+
+    lax.fori_loop(1, count, hello, 0)
+    pl.semaphore_wait(barrier, count - 1)
+    own = pltpu.make_async_copy(data.at[index if swap else 0], result.at[index], local_sem)
+    own.start()
+
+    def copy_of(step):
+        other, target = target_of(step)
+        return pltpu.make_async_remote_copy(
+            src_ref=data.at[other if swap else 0],
+            dst_ref=result.at[index],
+            send_sem=send_sem.at[step],
+            recv_sem=recv_sem.at[step],
+            device_id=target,
+            device_id_type=MESH,
+        )
+
+    def go(step, carry):
+        copy_of(step).start()
+        return carry
+
+    def done(step, carry):
+        copy_of(step).wait()
+        return carry
+
+    lax.fori_loop(1, count, go, 0)
+    own.wait()
+    lax.fori_loop(1, count, done, 0)
+
+
+def spread(data, wide, swap, collective_id):
+    count = lax.axis_size("dp") * (lax.axis_size("mp") if wide else 1)
+    block = data.shape[1:] if swap else data.shape
+    return pl.pallas_call(
+        functools.partial(spread_body, count, wide, swap),
+        out_shape=jax.ShapeDtypeStruct((count, *block), data.dtype),
+        in_specs=[VMEM],
+        out_specs=VMEM,
+        scratch_shapes=[
+            pltpu.SemaphoreType.DMA((count,)),
+            pltpu.SemaphoreType.DMA((count,)),
+            pltpu.SemaphoreType.DMA,
+        ],
+        compiler_params=pltpu.CompilerParams(
+            collective_id=collective_id, has_side_effects=True, vmem_limit_bytes=VMEM_BYTES
+        ),
+    )(data if swap else data[None])
 
 
 def layer_norm(values, gain_row, shift_row):
@@ -64,22 +355,31 @@
     )
 
 
+def project_turned(rows, turned):
+    return jnp.einsum("mvw,uw->mvu", rows, turned, preferred_element_type=jnp.float32)
+
+
+def project_back_turned(row_gradient_block, turned):
+    return jnp.einsum("tic,cv->tiv", row_gradient_block, turned, preferred_element_type=jnp.float32)
+
+
 def weight_grad(layer_input_list, row_gradient_block):
     return jnp.einsum(
         "hmq,hmw->qw", layer_input_list, row_gradient_block, preferred_element_type=jnp.float32
-    )
+    ).astype(jnp.bfloat16)
 
 
 def split_heads(values):
     return values.reshape(values.shape[0], values.shape[1], values.shape[2] // HEAD_DIM, HEAD_DIM)
 
 
-def merge_heads(partial_sum):
-    return lax.psum(partial_sum.astype(jnp.bfloat16), "mp").astype(jnp.float32)
-
-
-def merge_inputs(partial_sum):
-    return lax.psum(partial_sum.astype(jnp.bfloat16), "mp").astype(jnp.float32)
+def pair_sum(partial_sum):
+    mine = partial_sum.astype(jnp.bfloat16)
+    theirs = lax.ppermute(mine, "mp", [(0, 1), (1, 0)])
+    return mine.astype(jnp.float32) + theirs.astype(jnp.float32)
+
+
+merge_heads = merge_inputs = pair_sum
 
 
 def seq_scores(query_word, query_entity, key_rows):
@@ -162,12 +462,12 @@
         ),
     )
     mixed_low = mixed_heads.reshape(key_rows.shape).astype(jnp.bfloat16)
-    attended = merge_heads(project(mixed_low, out_mat))
+    attended = merge_heads(project_turned(mixed_low, out_mat))
     first_out = layer_norm(hidden + attended, gain_rows[0], gain_rows[1])
     first_low = first_out.astype(jnp.bfloat16)
     inner_pre = project(first_low, up_mat)
     inner_low = gelu_exact(inner_pre).astype(jnp.bfloat16)
-    outer_out = merge_heads(project(inner_low, down_mat))
+    outer_out = merge_heads(project_turned(inner_low, down_mat))
     result = layer_norm(first_out + outer_out, gain_rows[2], gain_rows[3])
     saved_acts = (
         hidden,
@@ -208,16 +508,16 @@
     second_back = jax.vjp(layer_norm, first_out + outer_out, gain_rows[2], gain_rows[3])[1]
     grad_second, grad_gain_late, grad_shift_late = second_back(grad_out)
     grad_outer = grad_second.astype(jnp.bfloat16)
-    grad_down = weight_grad(inner_low, grad_outer)
-    grad_inner = project_back(grad_outer, down_mat)
+    grad_down = weight_grad(grad_outer, inner_low)
+    grad_inner = project_back_turned(grad_outer, down_mat)
     grad_pre = jax.vjp(gelu_exact, inner_pre)[1](grad_inner)[0].astype(jnp.bfloat16)
     grad_up = weight_grad(first_low, grad_pre)
     grad_first = grad_second + merge_inputs(project_back(grad_pre, up_mat))
     first_back = jax.vjp(layer_norm, hidden + attended, gain_rows[0], gain_rows[1])[1]
     grad_first_in, grad_gain_early, grad_shift_early = first_back(grad_first)
     grad_attended = grad_first_in.astype(jnp.bfloat16)
-    grad_out_mat = weight_grad(mixed_low, grad_attended)
-    grad_mixed = project_back(grad_attended, out_mat).astype(jnp.bfloat16)
+    grad_out_mat = weight_grad(grad_attended, mixed_low)
+    grad_mixed = project_back_turned(grad_attended, out_mat).astype(jnp.bfloat16)
     grad_qw, grad_qe, grad_key, grad_value = lax.map(
         attend_backward,
         (
@@ -236,15 +536,10 @@
     grad_value = grad_value.reshape(flat_shape).astype(jnp.bfloat16)
     words_low = hidden_low[:, :WORDS]
     ents_low = hidden_low[:, WORDS:]
-    grad_mats = jnp.stack(
-        [
-            weight_grad(words_low, grad_qw[:, :WORDS]),
-            weight_grad(words_low, grad_qe[:, :WORDS]),
-            weight_grad(ents_low, grad_qw[:, WORDS:]),
-            weight_grad(ents_low, grad_qe[:, WORDS:]),
-            weight_grad(hidden_low, grad_key),
-            weight_grad(hidden_low, grad_value),
-        ]
+    grad_mats = (
+        weight_grad(words_low, jnp.concatenate([grad_qw[:, :WORDS], grad_qe[:, :WORDS]], axis=-1)),
+        weight_grad(ents_low, jnp.concatenate([grad_qw[:, WORDS:], grad_qe[:, WORDS:]], axis=-1)),
+        weight_grad(hidden_low, jnp.concatenate([grad_key, grad_value], axis=-1)),
     )
     part_words = project_back(grad_qw[:, :WORDS], attn_mats[0]) + project_back(
         grad_qe[:, :WORDS], attn_mats[1]
@@ -262,14 +557,99 @@
     return (grad_hidden, (grad_mats, grad_out_mat, grad_up, grad_down, grad_norms))
 
 
-def combine_partition(left_side, right_side):
-    peak_left, total_left, picked_left = left_side
-    peak_right, total_right, picked_right = right_side
-    peak_both = jnp.maximum(peak_left, peak_right)
-    total_both = total_left * jnp.exp(peak_left - peak_both) + total_right * jnp.exp(
-        peak_right - peak_both
-    )
-    return (peak_both, total_both, picked_left + picked_right)
+def padded_rows(values):
+    extra = -values.shape[-2] % 16
+    return jnp.pad(values, [(0, 0)] * (values.ndim - 2) + [(0, extra), (0, 0)])
+
+
+def gather_all(dims, attention_in, attention_out, feed_up, feed_down, norm_params, entity_proj, head_proj):
+    def turned(values):
+        return jnp.swapaxes(values, 1, 2)
+
+    mats = attention_in.reshape(-1, *attention_in.shape[2:])
+    norms = norm_params.reshape(1, -1, norm_params.shape[-1])
+    norms = jnp.pad(norms, [(0, 0), (0, 16 - norms.shape[1]), (0, -norms.shape[2] % 128)])
+    sources = [mats, turned(attention_out), feed_up, turned(feed_down), entity_proj[None], head_proj[None]]
+    heights = [part.shape[1] for part in sources]
+    shards = [padded_rows(part.astype(jnp.bfloat16)) for part in sources]
+    shards.append(norms.astype(jnp.bfloat16))
+    chunks = [(4, 0, 1, True), (5, 0, 1, False), (6, 0, 1, True)]
+    for layer in range(LAYERS):
+        chunks += [(0, 6 * layer, 3, True), (0, 6 * layer + 3, 3, False)]
+        chunks += [(1, layer, 1, layer == 0), (2, layer, 1, True), (3, layer, 1, False)]
+    wholes = gather_weights(dims, shards, chunks, 1)
+    flat = []
+    for part, height in zip(wholes, heights):
+        kept = part[..., :height, :]
+        flat.append(kept.reshape(part.shape[0], -1, part.shape[-1]))
+    norm_width = norm_params.shape[-1]
+    norm_all = wholes[6][0].reshape(-1, 16, wholes[6].shape[-1])[:, : LAYERS * 4, :norm_width]
+    norm_all = jnp.swapaxes(norm_all, 0, 1).reshape(LAYERS, 4, -1)
+    return (
+        flat[0].reshape(LAYERS, 6, *flat[0].shape[1:]),
+        flat[1],
+        flat[2],
+        flat[3],
+        norm_all,
+        flat[4][0],
+        flat[5][0],
+    )
+
+
+def sum_all(dims, layer_grads, grad_proj, grad_head):
+    n_dp = dims[0] * dims[1] * dims[2]
+
+    def blocks(values):
+        cut = values.astype(jnp.bfloat16).reshape(*dims, values.shape[0] // n_dp, values.shape[1])
+        return padded_rows(cut)
+
+    parts, flags, heights = [], [], []
+    for layer in reversed(range(LAYERS)):
+        (words_mat, ents_mat, shared_mat), out_mat, up_mat, down_mat, _ = layer_grads[layer]
+        late = layer % 2 == 0
+        for values, y_first in (
+            (up_mat, True),
+            (down_mat, False),
+            (words_mat, True),
+            (ents_mat, False),
+            (shared_mat, late),
+            (out_mat, not late),
+        ):
+            parts.append(blocks(values))
+            flags.append(y_first)
+            heights.append(values.shape[0] // n_dp)
+    for values, y_first in ((grad_proj, True), (grad_head, False)):
+        parts.append(blocks(values))
+        flags.append(y_first)
+        heights.append(values.shape[0] // n_dp)
+    norms = jnp.concatenate([layer_grads[layer][4] for layer in range(LAYERS)], axis=0)
+    width = norms.shape[1] // n_dp
+    norms = jnp.swapaxes(norms.reshape(norms.shape[0], n_dp, width), 0, 1)
+    norms = jnp.pad(norms, [(0, 0), (0, 16 - norms.shape[1]), (0, -width % 128)])
+    parts.append(norms.astype(jnp.bfloat16).reshape(*dims, *norms.shape[1:]))
+    flags.append(True)
+    totals = sum_gradients(dims, parts, flags, 2)
+    norm_sum = totals[-1][: LAYERS * 4, :width].reshape(LAYERS, 4, width)
+    totals = [total[:height] for total, height in zip(totals, heights)]
+    attn, outs, ups, downs = [], [], [], []
+    for layer in range(LAYERS):
+        at = 6 * (LAYERS - 1 - layer)
+        ups.append(totals[at])
+        downs.append(totals[at + 1].T)
+        for part in totals[at + 2 : at + 5]:
+            half = part.shape[1] // 2
+            attn += [part[:, :half], part[:, half:]]
+        outs.append(totals[at + 5].T)
+    attn = jnp.stack(attn)
+    return (
+        attn.reshape(LAYERS, 6, *attn.shape[1:]),
+        jnp.stack(outs),
+        jnp.stack(ups),
+        jnp.stack(downs),
+        norm_sum,
+        totals[-2],
+        totals[-1],
+    )
 
 
 def on_device(
@@ -305,16 +685,10 @@
     entity_table_first,
     entity_table_second,
 ):
-    gathered = (
-        lax.all_gather(attention_in.astype(jnp.bfloat16), "dp", axis=2, tiled=True),
-        lax.all_gather(attention_out.astype(jnp.bfloat16), "dp", axis=2, tiled=True),
-        lax.all_gather(feed_up.astype(jnp.bfloat16), "dp", axis=1, tiled=True),
-        lax.all_gather(feed_down.astype(jnp.bfloat16), "dp", axis=2, tiled=True),
-        lax.all_gather(norm_params.astype(jnp.bfloat16), "dp", axis=2, tiled=True),
-        lax.all_gather(entity_proj.astype(jnp.bfloat16), "dp", axis=0, tiled=True),
-        lax.all_gather(head_proj.astype(jnp.bfloat16), "dp", axis=0, tiled=True),
-    )
-    attn_low, out_low, up_low, down_low, norm_low, proj_low, head_low = gathered
+    dims = chip_grid(lax.axis_size("dp"))
+    attn_low, out_low, up_low, down_low, norm_low, proj_low, head_low = gather_all(
+        dims, attention_in, attention_out, feed_up, feed_down, norm_params, entity_proj, head_proj
+    )
     gain_all = norm_low.astype(jnp.float32)
     slot_total = entity_ids.shape[0]
     shard_rows = entity_table.shape[0]
@@ -335,7 +709,7 @@
     local_shard_rows = jnp.einsum(
         "wvt,wvi->ti", row_placement_plan, replied_rows_result, preferred_element_type=jnp.float32
     )
-    paired = lax.psum(local_shard_rows.astype(jnp.bfloat16), "mp").astype(jnp.float32)
+    paired = pair_sum(local_shard_rows)
     masked_slots = (
         jnp.arange(SEQ_DEV, dtype=jnp.int32)[:, None] * ENT_LEN + mask_positions
     ).reshape(-1)
@@ -369,7 +743,7 @@
     masked_low = hidden[seq_index, masked_rows].reshape(SEQ_DEV * MASK_ENT, D).astype(jnp.bfloat16)
     head_pre = jnp.dot(masked_low, head_low, preferred_element_type=jnp.float32)
     states_low = gelu_exact(head_pre).astype(jnp.bfloat16)
-    all_states = lax.all_gather(states_low, "dp", axis=0, tiled=True)
+    all_states = spread(states_low, False, False, 3).reshape(-1, states_low.shape[1])
     logits = lax.dot_general(
         all_states, table_low, (((1,), (1,)), ((), ())), preferred_element_type=jnp.float32
     )
@@ -380,9 +754,10 @@
     peak_value = jnp.max(logits, axis=1)
     exp_total = jnp.sum(jnp.exp(logits - peak_value[:, None]), axis=1)
     picked = jnp.sum(jnp.where(target_hits, logits, 0.0), axis=1)
-    peak_all, total_all, picked_all = joined(
-        (peak_value, exp_total, picked), ("dp", "mp"), combine_partition
-    )
+    shares = spread(jnp.stack([peak_value, exp_total, picked]), True, False, 4)
+    peak_all = jnp.max(shares[:, 0], axis=0)
+    total_all = jnp.sum(shares[:, 1] * jnp.exp(shares[:, 0] - peak_all), axis=0)
+    picked_all = jnp.sum(shares[:, 2], axis=0)
     log_norm = peak_all + jnp.log(total_all)
     row_losses = log_norm - picked_all
     prob_rows = jnp.exp(logits - log_norm[:, None])
@@ -392,13 +767,10 @@
     grad_table = lax.dot_general(
         grad_logits, all_states, (((0,), (0,)), ((), ())), preferred_element_type=jnp.float32
     )
-    grad_share = lax.psum_scatter(
-        jnp.dot(grad_logits, table_low, preferred_element_type=jnp.float32),
-        ("dp", "mp"),
-        scatter_dimension=0,
-        tiled=True,
-    )
-    grad_states = lax.all_gather(grad_share, "mp", axis=0, tiled=True)
+    grad_states = jnp.dot(grad_logits, table_low, preferred_element_type=jnp.float32)
+    grad_states = grad_states.reshape(lax.axis_size("dp"), -1, grad_states.shape[1])
+    grad_states = jnp.sum(spread(grad_states, False, True, 5), axis=0)
+    grad_states = grad_states + lax.ppermute(grad_states, "mp", [(0, 1), (1, 0)])
     grad_head_pre = jax.vjp(gelu_exact, head_pre)[1](grad_states)[0].astype(jnp.bfloat16)
     grad_head = lax.dot_general(
         masked_low, grad_head_pre, (((0,), (0,)), ((), ())), preferred_element_type=jnp.float32
@@ -453,24 +825,8 @@
                 jnp.where(owned_mask[:, :, None], incoming, 0.0)
             )
         kept_grads.insert(0, layer_grads)
-    stacked = tuple(
-        (
-            jnp.stack([kept_grads[layer_index][member_index] for layer_index in range(LAYERS)])
-            for member_index in range(5)
-        )
-    )
-    summed = (
-        lax.psum_scatter(stacked[0], "dp", scatter_dimension=2, tiled=True),
-        lax.psum_scatter(stacked[1], "dp", scatter_dimension=2, tiled=True),
-        lax.psum_scatter(stacked[2], "dp", scatter_dimension=1, tiled=True),
-        lax.psum_scatter(stacked[3], "dp", scatter_dimension=2, tiled=True),
-        lax.psum_scatter(stacked[4], "dp", scatter_dimension=2, tiled=True),
-        lax.psum_scatter(grad_proj, "dp", scatter_dimension=0, tiled=True),
-        lax.psum_scatter(grad_head, "dp", scatter_dimension=0, tiled=True),
-    )
-    reduced = summed[:5]
-    reduced_proj = summed[5]
-    reduced_head = summed[6]
+    reduced = sum_all(dims, kept_grads, grad_proj, grad_head)
+    reduced_proj, reduced_head = reduced[5:]
     attn_new = adam_update(
         attention_in, attention_in_first, attention_in_second, reduced[0], kind_rates[0]
     )

time: 2380 us -> 909 us (0.38)
  waiting for transfers between devices: 1340 us -> 8.29 us
  Pallas kernels: 0 us -> 386 us
  blocking collectives: 287 us -> 0 us
  other arithmetic: 218 us -> 105 us
  local copies, waits for them, and re-layouts: 153 us -> 82.3 us
  matrix products: 330 us -> 292 us
    reduce_scatter x5 -> x0, waiting for transfers between devices: 629 us -> none  [the longest x1 223 us: on_device(): lax.psum_scatter(stacked[0], 'dp', scatter_dimension=2, tiled=True)]
    unnamed x22 -> x0, waiting for transfers between devices: 468 us -> none
    pallas_call x0 -> x5, Pallas kernels: none -> 386 us  [the longest x1 180 us: gather_weights(): pl.pallas_call(functools.partial(gather_body, dims, chunks, count), out_s...]
    all_gather x8 -> x0, blocking collectives: 276 us -> none  [the longest x3 113 us: joined(): everything = jax.tree.map(lambda part: lax.all_gather(part, axis), x)]
    all_gather x4 -> x0, waiting for transfers between devices: 138 us -> none  [the longest x1 62 us: on_device(): lax.all_gather(feed_down.astype(jnp.bfloat16), 'dp', axis=2, tiled=True)]
    psum x9 -> x0, waiting for transfers between devices: 100 us -> none  [the longest x4 63.8 us: merge_inputs(): return lax.psum(partial_sum.astype(jnp.bfloat16), 'mp').astype(jnp.float32)]
    add x62 -> x0, other arithmetic: 78.7 us -> none  [the longest x31 39.4 us: combine_partition(): total_left * jnp.exp(peak_left - peak_both)]
    dynamic_slice x62 -> x0, local copies, waits for them, and re-layouts: 44 us -> none  [lap(): return combine(so_far, jax.tree.map(lambda part: part[k], everything))]
  transfers between devices with their start and end apart: 22 -> 13, of which waited for: 19 -> 3; matrix products, arithmetic and copies ran while one was open for 11% -> 11% of each run, Pallas kernels for 0% -> 39%
where the time goes in v1:
time: 909 us; the launch traced here: 904 us
  Pallas kernels  386 us (42%)
  matrix products  292 us (32%)
  other arithmetic  105 us (12%)
  local copies, waits for them, and re-layouts  82.3 us (9%)
  starting transfers between devices  27.4 us (3%)
    pallas_call x1, Pallas kernels, gather_weights(): pl.pallas_call(functools.partial(gather_body, dims, chunks, count), out_s...  180 us
    pallas_call x1, Pallas kernels, sum_gradients(): pl.pallas_call(functools.partial(sum_body, dims, flags), out_shape=[jax.S...  176 us
    sub x2, matrix products, attend_backward(): grad_probs - inner_sum  54.9 us
    dot_general x14, matrix products, project(): jnp.einsum('mvw,wu->mvu', fetched_row_values, weight_matrix_entry, prefer...  49.4 us
    unnamed x469, local copies, waits for them, and re-layouts  43 us
    dot_general x12, matrix products, weight_grad(): jnp.einsum('hmq,hmw->qw', layer_input_list, row_gradient_block, preferred...  37.4 us
    pallas_call x3, Pallas kernels, spread(): pl.pallas_call(functools.partial(spread_body, count, wide, swap), out_sha...  29.7 us
    dot_general x2, matrix products, attend_forward(): jnp.einsum('hqk,khd->qhd', prob_low, value_rows, preferred_element_type=j...  24.4 us
  transfers between devices with their start and end apart: 13, of which 3 were waited for; matrix products, arithmetic and copies ran while one was open for 11% of the time, Pallas kernels for 39%

profile of v1, /device:TPU:0, one launch (start us, length us, event | category | flops | bytes accessed | tf_op | source)
XLA Modules:
  0.0 903.7 jit_solution(14154310779951320079)
XLA Ops:
  4.3 8.3 all-to-all-start
  12.9 180.1 %shard_map.494 = (bf16[12,4,2,2,48,384]{5,4,3,2,1,0:T(8,128)(2,1)S(1)}, bf16[2,4,2,2,48,384]{5,4,3,2,1,0:T(8,128)(2,1)S(1)}, bf16[2,4,2,2,48,1536]{5,4,3,2,1,0:T...) custom-call(bf16[12,48,384]{2,1,0:T(8,128)(2,1)S(1)} %bitcast.479, ...), custom_call_target="tpu_custom_call" | custom-call | tf_op jit(solution)/shard_map/pallas_call | solution.py:127
  205.3 8.6 all-to-all-start.1
  253.5 4.4 fusion.4
  259.7 12.2 %fusion.104 = bf16[6,64,1024]{2,1,0:T(8,128)(2,1)} fusion(bf16[1024,6,64]{0,2,1:T(8,128)(2,1)} %bitcast.605, f32[6,1024]{1,0:T(8,128)S(1)} %fusion.4, f32[6,1024]{1,0:T(8,128)S(1)} %fusion.288, f32[6,1024,128]{1,2,0:T(8,128)} %copy-done.17, f32[6,1024,896]{1,2,0:T(8,128)} %copy-done.6), kind=kOutput, calls=%fused_computation.192 | convolution fusion | flops 837156864 | bytes 26787840 | tf_op jit(solution)/shard_map/while/body/eval_jaxpr/hqk,khd->qhd/dot_general | solution.py:402
  276.7 5.6 fusion.310
  282.3 4.2 fusion.308
  287.2 17.4 %multiply_convert_fusion.3 = (bf16[1024,1536]{1,0:T(8,128)(2,1)S(1)}, f32[1024,1536]{1,0:T(8,128)}, f32[1024,1536]{1,0:T(8,128)}) fusion(bf16[768,1536]{1,0:T(8,128)(2,1)S(1)} %bitcast.529, f32[1,1024,768]{2,1,0:T(8,128)S(1)} %get-tuple-element.251, f32[768]{0:T(1024)S(1)} %get-tuple-element.199, f32[768]{0:T(1024)S(1)} %get-tuple-element.200, ...), kind=kOutput, calls=%fused_computation.61 | convolution fusion | flops 2522087424 | bytes 21248000 | tf_op jit(solution)/shard_map/mvw,wu->mvu/dot_general | solution.py:347
  336.6 5.0 fusion.5
  343.3 12.1 %fusion.103 = bf16[6,64,1024]{2,1,0:T(8,128)(2,1)} fusion(bf16[1024,6,64]{0,2,1:T(8,128)(2,1)} %bitcast.609, f32[6,1024]{1,0:T(8,128)} %fusion.5, f32[6,1024]{1,0:T(8,128)} %copy-done.129, f32[6,1024,128]{1,2,0:T(8,128)} %copy-done.19, f32[6,1024,896]{1,2,0:T(8,128)} %copy-done.7), kind=kOutput, calls=%fused_computation.191 | convolution fusion | flops 837156864 | bytes 26787840 | tf_op jit(solution)/shard_map/while/body/eval_jaxpr/hqk,khd->qhd/dot_general | solution.py:402
  366.1 17.4 %multiply_convert_fusion.2 = (bf16[1024,1536]{1,0:T(8,128)(2,1)S(1)}, f32[1024,1536]{1,0:T(8,128)}, f32[1024,1536]{1,0:T(8,128)}) fusion(bf16[768,1536]{1,0:T(8,128)(2,1)S(1)} %bitcast.535, f32[1,1024,768]{2,1,0:T(8,128)S(1)} %get-tuple-element.245, f32[768]{0:T(1024)S(1)} %copy-done.198, f32[768]{0:T(1024)S(1)} %get-tuple-element.196, ...), kind=kOutput, calls=%fused_computation.48 | convolution fusion | flops 2522087424 | bytes 21248000 | tf_op jit(solution)/shard_map/mvw,wu->mvu/dot_general | solution.py:347
  400.9 9.1 %shard_map.495 = bf16[16,16,256]{2,1,0:T(8,128)(2,1)} custom-call(bf16[1,16,256]{2,1,0:T(8,128)(2,1)} %get-tuple-element.238.data), custom_call_target="tpu_custom_call" | custom-call | tf_op jit(solution)/shard_map/pallas_call | solution.py:309
  416.2 9.6 %shard_map.496 = f32[32,3,256]{2,1,0:T(4,128)} custom-call(f32[1,3,256]{2,1,0:T(4,128)} %maximum_bitcast_fusion.16.data), custom_call_target="tpu_custom_call" | custom-call | tf_op jit(solution)/shard_map/pallas_call | solution.py:309
  433.8 10.9 %shard_map.497 = f32[16,16,256]{2,1,0:T(8,128)} custom-call(f32[16,16,256]{2,1,0:T(8,128)} %bitcast.562), custom_call_target="tpu_custom_call" | custom-call | tf_op jit(solution)/shard_map/pallas_call | solution.py:309
  452.6 4.5 scatter_fusion
  462.7 8.6 add_convert_fusion.1
  488.8 27.6 %multiply_convert_fusion.1 = bf16[6,1024,1024]{1,2,0:T(8,128)(2,1)} fusion(f32[6,1024]{1,0:T(8,128)S(1)} %log_add_fusion.1, bf16[1024,6,64]{0,2,1:T(8,128)(2,1)} %bitcast.611, bf16[1024,6,64]{0,2,1:T(8,128)(2,1)} %bitcast.610, f32[6,1024,128]{1,2,0:T(8,128)S(1)} %copy-done.20, f32[6,1024,896]{1,2,0:T(8,128)} %copy-done.7), kind=kOutput, calls=%fused_computation.14 | convolution fusion | flops 1679825920 | bytes 39346176 | tf_op jit(solution)/shard_map/while/body/eval_jaxpr/sub | solution.py:422
  516.4 7.4 fusion.91
  525.9 4.3 fusion.137
  530.9 10.9 %fusion.97 = bf16[6,64,1024]{2,1,0:T(8,128)(2,1)} fusion(bf16[1024,6,64]{0,2,1:T(8,128)(2,1)} %bitcast.612, f32[6,1024]{1,0:T(8,128)S(1)} %log_add_fusion.1, f32[6,1024,128]{1,2,0:T(8,128)S(1)} %copy-done.20, f32[6,1024,896]{1,2,0:T(8,128)} %copy-done.7), kind=kOutput, calls=%fused_computation.187 | convolution fusion | flops 830865408 | bytes 26763264 | tf_op jit(solution)/shard_map/while/body/eval_jaxpr/hqk,qhd->khd/dot_general | solution.py:412
  551.3 4.2 convolution_convert_fusion.2
  575.0 4.6 add_convert_fusion
  586.3 6.1 convolution_convert_fusion
  592.5 4.6 convolution_convert_fusion.1
  605.6 27.3 %multiply_convert_fusion = bf16[6,1024,1024]{1,2,0:T(8,128)(2,1)} fusion(f32[6,1024]{1,0:T(8,128)S(1)} %log_add_fusion, bf16[1024,6,64]{0,2,1:T(8,128)(2,1)} %bitcast.613, bf16[1024,6,64]{0,2,1:T(8,128)(2,1)} %bitcast.606, f32[6,1024,128]{1,2,0:T(8,128)S(1)} %copy-done.18, f32[6,1024,896]{1,2,0:T(8,128)} %copy-done.6), kind=kOutput, calls=%fused_computation.10 | convolution fusion | flops 1679825920 | bytes 39346176 | tf_op jit(solution)/shard_map/while/body/eval_jaxpr/sub | solution.py:422
  633.0 7.4 fusion.94
  642.5 4.3 fusion.140
  647.5 11.1 %fusion.100 = bf16[6,64,1024]{2,1,0:T(8,128)(2,1)} fusion(bf16[1024,6,64]{0,2,1:T(8,128)(2,1)} %bitcast.614, f32[6,1024]{1,0:T(8,128)S(1)} %log_add_fusion, f32[6,1024,128]{1,2,0:T(8,128)S(1)} %copy-done.18, f32[6,1024,896]{1,2,0:T(8,128)} %copy-done.6), kind=kOutput, calls=%fused_computation.188 | convolution fusion | flops 830865408 | bytes 26763264 | tf_op jit(solution)/shard_map/while/body/eval_jaxpr/hqk,qhd->khd/dot_general | solution.py:412
  681.7 7.6 all-to-all-start.2
  691.3 176.1 %shard_map.498 = (f32[48,1536]{1,0:T(8,128)}, f32[48,1536]{1,0:T(8,128)}, f32[48,768]{1,0:T(8,128)}, f32[48,768]{1,0:T(8,128)}, f32[48,768]{1,0:T(8,128)}, /*ind...) custom-call(bf16[4,2,2,48,1536]{4,3,2,1,0:T(8,128)(2,1)} %bitcast.53, ...), custom_call_target="tpu_custom_call" | custom-call | tf_op jit(solution)/shard_map/pallas_call | solution.py:244
  886.9 5.5 scatter_custom_fusion.1
  892.4 11.1 %multiply_subtract_fusion = (f32[3968,256]{1,0:T(8,128)}, f32[3968,256]{1,0:T(8,128)}, f32[3968,256]{1,0:T(8,128)}) fusion(f32[3968,256]{1,0:T(8,128)} %param.59, f32[3968,256]{1,0:T(8,128)} %scatter_custom_fusion.1, f32[3968,256]{1,0:T(8,128)} %param.61, f32[3968,256]{1,0:T(8,128)} %param.60), kind=kLoop, calls=%fused_computation.82 | loop fusion | flops 15237120 | bytes 28442624 | tf_op jit(solution)/shard_map/sub | solution.py:340
  (691 shorter events, 261.5 us)
Async XLA Ops:
  4.3 198.1 %all-to-all-start = ((s32[16,1,8]{2,1,0:T(1,128)}), s32[16,1,8]{2,1,0:T(1,128)S(1)}, u32[]{:S(2)}, u32[]{:S(2)}) async-start(s32[16,1,8]{2,1,0:T(1,128)} %copy.168), calls=%async_computation | async-start | bytes 16384 | tf_op jit(solution)/shard_map/all_to_all | solution.py:699
  197.3 34.2 %copy-start.4 = (bf16[1,4,2,2,16,768]{5,4,3,2,1,0:T(8,128)(2,1)}, bf16[1,4,2,2,16,768]{5,4,3,2,1,0:T(8,128)(2,1)S(1)}, u32[]{:S(2)}) copy-start(bf16[1,4,2,2,16,768]{5,4,3,2,1,0:T(8,128)(2,1)S(1)} %get-tuple-element.156) | copy-start | bytes 1179652
  202.2 26.0 %copy-start.37 = (bf16[1,4,2,2,48,384]{5,4,3,2,1,0:T(8,128)(2,1)}, bf16[1,4,2,2,48,384]{5,4,3,2,1,0:T(8,128)(2,1)S(1)}, u32[]{:S(2)}) copy-start(bf16[1,4,2,2,48,384]{5,4,3,2,1,0:T(8,128)(2,1)S(1)} %get-tuple-element.259) | copy-start | bytes 1769476
  202.4 23.6 %copy-start.24 = (bf16[3968,256]{1,0:T(8,128)(2,1)}, bf16[3968,256]{1,0:T(8,128)(2,1)S(1)}, u32[]{:S(2)}) copy-start(bf16[3968,256]{1,0:T(8,128)(2,1)S(1)} %convert_element_type.551) | copy-start | bytes 6094852
  203.7 22.4 %copy-start.194 = (pred[16,8]{1,0:T(8,128)(4,1)}, pred[16,8]{1,0:T(8,128)(4,1)S(1)}, u32[]{:S(2)}) copy-start(pred[16,8]{1,0:T(8,128)(4,1)S(1)} %copy.170) | copy-start | bytes 388
  205.3 16.2 %all-to-all-start.1 = ((bf16[16,8,256]{2,1,0:T(8,128)(2,1)}), bf16[16,8,256]{2,1,0:T(8,128)(2,1)S(1)}, u32[]{:S(2)}, u32[]{:S(2)}) async-start(bf16[16,8,256]{2,1,0:T(8,128)(2,1)} %bitcast_select_fusion.1), calls=%async_computation.1 | async-start | bytes 131072 | tf_op jit(solution)/shard_map/all_to_all | solution.py:705
  223.2 8.2 collective-permute-start
  275.4 6.9 collective-permute-start.1
  276.7 36.1 %copy-start.167 = (f32[768]{0:T(1024)}, f32[768]{0:T(1024)S(1)}, u32[]{:S(2)}) copy-start(f32[768]{0:T(1024)S(1)} %get-tuple-element.200) | copy-start | bytes 9220
  276.7 84.7 %copy-start.155 = (f32[768]{0:T(1024)}, f32[768]{0:T(1024)S(1)}, u32[]{:S(2)}) copy-start(f32[768]{0:T(1024)S(1)} %get-tuple-element.198) | copy-start | bytes 9220
  282.3 22.3 %copy-start.66 = (bf16[1,4,2,2,48,1536]{5,4,3,2,1,0:T(8,128)(2,1)}, bf16[1,4,2,2,48,1536]{5,4,3,2,1,0:T(8,128)(2,1)S(1)}, u32[]{:S(2)}) copy-start(bf16[1,4,2,2,48,1536]{5,4,3,2,1,0:T(8,128)(2,1)S(1)} %get-tuple-element.265) | copy-start | bytes 7077892
  286.6 18.1 %copy-start.10 = (f32[1,1024,768]{2,1,0:T(8,128)}, f32[1,1024,768]{2,1,0:T(8,128)S(1)}, u32[]{:S(2)}) copy-start(f32[1,1024,768]{2,1,0:T(8,128)S(1)} %get-tuple-element.251) | copy-start | bytes 9437188
  286.6 26.2 %copy-start.157 = (f32[1024]{0:T(1024)}, f32[1024]{0:T(1024)S(1)}, u32[]{:S(2)}) copy-start(f32[1024]{0:T(1024)S(1)} %broadcast_multiply_fusion.3) | copy-start | bytes 12292
  308.4 4.4 collective-permute-start.2
  316.8 44.5 %copy-start.8 = (f32[1,1024,768]{2,1,0:T(8,128)}, f32[1,1024,768]{2,1,0:T(8,128)S(1)}, u32[]{:S(2)}) copy-start(f32[1,1024,768]{2,1,0:T(8,128)S(1)} %get-tuple-element.247) | copy-start | bytes 9437188
  316.9 44.5 %copy-start.147 = (f32[1024]{0:T(1024)}, f32[1024]{0:T(1024)S(1)}, u32[]{:S(2)}) copy-start(f32[1024]{0:T(1024)S(1)} %broadcast_multiply_fusion.2) | copy-start | bytes 12292
  317.4 44.0 %copy-start.159 = (f32[1024]{0:T(1024)}, f32[1024]{0:T(1024)S(1)}, u32[]{:S(2)}) copy-start(f32[1024]{0:T(1024)S(1)} %fusion.236) | copy-start | bytes 12292
  357.8 3.6 collective-permute-start.3
  363.2 20.2 %copy-start.12 = (f32[1,1024,768]{2,1,0:T(8,128)}, f32[1,1024,768]{2,1,0:T(8,128)S(1)}, u32[]{:S(2)}) copy-start(f32[1,1024,768]{2,1,0:T(8,128)S(1)} %get-tuple-element.245) | copy-start | bytes 9437188
  363.8 19.7 %copy-start.190 = (f32[1024]{0:T(1024)}, f32[1024]{0:T(1024)S(1)}, u32[]{:S(2)}) copy-start(f32[1024]{0:T(1024)S(1)} %multiply_reduce_fusion.10) | copy-start | bytes 12292
  363.8 26.0 %copy-start.171 = (f32[1024]{0:T(1024)}, f32[1024]{0:T(1024)S(1)}, u32[]{:S(2)}) copy-start(f32[1024]{0:T(1024)S(1)} %fusion.237) | copy-start | bytes 12292
  386.1 3.6 collective-permute-start.4
  446.3 4.6 collective-permute-start.5
  462.6 19.0 %copy-start.29 = (f32[1,1024,768]{2,1,0:T(8,128)}, f32[1,1024,768]{2,1,0:T(8,128)S(1)}, u32[]{:S(2)}) copy-start(f32[1,1024,768]{2,1,0:T(8,128)S(1)} %get-tuple-element.235) | copy-start | bytes 9437188
  474.0 7.6 collective-permute-start.6
  550.1 18.8 %collective-permute-start.7 = (bf16[1,1024,768]{2,1,0:T(8,128)(2,1)}, bf16[1,1024,768]{2,1,0:T(8,128)(2,1)}, u32[]{:S(2)}, u32[]{:S(2)}) collective-permute-start(bf16[1,1024,768]{2,1,0:T(8,128)(2,1)} %fusion.80), channel_id=1, source_target_pairs={{0,1},{1,0},{2,3},{3,2},{4,5},{5,4},{6,7},{7,6},{8,9},{9,8},{10,11... | collective-permute-start | bytes 4718600 | tf_op jit(solution)/shard_map/ppermute | solution.py:378
  583.4 13.7 %collective-permute-start.8 = (bf16[1,1024,768]{2,1,0:T(8,128)(2,1)}, bf16[1,1024,768]{2,1,0:T(8,128)(2,1)}, u32[]{:S(2)}, u32[]{:S(2)}) collective-permute-start(bf16[1,1024,768]{2,1,0:T(8,128)(2,1)} %fusion.84), channel_id=1, source_target_pairs={{0,1},{1,0},{2,3},{3,2},{4,5},{5,4},{6,7},{7,6},{8,9},{9,8},{10,11... | collective-permute-start | bytes 4718600 | tf_op jit(solution)/shard_map/ppermute | solution.py:378
  664.9 11.2 %collective-permute-start.9 = (bf16[1,1024,768]{2,1,0:T(8,128)(2,1)S(1)}, bf16[1,1024,768]{2,1,0:T(8,128)(2,1)}, u32[]{:S(2)}, u32[]{:S(2)}) collective-permute-start(bf16[1,1024,768]{2,1,0:T(8,128)(2,1)S(1)} %fusion.79), channel_id=1, source_target_pairs={{0,1},{1,0},{2,3},{3,2},{4,5},{5,4},{6,7},{7,6},{8,9},{9,8},{10,11... | collective-permute-start | bytes 4718600 | tf_op jit(solution)/shard_map/ppermute | solution.py:378
  681.7 205.3 %all-to-all-start.2 = ((bf16[16,8,256]{2,1,0:T(8,128)(2,1)}), bf16[16,8,256]{2,1,0:T(8,128)(2,1)S(1)}, u32[]{:S(2)}, u32[]{:S(2)}) async-start(bf16[16,8,256]{2,1,0:T(8,128)(2,1)} %fusion.201), calls=%async_computation.2 | async-start | bytes 131072 | tf_op jit(solution)/shard_map/all_to_all | solution.py:821
  691.2 187.5 %copy-start.53 = (f32[2,6,48,384]{3,2,1,0:T(8,128)S(1)}, f32[2,6,48,384]{3,2,1,0:T(8,128)}, u32[]{:S(2)}) copy-start(f32[2,6,48,384]{3,2,1,0:T(8,128)} %param.38) | copy-start | bytes 2654212
  691.3 187.5 %copy-start.95 = (f32[2,6,48,384]{3,2,1,0:T(8,128)S(1)}, f32[2,6,48,384]{3,2,1,0:T(8,128)}, u32[]{:S(2)}) copy-start(f32[2,6,48,384]{3,2,1,0:T(8,128)} %param.40) | copy-start | bytes 2654212
  691.3 187.5 %copy-start.96 = (f32[2,6,48,384]{3,2,1,0:T(8,128)S(1)}, f32[2,6,48,384]{3,2,1,0:T(8,128)}, u32[]{:S(2)}) copy-start(f32[2,6,48,384]{3,2,1,0:T(8,128)} %param.39) | copy-start | bytes 2654212
  (206 other events, 891.2 us)

commit v2 on v1

--- a/solution.py
+++ b/solution.py
@@ -557,12 +557,505 @@
     return (grad_hidden, (grad_mats, grad_out_mat, grad_up, grad_down, grad_norms))
 
 
+LOG2E = 1.4426950408889634
+SCORE_STEP = 0.125 * LOG2E
+LEN = WORDS + ENT_LEN
+BLOCK = 256
+BLOCKS = LEN // BLOCK
+
+
+def mm(left, right):
+    return lax.dot_general(
+        left, right, (((1,), (0,)), ((), ())), preferred_element_type=jnp.float32
+    )
+
+
+def mm_rt(left, right):
+    return lax.dot_general(
+        left, right, (((1,), (1,)), ((), ())), preferred_element_type=jnp.float32
+    )
+
+
+def mm_lt(left, right):
+    return lax.dot_general(
+        left, right, (((0,), (0,)), ((), ())), preferred_element_type=jnp.float32
+    )
+
+
+def flat(ref, *index):
+    value = ref[index] if index else ref[...]
+    return value.reshape(-1, value.shape[-1])
+
+
+def lane_mask(rows, which):
+    lane = lax.broadcasted_iota(jnp.int32, (rows, 2 * HEAD_DIM), 1)
+    return (lane // HEAD_DIM == which).astype(jnp.bfloat16)
+
+
+def normed(values):
+    centered = values - jnp.mean(values, axis=-1, keepdims=True)
+    spread_row = jnp.mean(centered * centered, axis=-1, keepdims=True)
+    scale = lax.rsqrt(spread_row + norm_eps)
+    return centered * scale, scale
+
+
+def gelu_parts(values):
+    cdf = 0.5 * (1.0 + lax.erf(values * 0.7071067811865476))
+    bell = jnp.exp2(values * values * (-0.5 * LOG2E)) * 0.3989422804014327
+    return values * cdf, cdf + values * bell
+
+
+class Gather:
+    def __init__(self, dims, chunks, shards, wholes, kept, sems, lags=(3, 2, 2)):
+        self.dims, self.chunks, self.shards, self.wholes, self.kept = dims, chunks, shards, wholes, kept
+        self.send_sem, self.recv_sem, self.local_sem, self.keep_sem = sems
+        self.spot = place(dims)
+        self.peers = [axis_peers(dims, axis) for axis in range(3)]
+        self.pending, self.step = {}, 0
+        self.ahead, self.lag1, self.lag2 = lags
+
+    def targets(self):
+        return [target for group in self.peers for _, target in group]
+
+    def start(self, stage, c):
+        which, rows, cols, y_first = self.chunks[c]
+        z, y, x = self.spot
+        whole = self.wholes[which].at[rows, :, :, :, :, cols]
+        shard = self.shards[which].at[rows, :, cols]
+        copies = []
+        if stage == 0:
+            own = pltpu.make_async_copy(shard, whole.at[:, z, y, x], self.local_sem.at[c])
+            own.start()
+            copies.append(own)
+            src, dst, group = shard, whole.at[:, z, y, x], self.peers[0]
+        elif stage == 1:
+            src = whole.at[:, :, y, x]
+            dst, group = src, self.peers[1 if y_first else 2]
+        else:
+            src = whole.at[:, :, :, x] if y_first else whole.at[:, :, y]
+            dst, group = src, self.peers[2 if y_first else 1]
+        base = (0, self.dims[0], self.dims[0] + max(self.dims[1:]))[stage]
+        for slot, (_, target) in enumerate(group):
+            sems = self.send_sem.at[c, base + slot], self.recv_sem.at[c, base + slot]
+            copies.append(send(src, dst, *sems, target))
+        self.pending[stage, c] = copies
+
+    def finish(self, stage, c):
+        for copy in self.pending.pop((stage, c)):
+            copy.wait()
+        if stage == 2:
+            which, rows, cols, _ = self.chunks[c]
+            keep = pltpu.make_async_copy(
+                self.wholes[which].at[rows, :, :, :, :, cols],
+                self.kept[which].at[rows, :, :, :, :, cols],
+                self.keep_sem.at[c],
+            )
+            keep.start()
+            self.pending[3, c] = [keep]
+
+    def begin(self):
+        for c in range(min(self.ahead, len(self.chunks))):
+            self.start(0, c)
+
+    def tick(self):
+        total, step = len(self.chunks), self.step
+        if step >= total + self.lag1 + self.lag2:
+            return
+        self.step += 1
+        if step + self.ahead < total:
+            self.start(0, step + self.ahead)
+        if step < total:
+            self.finish(0, step)
+            self.start(1, step)
+        late = step - self.lag1
+        if 0 <= late < total:
+            self.finish(1, late)
+            self.start(2, late)
+        late -= self.lag2
+        if 0 <= late < total:
+            self.finish(2, late)
+
+    def need(self, c):
+        while self.step < c + self.lag1 + self.lag2 + 1:
+            self.tick()
+
+    def close(self):
+        self.need(len(self.chunks) - 1)
+        for key in sorted(self.pending):
+            for copy in self.pending[key]:
+                copy.wait()
+
+
+class Pair:
+    def __init__(self, mine, theirs, sems):
+        self.mine, self.theirs = mine, theirs
+        self.send_sem, self.recv_sem = sems
+        self.phase = 0
+        self.other = (lax.axis_index("dp"), 1 - lax.axis_index("mp"))
+
+    def copy(self, phase, c):
+        return pltpu.make_async_remote_copy(
+            src_ref=self.mine.at[c],
+            dst_ref=self.theirs.at[phase % 2, c],
+            send_sem=self.send_sem.at[phase, c],
+            recv_sem=self.recv_sem.at[phase, c],
+            device_id=self.other,
+            device_id_type=MESH,
+        )
+
+    def run(self, compute, consume, between=None):
+        phase = self.phase
+        self.phase += 1
+
+        def take(c):
+            self.copy(phase, c).wait()
+            total = self.mine[c].astype(jnp.float32) + self.theirs[phase % 2, c].astype(jnp.float32)
+            consume(c, pl.ds(c * BLOCK, BLOCK), total)
+
+        for c in range(BLOCKS):
+            self.mine[c] = compute(c, pl.ds(c * BLOCK, BLOCK)).astype(jnp.bfloat16)
+            self.copy(phase, c).start()
+            if between is not None:
+                between()
+            if c:
+                take(c - 1)
+        take(BLOCKS - 1)
+
+
+SAVED = ("xb", "qw", "qe", "k", "v", "o", "n1", "h1b", "slope", "g", "n2", "stats")
+
+
+def saved_shapes(half, hidden):
+    wide, narrow = (LEN, D), (LEN, half)
+    low = jnp.bfloat16
+    return {
+        "xb": (wide, low),
+        "qw": (narrow, low),
+        "qe": (narrow, low),
+        "k": (narrow, low),
+        "v": (narrow, low),
+        "o": (narrow, low),
+        "n1": (wide, low),
+        "h1b": (wide, low),
+        "slope": ((LEN, hidden), low),
+        "g": ((LEN, hidden), low),
+        "n2": (wide, low),
+        "stats": ((LEN, 128), jnp.float32),
+    }
+
+
+def attend(act, pair):
+    lanes = slice(pair * 2 * HEAD_DIM, (pair + 1) * 2 * HEAD_DIM)
+
+    def block(i, carry):
+        rows = pl.ds(i * BLOCK, BLOCK)
+        keys, values = act["k"][:, lanes], act["v"][:, lanes]
+        total = None
+        for which in range(2):
+            q_mask, v_mask = lane_mask(BLOCK, which), lane_mask(LEN, which)
+            score_w = mm_rt(act["qw"][rows, lanes] * q_mask, keys[:WORDS])
+            score_e = mm_rt(act["qe"][rows, lanes] * q_mask, keys[WORDS:])
+            peak = jnp.maximum(
+                jnp.max(score_w, axis=-1, keepdims=True), jnp.max(score_e, axis=-1, keepdims=True)
+            )
+            exp_w = jnp.exp2((score_w - peak) * SCORE_STEP)
+            exp_e = jnp.exp2((score_e - peak) * SCORE_STEP)
+            weight = jnp.sum(exp_w, axis=-1, keepdims=True) + jnp.sum(exp_e, axis=-1, keepdims=True)
+            part = values * v_mask
+            mixed = mm(exp_w.astype(jnp.bfloat16), part[:WORDS])
+            mixed += mm(exp_e.astype(jnp.bfloat16), part[WORDS:])
+            mixed = mixed * (1.0 / weight)
+            total = mixed if total is None else total + mixed
+            head = 2 * pair + which
+            act["stats"][rows, head : head + 1] = peak * SCORE_STEP + jnp.log2(weight)
+        act["o"][rows, lanes] = total.astype(jnp.bfloat16)
+        return carry
+
+    lax.fori_loop(0, BLOCKS, block, 0)
+
+
+def project_rows(out_ref, x_ref, first, size, step, weights, index):
+    def block(i, carry):
+        rows = pl.ds(first + i * step, step)
+        out_ref[rows, :] = mm(x_ref[rows, :], flat(weights, index)).astype(jnp.bfloat16)
+        return carry
+
+    lax.fori_loop(0, size // step, block, 0)
+
+
+def forward_body(dims, chunks, needs, *refs):
+    refs = list(refs)
+
+    def take(count):
+        part = refs[:count]
+        del refs[:count]
+        return part
+
+    words, base, rows_in = take(3)
+    shards = take(len(needs["kinds"]))
+    kept = take(len(needs["kinds"]))
+    saved = [dict(zip(SAVED, take(len(SAVED)))) for _ in range(LAYERS)]
+    (ents_out,) = take(1)
+    wholes = take(len(needs["kinds"]))
+    act = dict(zip(SAVED, take(len(SAVED))))
+    x, h1, gains, mine, theirs = take(5)
+    gather_sems = take(4)
+    pair_sems = take(2)
+    (save_sem,) = take(1)
+
+    gather = Gather(dims, chunks, shards, wholes, kept, gather_sems)
+    pair = Pair(mine, theirs, pair_sems)
+    greet(gather.targets() + [pair.other])
+    gather.begin()
+    attn, outs, ups, downs, proj, _, norms = wholes
+    saving = {}
+
+    def save(layer, name):
+        slot = layer * len(SAVED) + SAVED.index(name)
+        copy = pltpu.make_async_copy(act[name], saved[layer][name], save_sem.at[slot])
+        copy.start()
+        saving[name] = copy
+
+    def free(name):
+        if name in saving:
+            saving.pop(name).wait()
+
+    x[:WORDS] = words[...].astype(jnp.float32)
+    gather.need(needs["norms"])
+    width = D // (dims[0] * dims[1] * dims[2])
+    count = dims[0] * dims[1] * dims[2]
+    gains[...] = jnp.zeros_like(gains)
+    for d in range(count):
+        z, rest = d // (dims[1] * dims[2]), d % (dims[1] * dims[2])
+        pick = lax.broadcasted_iota(jnp.int32, (128, D), 0) + d * width
+        lane = lax.broadcasted_iota(jnp.int32, (128, D), 1)
+        inside = lax.broadcasted_iota(jnp.int32, (128, D), 0) < width
+        hot = jnp.where((pick == lane) & inside, 1.0, 0.0).astype(jnp.bfloat16)
+        gains[...] += mm(norms[0, z, rest // dims[2], rest % dims[2]], hot)
+    gather.need(needs["proj"])
+    x[WORDS:] = base[...].astype(jnp.float32) + mm(rows_in[...], flat(proj, 0))
+
+    for layer in range(LAYERS):
+        gain = [gains[4 * layer + i : 4 * layer + i + 1, :] for i in range(4)]
+        free("xb")
+
+        def cast(i, carry):
+            rows = pl.ds(i * BLOCK, BLOCK)
+            act["xb"][rows, :] = x[rows, :].astype(jnp.bfloat16)
+            return carry
+
+        lax.fori_loop(0, BLOCKS, cast, 0)
+        save(layer, "xb")
+        for name, word_mat, ent_mat in (("k", 4, None), ("v", 5, None), ("qw", 0, 2), ("qe", 1, 3)):
+            free(name)
+            gather.need(needs["mat", layer, word_mat if ent_mat is None else ent_mat])
+            if ent_mat is None:
+                project_rows(act[name], act["xb"], 0, LEN, 512, attn, 6 * layer + word_mat)
+            else:
+                project_rows(act[name], act["xb"], 0, WORDS, 448, attn, 6 * layer + word_mat)
+                project_rows(act[name], act["xb"], WORDS, ENT_LEN, ENT_LEN, attn, 6 * layer + ent_mat)
+            save(layer, name)
+            gather.tick()
+        free("o")
+        free("stats")
+        for head_pair in range(act["o"].shape[1] // (2 * HEAD_DIM)):
+            attend(act, head_pair)
+            gather.tick()
+        save(layer, "o")
+        gather.need(needs["out", layer])
+        for name in ("n1", "h1b"):
+            free(name)
+
+        def out_part(c, rows):
+            return mm_rt(act["o"][rows, :], flat(outs, layer))
+
+        def first_norm(c, rows, total):
+            hat, scale = normed(x[rows, :] + total)
+            act["n1"][rows, :] = hat.astype(jnp.bfloat16)
+            act["stats"][rows, 8:9] = scale
+            value = hat * gain[0] + gain[1]
+            h1[rows, :] = value
+            act["h1b"][rows, :] = value.astype(jnp.bfloat16)
+
+        pair.run(out_part, first_norm, gather.tick)
+        save(layer, "n1")
+        save(layer, "h1b")
+        gather.need(needs["up", layer, 1])
+        for name in ("g", "slope", "n2"):
+            free(name)
+        hidden = act["g"].shape[1]
+        tile = 512
+
+        def up_block(c):
+            rows = pl.ds(c * BLOCK, BLOCK)
+            for first in range(0, hidden, tile):
+                cols = slice(first, first + tile)
+                weight = ups[layer, :, :, :, :, cols].reshape(D, tile)
+                value, slope = gelu_parts(mm(act["h1b"][rows, :], weight))
+                act["g"][rows, cols] = value.astype(jnp.bfloat16)
+                act["slope"][rows, cols] = slope.astype(jnp.bfloat16)
+
+        for c in range(BLOCKS):
+            up_block(c)
+            gather.tick()
+        save(layer, "g")
+        save(layer, "slope")
+        gather.need(needs["down", layer, 1])
+
+        def down_part(c, rows):
+            return mm_rt(act["g"][rows, :], flat(downs, layer))
+
+        def second_norm(c, rows, total):
+            hat, scale = normed(h1[rows, :] + total)
+            act["n2"][rows, :] = hat.astype(jnp.bfloat16)
+            act["stats"][rows, 9:10] = scale
+            x[rows, :] = hat * gain[2] + gain[3]
+
+        pair.run(down_part, second_norm, gather.tick)
+        save(layer, "n2")
+        save(layer, "stats")
+    ents_out[...] = x[WORDS:]
+    gather.close()
+    for name in list(saving):
+        free(name)
+
+
+KINDS = ("attn", "out", "up", "down", "proj", "head", "norms")
+
+
+MAT_ORDER = (4, 5, 0, 2, 1, 3)
+
+
+def gather_plan(hidden):
+    every = slice(None)
+    chunks = [(6, pl.ds(0, 1), every, True), (4, pl.ds(0, 1), every, False)]
+    needs = {"kinds": KINDS, "norms": 0, "proj": 1}
+    y_first = [True]
+
+    def add(name, which, row, cols):
+        chunks.append((which, pl.ds(row, 1), cols, y_first[0]))
+        y_first[0] = not y_first[0]
+        needs[name] = len(chunks) - 1
+
+    for layer in range(LAYERS):
+        for mat in MAT_ORDER:
+            add(("mat", layer, mat), 0, 6 * layer + mat, every)
+        add(("out", layer), 1, layer, every)
+        for which, name in ((2, "up"), (3, "down")):
+            for part in range(2):
+                add((name, layer, part), which, layer, pl.ds(part * (hidden // 2), hidden // 2))
+    add("head", 5, 0, every)
+    return chunks, needs
+
+
+def run_forward(dims, words, base, entity_rows, shards, collective_id):
+    half, hidden = shards[0].shape[-1], shards[2].shape[-1]
+    chunks, needs = gather_plan(hidden)
+    shapes = saved_shapes(half, hidden)
+    low, full = jnp.bfloat16, jnp.float32
+    wholes = [(s.shape[0], *dims, *s.shape[1:]) for s in shards]
+    copies = dims[0] + 2 * max(dims[1:])
+    saved_out = [jax.ShapeDtypeStruct(*shapes[name]) for _ in range(LAYERS) for name in SAVED]
+    result = pl.pallas_call(
+        functools.partial(forward_body, dims, chunks, needs),
+        out_shape=[jax.ShapeDtypeStruct(shape, low) for shape in wholes]
+        + saved_out
+        + [jax.ShapeDtypeStruct((ENT_LEN, D), full)],
+        in_specs=[VMEM] * 3 + [ANY] * len(shards),
+        out_specs=[ANY] * (len(wholes) + len(saved_out)) + [VMEM],
+        scratch_shapes=[pltpu.VMEM(shape, low) for shape in wholes]
+        + [pltpu.VMEM(*shapes[name]) for name in SAVED]
+        + [
+            pltpu.VMEM((LEN, D), full),
+            pltpu.VMEM((LEN, D), full),
+            pltpu.VMEM((16, D), full),
+            pltpu.VMEM((BLOCKS, BLOCK, D), low),
+            pltpu.VMEM((2, BLOCKS, BLOCK, D), low),
+            pltpu.SemaphoreType.DMA((len(chunks), copies)),
+            pltpu.SemaphoreType.DMA((len(chunks), copies)),
+            pltpu.SemaphoreType.DMA((len(chunks),)),
+            pltpu.SemaphoreType.DMA((len(chunks),)),
+            pltpu.SemaphoreType.DMA((2 * LAYERS, BLOCKS)),
+            pltpu.SemaphoreType.DMA((2 * LAYERS, BLOCKS)),
+            pltpu.SemaphoreType.DMA((LAYERS * len(SAVED),)),
+        ],
+        compiler_params=pltpu.CompilerParams(
+            collective_id=collective_id, has_side_effects=True, vmem_limit_bytes=VMEM_BYTES
+        ),
+    )(words, base, entity_rows, *shards)
+    kept = result[: len(wholes)]
+    saved = [
+        dict(zip(SAVED, result[len(wholes) + layer * len(SAVED) :][: len(SAVED)]))
+        for layer in range(LAYERS)
+    ]
+    return kept, saved, result[-1]
+
+
+def norm_back(grad, hat, scale, gain_row):
+    hat = hat.astype(jnp.float32)
+    wide = grad * gain_row
+    inner = jnp.mean(wide * hat, axis=-1, keepdims=True)
+    back = scale * (wide - jnp.mean(wide, axis=-1, keepdims=True) - hat * inner)
+    return back, jnp.sum(grad * hat, axis=0), jnp.sum(grad, axis=0)
+
+
+def saved_backward(grad_out, saved, attn_mats, out_mat, up_mat, down_mat, gain_rows):
+    low = jnp.bfloat16
+    stats = saved["stats"]
+    heads = saved["k"].shape[1] // HEAD_DIM
+    grad_second, gain_late, shift_late = norm_back(
+        grad_out, saved["n2"], stats[:, 9:10], gain_rows[2]
+    )
+    grad_outer = grad_second.astype(low)
+    grad_down = mm_lt(grad_outer, saved["g"])
+    grad_pre = (mm(grad_outer, down_mat) * saved["slope"].astype(jnp.float32)).astype(low)
+    grad_up = mm_lt(saved["h1b"], grad_pre)
+    grad_first = grad_second + pair_sum(mm_rt(grad_pre, up_mat))
+    grad_first_in, gain_early, shift_early = norm_back(
+        grad_first, saved["n1"], stats[:, 8:9], gain_rows[0]
+    )
+    grad_attended = grad_first_in.astype(low)
+    grad_out_mat = mm_lt(grad_attended, saved["o"])
+    grad_mixed = mm(grad_attended, out_mat).astype(low)
+
+    def heads_of(values):
+        return values.reshape(LEN, heads, HEAD_DIM)
+
+    log_norm = stats[:, :heads].T / LOG2E
+    parts = attend_backward(
+        (
+            heads_of(saved["qw"]),
+            heads_of(saved["qe"]),
+            heads_of(saved["k"]),
+            heads_of(saved["v"]),
+            log_norm,
+            heads_of(grad_mixed),
+        )
+    )
+    grad_qw, grad_qe, grad_key, grad_value = [
+        part.reshape(LEN, heads * HEAD_DIM).astype(low) for part in parts
+    ]
+    xb = saved["xb"]
+    grad_mats = (
+        mm_lt(xb[:WORDS], jnp.concatenate([grad_qw[:WORDS], grad_qe[:WORDS]], axis=1)),
+        mm_lt(xb[WORDS:], jnp.concatenate([grad_qw[WORDS:], grad_qe[WORDS:]], axis=1)),
+        mm_lt(xb, jnp.concatenate([grad_key, grad_value], axis=1)),
+    )
+    part_words = mm_rt(grad_qw[:WORDS], attn_mats[0]) + mm_rt(grad_qe[:WORDS], attn_mats[1])
+    part_ents = mm_rt(grad_qw[WORDS:], attn_mats[2]) + mm_rt(grad_qe[WORDS:], attn_mats[3])
+    part = jnp.concatenate([part_words, part_ents], axis=0)
+    part += mm_rt(grad_key, attn_mats[4]) + mm_rt(grad_value, attn_mats[5])
+    grad_hidden = grad_first_in + pair_sum(part)
+    grad_norms = jnp.stack([gain_early, shift_early, gain_late, shift_late])
+    return grad_hidden, (grad_mats, grad_out_mat, grad_up, grad_down, grad_norms)
+
+
 def padded_rows(values):
     extra = -values.shape[-2] % 16
     return jnp.pad(values, [(0, 0)] * (values.ndim - 2) + [(0, extra), (0, 0)])
 
 
-def gather_all(dims, attention_in, attention_out, feed_up, feed_down, norm_params, entity_proj, head_proj):
+def weight_shards(attention_in, attention_out, feed_up, feed_down, norm_params, entity_proj, head_proj):
     def turned(values):
         return jnp.swapaxes(values, 1, 2)
 
@@ -573,27 +1066,33 @@
     heights = [part.shape[1] for part in sources]
     shards = [padded_rows(part.astype(jnp.bfloat16)) for part in sources]
     shards.append(norms.astype(jnp.bfloat16))
+    return shards, heights
+
+
+def unpack_weights(wholes, heights, norm_width):
+    kept = []
+    for part, height in zip(wholes, heights):
+        part = part[..., :height, :]
+        kept.append(part.reshape(part.shape[0], -1, part.shape[-1]))
+    norm_all = wholes[6][0].reshape(-1, 16, wholes[6].shape[-1])[:, : LAYERS * 4, :norm_width]
+    norm_all = jnp.swapaxes(norm_all, 0, 1).reshape(LAYERS, 4, -1)
+    return (
+        kept[0].reshape(LAYERS, 6, *kept[0].shape[1:]),
+        kept[1],
+        kept[2],
+        kept[3],
+        norm_all,
+        kept[4][0],
+        kept[5][0],
+    )
+
+
+def gather_apart(dims, shards):
     chunks = [(4, 0, 1, True), (5, 0, 1, False), (6, 0, 1, True)]
     for layer in range(LAYERS):
         chunks += [(0, 6 * layer, 3, True), (0, 6 * layer + 3, 3, False)]
         chunks += [(1, layer, 1, layer == 0), (2, layer, 1, True), (3, layer, 1, False)]
-    wholes = gather_weights(dims, shards, chunks, 1)
-    flat = []
-    for part, height in zip(wholes, heights):
-        kept = part[..., :height, :]
-        flat.append(kept.reshape(part.shape[0], -1, part.shape[-1]))
-    norm_width = norm_params.shape[-1]
-    norm_all = wholes[6][0].reshape(-1, 16, wholes[6].shape[-1])[:, : LAYERS * 4, :norm_width]
-    norm_all = jnp.swapaxes(norm_all, 0, 1).reshape(LAYERS, 4, -1)
-    return (
-        flat[0].reshape(LAYERS, 6, *flat[0].shape[1:]),
-        flat[1],
-        flat[2],
-        flat[3],
-        norm_all,
-        flat[4][0],
-        flat[5][0],
-    )
+    return gather_weights(dims, shards, chunks, 1)
 
 
 def sum_all(dims, layer_grads, grad_proj, grad_head):
@@ -686,10 +1185,10 @@
     entity_table_second,
 ):
     dims = chip_grid(lax.axis_size("dp"))
-    attn_low, out_low, up_low, down_low, norm_low, proj_low, head_low = gather_all(
-        dims, attention_in, attention_out, feed_up, feed_down, norm_params, entity_proj, head_proj
-    )
-    gain_all = norm_low.astype(jnp.float32)
+    shards, heights = weight_shards(
+        attention_in, attention_out, feed_up, feed_down, norm_params, entity_proj, head_proj
+    )
+    fused = heights[0] % 16 == 0 and heights[4] % 16 == 0
     slot_total = entity_ids.shape[0]
     shard_rows = entity_table.shape[0]
     bucket_rows = buckets.reshape(buckets.shape[2], buckets.shape[3])
@@ -717,30 +1216,42 @@
         jnp.arange(slot_total, dtype=jnp.int32)[:, None] == masked_slots[None, :], axis=1
     ).astype(jnp.float32)
     entity_rows = (paired * keep_weight[:, None]).astype(jnp.bfloat16)
-    entity_inputs = entity_base.astype(jnp.float32) + jnp.dot(
-        entity_rows, proj_low, preferred_element_type=jnp.float32
-    )
-    hidden = jnp.concatenate(
-        [
-            word_inputs.astype(jnp.float32).reshape(SEQ_DEV, WORDS, D),
-            entity_inputs.reshape(SEQ_DEV, ENT_LEN, D),
-        ],
-        axis=1,
-    )
-    saved_layers = []
-    for layer_index in range(LAYERS):
-        hidden, saved_acts = layer_forward(
-            hidden,
-            attn_low[layer_index],
-            out_low[layer_index],
-            up_low[layer_index],
-            down_low[layer_index],
-            gain_all[layer_index],
+    if fused:
+        wholes, saved_layers, ents = run_forward(
+            dims, word_inputs, entity_base, entity_rows, shards, 6
         )
-        saved_layers.append(saved_acts)
+    else:
+        wholes = gather_apart(dims, shards)
+    attn_low, out_low, up_low, down_low, norm_low, proj_low, head_low = unpack_weights(
+        wholes, heights, norm_params.shape[-1]
+    )
+    gain_all = norm_low.astype(jnp.float32)
+    if not fused:
+        entity_inputs = entity_base.astype(jnp.float32) + jnp.dot(
+            entity_rows, proj_low, preferred_element_type=jnp.float32
+        )
+        hidden = jnp.concatenate(
+            [
+                word_inputs.astype(jnp.float32).reshape(SEQ_DEV, WORDS, D),
+                entity_inputs.reshape(SEQ_DEV, ENT_LEN, D),
+            ],
+            axis=1,
+        )
+        saved_layers = []
+        for layer_index in range(LAYERS):
+            hidden, saved_acts = layer_forward(
+                hidden,
+                attn_low[layer_index],
+                out_low[layer_index],
+                up_low[layer_index],
+                down_low[layer_index],
+                gain_all[layer_index],
+            )
+            saved_layers.append(saved_acts)
+        ents = hidden[0, WORDS:]
     seq_index = jnp.arange(SEQ_DEV, dtype=jnp.int32)[:, None]
     masked_rows = WORDS + mask_positions
-    masked_low = hidden[seq_index, masked_rows].reshape(SEQ_DEV * MASK_ENT, D).astype(jnp.bfloat16)
+    masked_low = ents[mask_positions.reshape(-1)].astype(jnp.bfloat16)
     head_pre = jnp.dot(masked_low, head_low, preferred_element_type=jnp.float32)
     states_low = gelu_exact(head_pre).astype(jnp.bfloat16)
     all_states = spread(states_low, False, False, 3).reshape(-1, states_low.shape[1])
@@ -790,8 +1301,8 @@
     )
     kept_grads = []
     for layer_index in reversed(range(LAYERS)):
-        grad_hidden, layer_grads = layer_backward(
-            grad_hidden,
+        grad_hidden, layer_grads = (saved_backward if fused else layer_backward)(
+            grad_hidden[0] if fused else grad_hidden,
             saved_layers[layer_index],
             attn_low[layer_index],
             out_low[layer_index],
@@ -799,6 +1310,8 @@
             down_low[layer_index],
             gain_all[layer_index],
         )
+        if fused:
+            grad_hidden = grad_hidden[None]
         if layer_index == 0:
             word_grads = grad_hidden[:, :WORDS].reshape(SEQ_DEV * WORDS, D)
             grad_entity = grad_hidden[:, WORDS:].reshape(slot_total, D).astype(jnp.bfloat16)

time: 909 us -> 855 us (0.941)
  matrix products: 292 us -> 175 us
  other arithmetic: 105 us -> 149 us
  Pallas kernels: 386 us -> 413 us
    sub x0 -> x2, other arithmetic: none -> 75.7 us  [attend_backward(): grad_probs - inner_sum]
    dot_general x51 -> x32, matrix products: 162 us -> 92.1 us  [the longest x12 39.4 us: mm_lt(): lax.dot_general(left, right, (((0,), (0,)), ((), ())), preferred_element_...]
    sub x2 -> x0, matrix products: 54.9 us -> none  [attend_backward(): grad_probs - inner_sum]
    reduce_sum x19 -> x4, other arithmetic: 45.5 us -> 12 us  [norm_back(): return (back, jnp.sum(grad * hat, axis=0), jnp.sum(grad, axis=0))]
    pallas_call x1, Pallas kernels: 180 us -> 205 us  [run_forward(): pl.pallas_call(functools.partial(forward_body, dims, chunks, needs), out_...]
    unnamed x469 -> x295, local copies, waits for them, and re-layouts: 43 us -> 19.4 us
    slice x13 -> x19, local copies, waits for them, and re-layouts: 8.85 us -> 26.3 us  [the longest x1 6.28 us: saved_backward(): part += mm_rt(grad_key, attn_mats[4]) + mm_rt(grad_value, attn_mats[5])]
    dot_general x8 -> x0, local copies, waits for them, and re-layouts: 11.8 us -> none  [project(): jnp.einsum('mvw,wu->mvu', fetched_row_values, weight_matrix_entry, prefer...]
  transfers between devices with their start and end apart: 13 -> 9, of which waited for: 3 -> 2; matrix products, arithmetic and copies ran while one was open for 11% -> 14% of each run, Pallas kernels for 39% -> 0%
where the time goes in v2:
time: 855 us; the launch traced here: 846 us
  Pallas kernels  413 us (48%)
  matrix products  175 us (20%)
  other arithmetic  149 us (17%)
  local copies, waits for them, and re-layouts  79.1 us (9%)
  starting transfers between devices  18.6 us (2%)
  waiting for transfers between devices  9.05 us (1%)
    pallas_call x1, Pallas kernels, run_forward(): pl.pallas_call(functools.partial(forward_body, dims, chunks, needs), out_...  205 us
    pallas_call x1, Pallas kernels, sum_gradients(): pl.pallas_call(functools.partial(sum_body, dims, flags), out_shape=[jax.S...  177 us
    sub x2, other arithmetic, attend_backward(): grad_probs - inner_sum  75.7 us
    dot_general x12, matrix products, mm_lt(): lax.dot_general(left, right, (((0,), (0,)), ((), ())), preferred_element_...  39.4 us
    pallas_call x3, Pallas kernels, spread(): pl.pallas_call(functools.partial(spread_body, count, wide, swap), out_sha...  31.6 us
    dot_general x2, matrix products, attend_backward(): jnp.einsum('hqk,qhd->khd', prob_rows.astype(jnp.bfloat16), grad_mixed, pr...  23.5 us
    dot_general x14, matrix products, mm_rt(): lax.dot_general(left, right, (((1,), (1,)), ((), ())), preferred_element_...  21.6 us
    dot_general x2, matrix products, attend_backward(): jnp.einsum('qhd,khd->hqk', grad_mixed, value_rows, preferred_element_type...  20.7 us
  transfers between devices with their start and end apart: 9, of which 2 were waited for; matrix products, arithmetic and copies ran while one was open for 14% of the time, Pallas kernels for 0%

profile of v2, /device:TPU:0, one launch (start us, length us, event | category | flops | bytes accessed | tf_op | source)
XLA Modules:
  0.0 846.1 jit_solution(786033215766945681)
XLA Ops:
  3.8 8.3 all-to-all-start
  23.2 5.5 all-to-all-start.1
  28.7 7.6 all-to-all-done.1
  45.8 205.0 %shard_map.494 = (bf16[12,4,2,2,48,384]{5,4,3,2,1,0:T(8,128)(2,1)}, bf16[2,4,2,2,48,384]{5,4,3,2,1,0:T(8,128)(2,1)}, bf16[2,4,2,2,48,1536]{5,4,3,2,1,0:T(8,128)(...) custom-call(bf16[896,768]{1,0:T(8,128)(2,1)} %refs_0_.1, ...), custom_call_target="tpu_custom_call" | custom-call | tf_op jit(solution)/shard_map/pallas_call | solution.py:959
  262.9 10.1 %shard_map.495 = bf16[16,16,256]{2,1,0:T(8,128)(2,1)} custom-call(bf16[1,16,256]{2,1,0:T(8,128)(2,1)} %get-tuple-element.177.data), custom_call_target="tpu_custom_call" | custom-call | tf_op jit(solution)/shard_map/pallas_call | solution.py:309
  277.2 10.2 %shard_map.496 = f32[32,3,256]{2,1,0:T(4,128)} custom-call(f32[1,3,256]{2,1,0:T(4,128)} %maximum_bitcast_fusion.data), custom_call_target="tpu_custom_call" | custom-call | tf_op jit(solution)/shard_map/pallas_call | solution.py:309
  294.9 5.1 fusion.206
  300.0 11.2 %shard_map.497 = f32[16,16,256]{2,1,0:T(8,128)} custom-call(f32[16,16,256]{2,1,0:T(8,128)} %bitcast.354), custom_call_target="tpu_custom_call" | custom-call | tf_op jit(solution)/shard_map/pallas_call | solution.py:309
  312.8 5.1 fusion.205
  322.7 6.3 fusion.204
  333.9 9.0 %fusion.211 = f32[6,1024,896]{1,2,0:T(8,128)} fusion(bf16[1024,6,64]{0,2,1:T(8,128)(2,1)S(1)} %bitcast.288, bf16[896,6,64]{0,2,1:T(8,128)(2,1)S(1)} %bitcast.292), kind=kOutput, calls=%fused_computation.335 | convolution fusion | flops 704643072 | bytes 23494656 | tf_op jit(solution)/shard_map/qhd,khd->hqk/dot_general | solution.py:386
  365.3 5.2 multiply_convert_fusion.3
  375.4 9.1 %fusion.216 = f32[6,1024,896]{1,2,0:T(8,128)} fusion(bf16[1024,6,64]{0,2,1:T(8,128)(2,1)S(1)} %bitcast.286, bf16[896,6,64]{0,2,1:T(8,128)(2,1)S(1)} %bitcast.291), kind=kOutput, calls=%fused_computation.340 | convolution fusion | flops 704643072 | bytes 23494656 | tf_op jit(solution)/shard_map/qhd,khd->hqk/dot_general | solution.py:386
  384.5 4.7 convolution_convert_fusion.2
  394.9 10.1 %fusion.213 = f32[6,1024,1024]{1,2,0:T(8,128)} fusion(bf16[1024,6,64]{0,2,1:T(8,128)(2,1)S(1)} %bitcast.298, bf16[1024,6,64]{0,2,1:T(8,128)(2,1)S(1)} %bitcast.297), kind=kOutput, calls=%fused_computation.337 | convolution fusion | flops 805306368 | bytes 26738688 | tf_op jit(solution)/shard_map/qhd,khd->hqk/dot_general | solution.py:418
  405.1 38.1 %multiply_convert_fusion.1 = bf16[6,1024,1024]{1,2,0:T(8,128)(2,1)} fusion(f32[6,1024,1024]{1,2,0:T(8,128)} %fusion.213, f32[6,1024]{1,0:T(8,128)S(1)} %copy-done.111, f32[6,1024,128]{1,2,0:T(8,128)} %fusion.212, f32[6,1024,896]{1,2,0:T(8,128)} %fusion.211), kind=kOutput, calls=%fused_computation.17 | output fusion | flops 69213184 | bytes 62939136 | tf_op jit(solution)/shard_map/sub | solution.py:422
  443.2 6.5 fusion.96
  454.1 4.3 fusion.87
  458.4 11.8 %fusion.67 = bf16[6,64,1024]{2,1,0:T(8,128)(2,1)} fusion(bf16[1024,6,64]{0,2,1:T(8,128)(2,1)} %bitcast.299, f32[6,1024]{1,0:T(8,128)S(1)} %copy-done.111, f32[6,1024,128]{1,2,0:T(8,128)} %fusion.212, f32[6,1024,896]{1,2,0:T(8,128)} %fusion.211), kind=kOutput, calls=%fused_computation.110 | convolution fusion | flops 830865408 | bytes 26763264 | tf_op jit(solution)/shard_map/hqk,qhd->khd/dot_general | solution.py:412
  479.6 4.0 convolution_convert_fusion.3
  486.2 4.3 convolution_convert_fusion.9
  494.8 3.7 fusion.40
  506.7 6.6 convolution_convert_fusion.1
  513.3 4.7 convolution_convert_fusion
  523.7 10.5 %fusion.218 = f32[6,1024,1024]{1,2,0:T(8,128)} fusion(bf16[1024,6,64]{0,2,1:T(8,128)(2,1)S(1)} %bitcast.300, bf16[1024,6,64]{0,2,1:T(8,128)(2,1)S(1)} %bitcast.296), kind=kOutput, calls=%fused_computation.342 | convolution fusion | flops 805306368 | bytes 26738688 | tf_op jit(solution)/shard_map/qhd,khd->hqk/dot_general | solution.py:418
  534.2 37.7 %multiply_convert_fusion = bf16[6,1024,1024]{1,2,0:T(8,128)(2,1)} fusion(f32[6,1024,1024]{1,2,0:T(8,128)} %fusion.218, f32[6,1024]{1,0:T(8,128)S(1)} %copy-done.110, f32[6,1024,128]{1,2,0:T(8,128)} %fusion.217, f32[6,1024,896]{1,2,0:T(8,128)} %fusion.216), kind=kOutput, calls=%fused_computation.14 | output fusion | flops 69213184 | bytes 62939136 | tf_op jit(solution)/shard_map/sub | solution.py:422
  571.9 6.5 fusion.93
  582.8 4.3 fusion.90
  587.2 11.8 %fusion.70 = bf16[6,64,1024]{2,1,0:T(8,128)(2,1)} fusion(bf16[1024,6,64]{0,2,1:T(8,128)(2,1)} %bitcast.301, f32[6,1024]{1,0:T(8,128)S(1)} %copy-done.110, f32[6,1024,128]{1,2,0:T(8,128)} %fusion.217, f32[6,1024,896]{1,2,0:T(8,128)} %fusion.216), kind=kOutput, calls=%fused_computation.111 | convolution fusion | flops 830865408 | bytes 26763264 | tf_op jit(solution)/shard_map/hqk,qhd->khd/dot_general | solution.py:412
  624.9 176.8 %shard_map.498 = (f32[48,1536]{1,0:T(8,128)}, f32[48,1536]{1,0:T(8,128)}, f32[48,768]{1,0:T(8,128)}, f32[48,768]{1,0:T(8,128)}, f32[48,768]{1,0:T(8,128)}, /*ind...) custom-call(bf16[4,2,2,48,1536]{4,3,2,1,0:T(8,128)(2,1)} %bitcast.31, ...), custom_call_target="tpu_custom_call" | custom-call | tf_op jit(solution)/shard_map/pallas_call | solution.py:244
  829.3 5.5 scatter_custom_fusion.1
  834.8 11.1 %multiply_subtract_fusion = (f32[3968,256]{1,0:T(8,128)}, f32[3968,256]{1,0:T(8,128)}, f32[3968,256]{1,0:T(8,128)}) fusion(f32[3968,256]{1,0:T(8,128)} %param.59, f32[3968,256]{1,0:T(8,128)} %scatter_custom_fusion.1, f32[3968,256]{1,0:T(8,128)} %param.61, f32[3968,256]{1,0:T(8,128)} %param.60), kind=kLoop, calls=%fused_computation.48 | loop fusion | flops 15237120 | bytes 28442624 | tf_op jit(solution)/shard_map/sub | solution.py:340
  (471 shorter events, 182.7 us)
Async XLA Ops:
  1.6 11.2 %copy-start.49 = (f32[2,1536,48]{1,2,0:T(8,128)S(1)}, f32[2,1536,48]{1,2,0:T(8,128)}, u32[]{:S(2)}) copy-start(f32[2,1536,48]{1,2,0:T(8,128)} %param.47) | copy-start | bytes 1769476
  1.6 11.9 %copy-start.89 = (f32[16,768]{1,0:T(8,128)S(1)}, f32[16,768]{1,0:T(8,128)}, u32[]{:S(2)}) copy-start(f32[16,768]{1,0:T(8,128)} %param.53) | copy-start | bytes 147460
  1.6 12.5 %copy-start.91 = (f32[48,256]{1,0:T(8,128)S(1)}, f32[48,256]{1,0:T(8,128)}, u32[]{:S(2)}) copy-start(f32[48,256]{1,0:T(8,128)} %param.56) | copy-start | bytes 147460
  1.6 13.7 %copy-start.124 = (s32[16,16]{1,0:T(8,128)S(1)}, s32[16,16]{1,0:T(8,128)}, u32[]{:S(2)}) copy-start(s32[16,16]{1,0:T(8,128)} %param.36) | copy-start | bytes 3076
  3.8 15.5 %all-to-all-start = ((s32[16,1,8]{2,1,0:T(1,128)}), s32[16,1,8]{2,1,0:T(1,128)S(1)}, u32[]{:S(2)}, u32[]{:S(2)}) async-start(s32[16,1,8]{2,1,0:T(1,128)} %copy.170), calls=%async_computation | async-start | bytes 16384 | tf_op jit(solution)/shard_map/all_to_all | solution.py:1198
  17.8 24.3 %copy-start.3 = (bf16[3968,256]{1,0:T(8,128)(2,1)}, bf16[3968,256]{1,0:T(8,128)(2,1)S(1)}, u32[]{:S(2)}) copy-start(bf16[3968,256]{1,0:T(8,128)(2,1)S(1)} %convert_element_type.289) | copy-start | bytes 6094852
  17.8 23.5 %copy-start.24 = (f32[2,6,48,384]{3,2,1,0:T(8,128)S(1)}, f32[2,6,48,384]{3,2,1,0:T(8,128)}, u32[]{:S(2)}) copy-start(f32[2,6,48,384]{3,2,1,0:T(8,128)} %param.38) | copy-start | bytes 2654212
  19.6 22.5 %copy-start.114 = (pred[16,8]{1,0:T(8,128)(4,1)}, pred[16,8]{1,0:T(8,128)(4,1)S(1)}, u32[]{:S(2)}) copy-start(pred[16,8]{1,0:T(8,128)(4,1)S(1)} %copy.172) | copy-start | bytes 388
  21.6 20.5 %copy-start.47 = (f32[2,48,1536]{2,1,0:T(8,128)S(1)}, f32[2,48,1536]{2,1,0:T(8,128)}, u32[]{:S(2)}) copy-start(f32[2,48,1536]{2,1,0:T(8,128)} %param.44) | copy-start | bytes 1769476
  23.2 13.1 %all-to-all-start.1 = ((bf16[16,8,256]{2,1,0:T(8,128)(2,1)}), bf16[16,8,256]{2,1,0:T(8,128)(2,1)}, u32[]{:S(2)}, u32[]{:S(2)}) async-start(bf16[16,8,256]{2,1,0:T(8,128)(2,1)} %bitcast_select_fusion.1), calls=%async_computation.1 | async-start | bytes 131072 | tf_op jit(solution)/shard_map/all_to_all | solution.py:1204
  28.7 15.5 %copy-start.127 = (f32[128]{0:T(128)}, f32[128]{0:T(128)S(1)}, u32[]{:S(2)}) copy-start(f32[128]{0:T(128)S(1)} %convert_subtract_fusion) | copy-start | bytes 1540
  38.0 6.2 collective-permute-start
  261.5 11.6 %copy-start.85 = (bf16[16,768]{1,0:T(8,128)(2,1)}, bf16[16,768]{1,0:T(8,128)(2,1)S(1)}, u32[]{:S(2)}) copy-start(bf16[16,768]{1,0:T(8,128)(2,1)S(1)} %gather_fusion.2) | copy-start | bytes 73732
  312.8 45.6 %collective-permute-start.1 = (f32[16,256]{1,0:T(8,128)}, f32[16,256]{1,0:T(8,128)}, u32[]{:S(2)}, u32[]{:S(2)}) collective-permute-start(f32[16,256]{1,0:T(8,128)} %reduce_sum.211), channel_id=1, source_target_pairs={{0,1},{1,0},{2,3},{3,2},{4,5},{5,4},{6,7},{7,6},{8,9},{9,8},{10,11... | collective-permute-start | bytes 49160 | tf_op jit(solution)/shard_map/ppermute | solution.py:1284
  318.3 15.6 %copy-start.18 = (bf16[896,384]{0,1:T(8,128)(2,1)}, bf16[896,384]{0,1:T(8,128)(2,1)S(1)}, u32[]{:S(2)}) copy-start(bf16[896,384]{0,1:T(8,128)(2,1)S(1)} %copy.178) | copy-start | bytes 2064388
  322.7 11.2 %copy-start.15 = (bf16[1024,384]{0,1:T(8,128)(2,1)}, bf16[1024,384]{0,1:T(8,128)(2,1)S(1)}, u32[]{:S(2)}) copy-start(bf16[1024,384]{0,1:T(8,128)(2,1)S(1)} %copy.179) | copy-start | bytes 2359300
  330.4 12.4 %copy-start.26 = (bf16[1024,384]{0,1:T(8,128)(2,1)}, bf16[1024,384]{0,1:T(8,128)(2,1)S(1)}, u32[]{:S(2)}) copy-start(bf16[1024,384]{0,1:T(8,128)(2,1)S(1)} %copy.191) | copy-start | bytes 2359300
  331.6 11.3 %copy-start.59 = (bf16[128,384]{0,1:T(8,128)(2,1)}, bf16[128,384]{0,1:T(8,128)(2,1)S(1)}, u32[]{:S(2)}) copy-start(bf16[128,384]{0,1:T(8,128)(2,1)S(1)} %copy.192) | copy-start | bytes 294916
  347.8 11.4 %copy-start.56 = (bf16[1,4,2,2,48,256]{5,4,3,2,1,0:T(8,128)(2,1)S(1)}, bf16[1,4,2,2,48,256]{5,4,3,2,1,0:T(8,128)(2,1)}, u32[]{:S(2)}) copy-start(bf16[1,4,2,2,48,256]{5,4,3,2,1,0:T(8,128)(2,1)} %get-tuple-element.74) | copy-start | bytes 1179652
  347.8 12.3 %copy-start.2 = (f32[1024,768]{1,0:T(8,128)S(1)}, f32[1024,768]{1,0:T(8,128)}, u32[]{:S(2)}) copy-start(f32[1024,768]{1,0:T(8,128)} %bitcast_convert_fusion) | copy-start | bytes 9437188
  374.8 14.4 %collective-permute-start.2 = (bf16[1024,768]{1,0:T(8,128)(2,1)S(1)}, bf16[1024,768]{1,0:T(8,128)(2,1)S(1)}, u32[]{:S(2)}, u32[]{:S(2)}) collective-permute-start(bf16[1024,768]{1,0:T(8,128)(2,1)S(1)} %convolution_convert_fusion.5), channel_id=1, source_target_pairs={{0,1},{1,0},{2,3},{3,2},{4,5},{5,4},{6,7},{7,6},{8,9},{9,8},{10,11... | collective-permute-start | bytes 4718600 | tf_op jit(solution)/shard_map/ppermute | solution.py:378
  478.8 15.9 %collective-permute-start.3 = (bf16[1024,768]{1,0:T(8,128)(2,1)}, bf16[1024,768]{1,0:T(8,128)(2,1)}, u32[]{:S(2)}, u32[]{:S(2)}) collective-permute-start(bf16[1024,768]{1,0:T(8,128)(2,1)} %fusion.45), channel_id=1, source_target_pairs={{0,1},{1,0},{2,3},{3,2},{4,5},{5,4},{6,7},{7,6},{8,9},{9,8},{10,11... | collective-permute-start | bytes 4718600 | tf_op jit(solution)/shard_map/ppermute | solution.py:378
  504.9 13.2 %collective-permute-start.4 = (bf16[1024,768]{1,0:T(8,128)(2,1)S(1)}, bf16[1024,768]{1,0:T(8,128)(2,1)S(1)}, u32[]{:S(2)}, u32[]{:S(2)}) collective-permute-start(bf16[1024,768]{1,0:T(8,128)(2,1)S(1)} %convolution_convert_fusion.4), channel_id=1, source_target_pairs={{0,1},{1,0},{2,3},{3,2},{4,5},{5,4},{6,7},{7,6},{8,9},{9,8},{10,11... | collective-permute-start | bytes 4718600 | tf_op jit(solution)/shard_map/ppermute | solution.py:378
  607.6 12.0 %collective-permute-start.5 = (bf16[1024,768]{1,0:T(8,128)(2,1)}, bf16[1024,768]{1,0:T(8,128)(2,1)}, u32[]{:S(2)}, u32[]{:S(2)}) collective-permute-start(bf16[1024,768]{1,0:T(8,128)(2,1)} %fusion.46), channel_id=1, source_target_pairs={{0,1},{1,0},{2,3},{3,2},{4,5},{5,4},{6,7},{7,6},{8,9},{9,8},{10,11... | collective-permute-start | bytes 4718600 | tf_op jit(solution)/shard_map/ppermute | solution.py:378
  624.9 188.4 %copy-start.79 = (bf16[1,4,2,2,16,768]{5,4,3,2,1,0:T(8,128)(2,1)S(1)}, bf16[1,4,2,2,16,768]{5,4,3,2,1,0:T(8,128)(2,1)}, u32[]{:S(2)}) copy-start(bf16[1,4,2,2,16,768]{5,4,3,2,1,0:T(8,128)(2,1)} %get-tuple-element.119) | copy-start | bytes 1179652
  624.9 188.4 %copy-start.128 = (f32[128]{0:T(128)S(1)}, f32[128]{0:T(128)}, u32[]{:S(2)}) copy-start(f32[128]{0:T(128)} %copy-done.127) | copy-start | bytes 1540
  624.9 189.7 %copy-start.97 = (s32[1024]{0:T(1024)S(1)}, s32[1024]{0:T(1024)}, u32[]{:S(2)}) copy-start(s32[1024]{0:T(1024)} %copy-done.96) | copy-start | bytes 12292
  801.7 13.7 %copy-start.123 = (pred[16,8]{1,0:T(8,128)(4,1)S(1)}, pred[16,8]{1,0:T(8,128)(4,1)}, u32[]{:S(2)}) copy-start(pred[16,8]{1,0:T(8,128)(4,1)} %copy.201) | copy-start | bytes 388
  801.8 18.1 %copy-start.25 = (f32[2,6,48,384]{3,2,1,0:T(8,128)S(1)}, f32[2,6,48,384]{3,2,1,0:T(8,128)}, u32[]{:S(2)}) copy-start(f32[2,6,48,384]{3,2,1,0:T(8,128)} %param.38) | copy-start | bytes 2654212
  801.8 18.1 %copy-start.63 = (f32[2,6,48,384]{3,2,1,0:T(8,128)S(1)}, f32[2,6,48,384]{3,2,1,0:T(8,128)}, u32[]{:S(2)}) copy-start(f32[2,6,48,384]{3,2,1,0:T(8,128)} %param.40) | copy-start | bytes 2654212
  816.2 13.1 %all-to-all-start.2 = ((bf16[16,8,256]{2,1,0:T(8,128)(2,1)}), bf16[16,8,256]{2,1,0:T(8,128)(2,1)S(1)}, u32[]{:S(2)}, u32[]{:S(2)}) async-start(bf16[16,8,256]{2,1,0:T(8,128)(2,1)} %fusion.143), calls=%async_computation.2 | async-start | bytes 131072 | tf_op jit(solution)/shard_map/all_to_all | solution.py:1334
  834.8 11.1 %copy-start.1 = (s32[128]{0:T(128)S(1)}, s32[128]{0:T(128)}, u32[]{:S(2)}) copy-start(s32[128]{0:T(128)} %param.33) | copy-start | bytes 1540
  (115 other events, 490.4 us)

commit v3 on v2

--- a/solution.py
+++ b/solution.py
@@ -795,7 +795,7 @@
     shards = take(len(needs["kinds"]))
     kept = take(len(needs["kinds"]))
     saved = [dict(zip(SAVED, take(len(SAVED)))) for _ in range(LAYERS)]
-    (ents_out,) = take(1)
+    ents_out, gains_out = take(2)
     wholes = take(len(needs["kinds"]))
     act = dict(zip(SAVED, take(len(SAVED))))
     x, h1, gains, mine, theirs = take(5)
@@ -915,6 +915,7 @@
         save(layer, "n2")
         save(layer, "stats")
     ents_out[...] = x[WORDS:]
+    gains_out[...] = gains[...]
     gather.close()
     for name in list(saving):
         free(name)
@@ -960,9 +961,9 @@
         functools.partial(forward_body, dims, chunks, needs),
         out_shape=[jax.ShapeDtypeStruct(shape, low) for shape in wholes]
         + saved_out
-        + [jax.ShapeDtypeStruct((ENT_LEN, D), full)],
+        + [jax.ShapeDtypeStruct((ENT_LEN, D), full), jax.ShapeDtypeStruct((16, D), full)],
         in_specs=[VMEM] * 3 + [ANY] * len(shards),
-        out_specs=[ANY] * (len(wholes) + len(saved_out)) + [VMEM],
+        out_specs=[ANY] * (len(wholes) + len(saved_out)) + [VMEM] * 2,
         scratch_shapes=[pltpu.VMEM(shape, low) for shape in wholes]
         + [pltpu.VMEM(*shapes[name]) for name in SAVED]
         + [
@@ -988,7 +989,7 @@
         dict(zip(SAVED, result[len(wholes) + layer * len(SAVED) :][: len(SAVED)]))
         for layer in range(LAYERS)
     ]
-    return kept, saved, result[-1]
+    return kept, saved, *result[-2:]
 
 
 def norm_back(grad, hat, scale, gain_row):
@@ -996,58 +997,491 @@
     wide = grad * gain_row
     inner = jnp.mean(wide * hat, axis=-1, keepdims=True)
     back = scale * (wide - jnp.mean(wide, axis=-1, keepdims=True) - hat * inner)
-    return back, jnp.sum(grad * hat, axis=0), jnp.sum(grad, axis=0)
-
-
-def saved_backward(grad_out, saved, attn_mats, out_mat, up_mat, down_mat, gain_rows):
-    low = jnp.bfloat16
-    stats = saved["stats"]
-    heads = saved["k"].shape[1] // HEAD_DIM
-    grad_second, gain_late, shift_late = norm_back(
-        grad_out, saved["n2"], stats[:, 9:10], gain_rows[2]
-    )
-    grad_outer = grad_second.astype(low)
-    grad_down = mm_lt(grad_outer, saved["g"])
-    grad_pre = (mm(grad_outer, down_mat) * saved["slope"].astype(jnp.float32)).astype(low)
-    grad_up = mm_lt(saved["h1b"], grad_pre)
-    grad_first = grad_second + pair_sum(mm_rt(grad_pre, up_mat))
-    grad_first_in, gain_early, shift_early = norm_back(
-        grad_first, saved["n1"], stats[:, 8:9], gain_rows[0]
-    )
-    grad_attended = grad_first_in.astype(low)
-    grad_out_mat = mm_lt(grad_attended, saved["o"])
-    grad_mixed = mm(grad_attended, out_mat).astype(low)
-
-    def heads_of(values):
-        return values.reshape(LEN, heads, HEAD_DIM)
-
-    log_norm = stats[:, :heads].T / LOG2E
-    parts = attend_backward(
-        (
-            heads_of(saved["qw"]),
-            heads_of(saved["qe"]),
-            heads_of(saved["k"]),
-            heads_of(saved["v"]),
-            log_norm,
-            heads_of(grad_mixed),
-        )
-    )
-    grad_qw, grad_qe, grad_key, grad_value = [
-        part.reshape(LEN, heads * HEAD_DIM).astype(low) for part in parts
-    ]
-    xb = saved["xb"]
-    grad_mats = (
-        mm_lt(xb[:WORDS], jnp.concatenate([grad_qw[:WORDS], grad_qe[:WORDS]], axis=1)),
-        mm_lt(xb[WORDS:], jnp.concatenate([grad_qw[WORDS:], grad_qe[WORDS:]], axis=1)),
-        mm_lt(xb, jnp.concatenate([grad_key, grad_value], axis=1)),
-    )
-    part_words = mm_rt(grad_qw[:WORDS], attn_mats[0]) + mm_rt(grad_qe[:WORDS], attn_mats[1])
-    part_ents = mm_rt(grad_qw[WORDS:], attn_mats[2]) + mm_rt(grad_qe[WORDS:], attn_mats[3])
-    part = jnp.concatenate([part_words, part_ents], axis=0)
-    part += mm_rt(grad_key, attn_mats[4]) + mm_rt(grad_value, attn_mats[5])
-    grad_hidden = grad_first_in + pair_sum(part)
-    grad_norms = jnp.stack([gain_early, shift_early, gain_late, shift_late])
-    return grad_hidden, (grad_mats, grad_out_mat, grad_up, grad_down, grad_norms)
+    gain_part = jnp.sum(grad * hat, axis=0, keepdims=True)
+    return back, gain_part, jnp.sum(grad, axis=0, keepdims=True)
+
+
+class Sums:
+    def __init__(self, dims, units, buffers, totals, sems, free_sem):
+        self.dims, self.units, self.totals = dims, units, totals
+        self.buffers = buffers
+        self.send_sem, self.recv_sem = sems
+        self.free_sem = free_sem
+        self.spot = place(dims)
+        self.peers = [axis_peers(dims, axis) for axis in range(3)]
+        self.queue, self.done = [], set()
+        self.least = 2
+
+    def group(self, stage, y_first):
+        return self.peers[((1, 2, 0) if y_first else (2, 1, 0))[stage]]
+
+    def start(self, stage, u):
+        slot, y_first, turn = self.units[u]
+        part, first, second, third = self.buffers[slot]
+        z, y, x = self.spot
+        group = self.group(stage, y_first)
+        if turn and group:
+            pl.semaphore_wait(self.free_sem.at[slot, stage], len(group))
+        copies = []
+        base = (0, max(self.dims[1:]), 2 * max(self.dims[1:]))[stage]
+        for k, (spot, target) in enumerate(group):
+            if stage == 0:
+                src = part.at[:, spot] if y_first else part.at[:, :, spot]
+                dst = first.at[k]
+            elif stage == 1:
+                src = part.at[:, y, spot] if y_first else part.at[:, spot, x]
+                dst = second.at[k]
+            else:
+                src, dst = part.at[spot, y, x], third.at[k]
+            sems = self.send_sem.at[u, base + k], self.recv_sem.at[u, base + k]
+            copies.append(send(src, dst, *sems, target))
+        self.queue.append((stage, u, copies))
+
+    def advance(self):
+        stage, u, copies = self.queue.pop(0)
+        slot, y_first, turn = self.units[u]
+        part, first, second, third = self.buffers[slot]
+        z, y, x = self.spot
+        for copy in copies:
+            copy.wait()
+        group = self.group(stage, y_first)
+        across = self.dims[2] if y_first else self.dims[1]
+        if stage == 0 and group:
+
+            def add_first(i, carry):
+                a, b = i // across, i % across
+                at = (a, y, b) if y_first else (a, b, x)
+                value = part[at].astype(jnp.float32)
+                for k in range(len(group)):
+                    value += first[k, a, b].astype(jnp.float32)
+                part[at] = value.astype(part.dtype)
+                return carry
+
+            lax.fori_loop(0, self.dims[0] * across, add_first, 0)
+        if stage == 1 and group:
+
+            def add_second(i, carry):
+                value = part[i, y, x].astype(jnp.float32)
+                for k in range(len(group)):
+                    value += second[k, i].astype(jnp.float32)
+                part[i, y, x] = value.astype(part.dtype)
+                return carry
+
+            lax.fori_loop(0, self.dims[0], add_second, 0)
+        if stage == 2:
+            value = part[z, y, x].astype(jnp.float32)
+            for k in range(len(group)):
+                value += third[k].astype(jnp.float32)
+            self.totals[u][...] = value
+            self.done.add(u)
+        if self.reused(u):
+            for _, target in group:
+                pl.semaphore_signal(
+                    self.free_sem.at[slot, stage], inc=1, device_id=target, device_id_type=MESH
+                )
+        if stage < 2:
+            self.start(stage + 1, u)
+
+    def reused(self, u):
+        slot, _, turn = self.units[u]
+        return not turn and sum(unit[0] == slot for unit in self.units) > 1
+
+    def tick(self):
+        if len(self.queue) > self.least:
+            self.advance()
+
+    def need(self, u):
+        while u not in self.done:
+            self.advance()
+
+    def close(self):
+        while self.queue:
+            self.advance()
+
+
+UNITS = ("down0", "down1", "up0", "up1", "out", "words", "ents", "key", "value")
+EXTRA = ("head", "proj", "norms")
+UNIT_FIRST = dict(
+    down0=True, down1=False, up0=True, up1=False, out=True, words=True, ents=False, key=True,
+    value=False, head=True, proj=False, norms=True,
+)
+
+
+def sum_plan():
+    names = ["head"]
+    for layer in reversed(range(LAYERS)):
+        names += [(layer, name) for name in UNITS]
+    names += ["proj", "norms"]
+    return names
+
+
+def unit_width(name, half, hidden):
+    return {
+        "down0": hidden // 2, "down1": hidden // 2, "up0": hidden // 2, "up1": hidden // 2,
+        "out": half, "words": 2 * half, "ents": 2 * half, "key": half, "value": half,
+    }[name]
+
+
+def backward_body(dims, names, half, hidden, *refs):
+    refs = list(refs)
+
+    def take(count):
+        part = refs[:count]
+        del refs[:count]
+        return part
+
+    cotangent, grad_ents, grad_head, gains, entity_rows = take(5)
+    w_attn, w_out, w_up, w_down, w_proj = take(5)
+    saved = [dict(zip(SAVED, take(len(SAVED)))) for _ in range(LAYERS)]
+    word_grads, row_grads = take(2)
+    totals = take(len(names))
+    slots = list(UNITS + EXTRA)
+    buffers = [take(4) for _ in slots]
+    left, right, hat, xh, o, stats, stats_t = take(7)
+    mat_wide, mat_out, mat_attn, mat_proj = take(4)
+    gacc, glow, gmix, delta, dk_acc, dv_acc, gnorm = take(7)
+    mine, theirs = take(2)
+    sum_sems = take(2)
+    (free_sem,) = take(1)
+    pair_sems = take(2)
+    (load_sem,) = take(1)
+
+    units = []
+    for name in names:
+        kind = name if isinstance(name, str) else name[1]
+        turn = not isinstance(name, str) and name[0] < LAYERS - 1
+        units.append((slots.index(kind), UNIT_FIRST[kind], turn))
+    sums = Sums(dims, units, buffers, totals, sum_sems, free_sem)
+    pair = Pair(mine, theirs, pair_sems)
+    greet([target for group in sums.peers for _, target in group] + [pair.other])
+    part_of = {slot: buffers[i][0] for i, slot in enumerate(slots)}
+    loads, counter = {}, [0]
+
+    def load(key, src, dst):
+        copy = pltpu.make_async_copy(src, dst, load_sem.at[counter[0]])
+        counter[0] += 1
+        copy.start()
+        loads.setdefault(key, []).append(copy)
+
+    def ready(key):
+        for copy in loads.pop(key, []):
+            copy.wait()
+
+    def tick(times=1):
+        for _ in range(times):
+            sums.tick()
+
+    def begin_layer(layer):
+        s = saved[layer]
+        load("n2", s["n2"], hat)
+        load("stats", s["stats"], stats)
+        load("g", s["g"], left)
+        load("down", w_down.at[layer], mat_wide)
+        load("slope", s["slope"], right)
+        load("h1b", s["h1b"], xh)
+        load("out", w_out.at[layer], mat_out)
+        load("o", s["o"], o)
+        load("attn", w_attn.at[pl.ds(6 * layer, 6)], mat_attn)
+
+    begin_layer(LAYERS - 1)
+    load("proj", w_proj.at[0], mat_proj)
+    slab = 2 if dims[0] % 2 == 0 else 1
+    height = slab * D // dims[0]
+
+    def fill(name, lhs, rhs, rhs_cols, row_slice=slice(None)):
+        part = part_of[name]
+        width = part.shape[-1]
+
+        def block(i, carry):
+            cols = pl.ds(pl.multiple_of(i * height, 128), height)
+            value = mm_lt(lhs[row_slice, cols], rhs[row_slice, rhs_cols])
+            shape = (slab, dims[1], dims[2], part.shape[3], width)
+            part[pl.ds(i * slab, slab)] = value.astype(jnp.bfloat16).reshape(shape)
+            return carry
+
+        lax.fori_loop(0, dims[0] // slab, block, 0)
+
+    def submit(layer, name):
+        sums.start(0, names.index((layer, name)))
+
+    head_part = part_of["head"]
+    head_part[...] = grad_head[...]
+    sums.start(0, names.index("head"))
+    gacc[:WORDS] = cotangent[...].astype(jnp.float32)
+    gacc[WORDS:] = grad_ents[...]
+    gnorm[...] = jnp.zeros_like(gnorm)
+
+    def add_norm(row, value):
+        gnorm[row : row + 1, :] += value
+
+    for layer in reversed(range(LAYERS)):
+        last = layer == LAYERS - 1
+        gain = [gains[4 * layer + i : 4 * layer + i + 1, :] for i in range(4)]
+        ready("n2")
+        ready("stats")
+
+        def late_norm(c, carry):
+            rows = pl.ds(c * BLOCK, BLOCK)
+            back, gain_part, shift_part = norm_back(
+                gacc[rows, :], hat[rows, :], stats[rows, 9:10], gain[2]
+            )
+            gacc[rows, :] = back
+            glow[rows, :] = back.astype(jnp.bfloat16)
+            add_norm(4 * layer + 2, gain_part)
+            add_norm(4 * layer + 3, shift_part)
+            return carry
+
+        lax.fori_loop(0, BLOCKS, late_norm, 0)
+        load("n1", saved[layer]["n1"], hat)
+        ready("g")
+        for i in range(2):
+            if not last:
+                sums.need(names.index((layer + 1, "down%d" % i)))
+            cols = slice(i * (hidden // 2), (i + 1) * (hidden // 2))
+            fill("down%d" % i, glow, left, cols)
+            submit(layer, "down%d" % i)
+            tick()
+        ahead = saved[layer]
+        for i, name in enumerate(("k", "qw", "qe", "v")):
+            load("qkv", ahead[name], left.at[:, pl.ds(i * half, half)])
+        ready("down")
+        ready("slope")
+
+        def inner(c, carry):
+            rows = pl.ds(c * BLOCK, BLOCK)
+            for first in range(0, hidden, 512):
+                cols = slice(first, first + 512)
+                weight = mat_wide[:, :, :, :, cols].reshape(D, 512)
+                value = mm(glow[rows, :], weight) * right[rows, cols].astype(jnp.float32)
+                right[rows, cols] = value.astype(jnp.bfloat16)
+            return carry
+
+        lax.fori_loop(0, BLOCKS, inner, 0)
+        tick()
+        load("up", w_up.at[layer], mat_wide)
+        ready("h1b")
+        for i in range(2):
+            if not last:
+                sums.need(names.index((layer + 1, "up%d" % i)))
+            cols = slice(i * (hidden // 2), (i + 1) * (hidden // 2))
+            fill("up%d" % i, xh, right, cols)
+            submit(layer, "up%d" % i)
+            tick()
+        load("xb", saved[layer]["xb"], xh)
+        ready("up")
+        ready("n1")
+
+        def up_part(c, rows):
+            return mm_rt(right[rows, :], flat(mat_wide))
+
+        def early_norm(c, rows, total):
+            back, gain_part, shift_part = norm_back(
+                gacc[rows, :] + total, hat[rows, :], stats[rows, 8:9], gain[0]
+            )
+            gacc[rows, :] = back
+            glow[rows, :] = back.astype(jnp.bfloat16)
+            add_norm(4 * layer, gain_part)
+            add_norm(4 * layer + 1, shift_part)
+
+        pair.run(up_part, early_norm, tick)
+        ready("o")
+        ready("out")
+        if not last:
+            sums.need(names.index((layer + 1, "out")))
+        fill("out", glow, o, slice(None))
+        submit(layer, "out")
+
+        def mixed(c, carry):
+            rows = pl.ds(c * BLOCK, BLOCK)
+            gmix[rows, :] = mm(glow[rows, :], flat(mat_out)).astype(jnp.bfloat16)
+            stats_t[:, rows] = stats[rows, :].T
+            return carry
+
+        lax.fori_loop(0, BLOCKS, mixed, 0)
+        tick()
+        ready("qkv")
+        for head_pair in range(half // (2 * HEAD_DIM)):
+            lo = head_pair * 2 * HEAD_DIM
+            lanes = slice(lo, lo + 2 * HEAD_DIM)
+            k_lanes, qw_lanes, qe_lanes, v_lanes = [
+                slice(j * half + lo, j * half + lo + 2 * HEAD_DIM) for j in range(4)
+            ]
+
+            def products(c, carry):
+                rows = pl.ds(c * BLOCK, BLOCK)
+                both = gmix[rows, lanes].astype(jnp.float32) * o[rows, lanes].astype(jnp.float32)
+                turned = both.T
+                delta[0:1, rows] = jnp.sum(turned[:HEAD_DIM], axis=0, keepdims=True)
+                delta[1:2, rows] = jnp.sum(turned[HEAD_DIM:], axis=0, keepdims=True)
+                return carry
+
+            lax.fori_loop(0, BLOCKS, products, 0)
+            dk_acc[...] = jnp.zeros_like(dk_acc)
+            dv_acc[...] = jnp.zeros_like(dv_acc)
+
+            def block(i, carry):
+                rows = pl.ds(i * BLOCK, BLOCK)
+                keys, values = left[:, k_lanes], left[:, v_lanes]
+                grad_qw = grad_qe = None
+                for which in range(2):
+                    head = 2 * head_pair + which
+                    q_mask, k_mask = lane_mask(BLOCK, which), lane_mask(LEN, which)
+                    query_w = left[rows, qw_lanes] * q_mask
+                    query_e = left[rows, qe_lanes] * q_mask
+                    grad_o = gmix[rows, lanes] * q_mask
+                    log_row = stats_t[head : head + 1, rows]
+                    inner_row = delta[which : which + 1, rows]
+                    own_keys = keys * k_mask
+                    for span, query in ((slice(0, WORDS), query_w), (slice(WORDS, LEN), query_e)):
+                        prob = jnp.exp2(mm_rt(keys[span], query) * SCORE_STEP - log_row)
+                        grad_prob = mm_rt(values[span], grad_o)
+                        dv_acc[span, :] += mm(prob.astype(jnp.bfloat16), grad_o)
+                        grad_score = (prob * (grad_prob - inner_row)).astype(jnp.bfloat16)
+                        dk_acc[span, :] += mm(grad_score, query)
+                        part = mm_lt(grad_score, own_keys[span])
+                        if span.start == 0:
+                            grad_qw = part if grad_qw is None else grad_qw + part
+                        else:
+                            grad_qe = part if grad_qe is None else grad_qe + part
+                right[rows, lanes] = (grad_qw * 0.125).astype(jnp.bfloat16)
+                right[rows, half + lo : half + lo + 2 * HEAD_DIM] = (grad_qe * 0.125).astype(
+                    jnp.bfloat16
+                )
+                return carry
+
+            for first in range(0, BLOCKS, 2):
+                lax.fori_loop(first, first + 2, block, 0)
+                tick()
+            at = 2 * half + lo
+            right[:, at : at + 2 * HEAD_DIM] = (dk_acc[...] * 0.125).astype(jnp.bfloat16)
+            at = 3 * half + lo
+            right[:, at : at + 2 * HEAD_DIM] = dv_acc[...].astype(jnp.bfloat16)
+        ready("xb")
+        words, ents = slice(0, WORDS), slice(WORDS, LEN)
+        for name, cols, rows in (
+            ("words", slice(0, 2 * half), words),
+            ("ents", slice(0, 2 * half), ents),
+            ("key", slice(2 * half, 3 * half), slice(None)),
+            ("value", slice(3 * half, 4 * half), slice(None)),
+        ):
+            if not last:
+                sums.need(names.index((layer + 1, name)))
+            fill(name, xh, right, cols, rows)
+            submit(layer, name)
+            tick()
+        ready("attn")
+        mats = [slice(j * half, (j + 1) * half) for j in range(4)]
+
+        def input_part(c, rows):
+            total = mm_rt(right[rows, mats[2]], flat(mat_attn, 4))
+            total += mm_rt(right[rows, mats[3]], flat(mat_attn, 5))
+            start = c * BLOCK
+            edge = min(max(WORDS - start, 0), BLOCK)
+            pieces = []
+            for low, high, pick in ((0, edge, (0, 1)), (edge, BLOCK, (2, 3))):
+                if high > low:
+                    span = slice(start + low, start + high)
+                    piece = mm_rt(right[span, mats[0]], flat(mat_attn, pick[0]))
+                    pieces.append(piece + mm_rt(right[span, mats[1]], flat(mat_attn, pick[1])))
+            return total + (pieces[0] if len(pieces) == 1 else jnp.concatenate(pieces, axis=0))
+
+        def to_input(c, rows, total):
+            gacc[rows, :] += total
+
+        pair.run(input_part, to_input, tick)
+        if layer:
+            begin_layer(layer - 1)
+    ready("proj")
+    leaving = pltpu.make_async_copy(gacc.at[pl.ds(0, WORDS)], word_grads, load_sem.at[counter[0]])
+    leaving.start()
+    grad_entity = gacc[WORDS:].astype(jnp.bfloat16)
+    proj_part = part_of["proj"]
+    proj_part[...] = mm_lt(entity_rows[...], grad_entity).astype(jnp.bfloat16).reshape(proj_part.shape)
+    sums.start(0, names.index("proj"))
+    count = dims[0] * dims[1] * dims[2]
+    width = D // count
+    norm_low = gnorm[...].astype(jnp.bfloat16)
+    for d in range(count):
+        z, rest = d // (dims[1] * dims[2]), d % (dims[1] * dims[2])
+        row = lax.broadcasted_iota(jnp.int32, (128, D), 0)
+        lane = lax.broadcasted_iota(jnp.int32, (128, D), 1)
+        hot = jnp.where((row + d * width == lane) & (row < width), 1.0, 0.0).astype(jnp.bfloat16)
+        block = mm_rt(norm_low, hot).astype(jnp.bfloat16)
+        part_of["norms"][z, rest // dims[2], rest % dims[2]] = block
+    sums.start(0, names.index("norms"))
+    row_grads[...] = mm_rt(grad_entity, flat(mat_proj))
+    sums.close()
+    leaving.wait()
+
+
+def run_backward(dims, cotangent, grad_ents, grad_head, gains, entity_rows, kept, saved, collective_id):
+    names = sum_plan()
+    half, hidden = kept[0].shape[-1], kept[2].shape[-1]
+    low, full = jnp.bfloat16, jnp.float32
+    rows = kept[0].shape[4]
+    blocks = {name: (rows, unit_width(name, half, hidden)) for name in UNITS}
+    blocks["head"] = (rows, kept[5].shape[-1])
+    blocks["proj"] = (kept[4].shape[4], D)
+    blocks["norms"] = (16, 128)
+    scratch = []
+    for name in UNITS + EXTRA:
+        y_first = UNIT_FIRST[name]
+        own = (dims[0], dims[2] if y_first else dims[1])
+        turns = (dims[1], dims[2]) if y_first else (dims[2], dims[1])
+        block = blocks[name]
+        scratch += [
+            pltpu.VMEM((*dims, *block), low),
+            pltpu.VMEM((max(turns[0] - 1, 1), *own, *block), low),
+            pltpu.VMEM((max(turns[1] - 1, 1), dims[0], *block), low),
+            pltpu.VMEM((max(dims[0] - 1, 1), *block), low),
+        ]
+    copies = dims[0] + 2 * max(dims[1:])
+    kinds = [name if isinstance(name, str) else name[1] for name in names]
+    inputs = [cotangent, grad_ents, grad_head, gains, entity_rows, *kept[:5]]
+    inputs += [saved[layer][name] for layer in range(LAYERS) for name in SAVED]
+    result = pl.pallas_call(
+        functools.partial(backward_body, dims, names, half, hidden),
+        out_shape=[
+            jax.ShapeDtypeStruct((WORDS, D), full),
+            jax.ShapeDtypeStruct((ENT_LEN, kept[5].shape[-1]), full),
+        ]
+        + [jax.ShapeDtypeStruct(blocks[kind], full) for kind in kinds],
+        in_specs=[VMEM] * 5 + [ANY] * (len(inputs) - 5),
+        out_specs=[ANY] + [VMEM] * (1 + len(names)),
+        scratch_shapes=scratch
+        + [
+            pltpu.VMEM((LEN, hidden), low),
+            pltpu.VMEM((LEN, hidden), low),
+            pltpu.VMEM((LEN, D), low),
+            pltpu.VMEM((LEN, D), low),
+            pltpu.VMEM((LEN, half), low),
+            pltpu.VMEM((LEN, 128), full),
+            pltpu.VMEM((128, LEN), full),
+            pltpu.VMEM(kept[2].shape[1:], low),
+            pltpu.VMEM(kept[1].shape[1:], low),
+            pltpu.VMEM((6, *kept[0].shape[1:]), low),
+            pltpu.VMEM(kept[4].shape[1:], low),
+            pltpu.VMEM((LEN, D), full),
+            pltpu.VMEM((LEN, D), low),
+            pltpu.VMEM((LEN, half), low),
+            pltpu.VMEM((8, LEN), full),
+            pltpu.VMEM((LEN, 2 * HEAD_DIM), full),
+            pltpu.VMEM((LEN, 2 * HEAD_DIM), full),
+            pltpu.VMEM((16, D), full),
+            pltpu.VMEM((BLOCKS, BLOCK, D), low),
+            pltpu.VMEM((2, BLOCKS, BLOCK, D), low),
+            pltpu.SemaphoreType.DMA((len(names), copies)),
+            pltpu.SemaphoreType.DMA((len(names), copies)),
+            pltpu.SemaphoreType.REGULAR((len(UNITS + EXTRA), 3)),
+            pltpu.SemaphoreType.DMA((2 * LAYERS, BLOCKS)),
+            pltpu.SemaphoreType.DMA((2 * LAYERS, BLOCKS)),
+            pltpu.SemaphoreType.DMA((64,)),
+        ],
+        compiler_params=pltpu.CompilerParams(
+            collective_id=collective_id, has_side_effects=True, vmem_limit_bytes=VMEM_BYTES
+        ),
+    )(*inputs)
+    return result[0], result[1], dict(zip(names, result[2:]))
 
 
 def padded_rows(values):
@@ -1151,6 +1585,30 @@
     )
 
 
+def fused_sums(totals, width):
+    layers = range(LAYERS)
+
+    def halves(name):
+        parts = [totals[layer, name] for layer in layers]
+        cut = parts[0].shape[1] // 2
+        return [[part[:, :cut], part[:, cut:]] for part in parts]
+
+    words, ents = halves("words"), halves("ents")
+    attn = jnp.stack(
+        [
+            jnp.stack(words[layer] + ents[layer] + [totals[layer, "key"], totals[layer, "value"]])
+            for layer in layers
+        ]
+    )
+    ups = jnp.stack([jnp.concatenate([totals[i, "up0"], totals[i, "up1"]], axis=1) for i in layers])
+    downs = jnp.stack(
+        [jnp.concatenate([totals[i, "down0"], totals[i, "down1"]], axis=1).T for i in layers]
+    )
+    outs = jnp.stack([totals[i, "out"].T for i in layers])
+    norms = totals["norms"][: LAYERS * 4, :width].reshape(LAYERS, 4, width)
+    return attn, outs, ups, downs, norms, totals["proj"], totals["head"]
+
+
 def on_device(
     word_inputs,
     entity_base,
@@ -1217,16 +1675,15 @@
     ).astype(jnp.float32)
     entity_rows = (paired * keep_weight[:, None]).astype(jnp.bfloat16)
     if fused:
-        wholes, saved_layers, ents = run_forward(
+        wholes, saved_layers, ents, gain_rows = run_forward(
             dims, word_inputs, entity_base, entity_rows, shards, 6
         )
     else:
         wholes = gather_apart(dims, shards)
-    attn_low, out_low, up_low, down_low, norm_low, proj_low, head_low = unpack_weights(
-        wholes, heights, norm_params.shape[-1]
-    )
-    gain_all = norm_low.astype(jnp.float32)
-    if not fused:
+        attn_low, out_low, up_low, down_low, norm_low, proj_low, head_low = unpack_weights(
+            wholes, heights, norm_params.shape[-1]
+        )
+        gain_all = norm_low.astype(jnp.float32)
         entity_inputs = entity_base.astype(jnp.float32) + jnp.dot(
             entity_rows, proj_low, preferred_element_type=jnp.float32
         )
@@ -1249,6 +1706,8 @@
             )
             saved_layers.append(saved_acts)
         ents = hidden[0, WORDS:]
+    if fused:
+        head_low = wholes[5].reshape(-1, wholes[5].shape[-1])
     seq_index = jnp.arange(SEQ_DEV, dtype=jnp.int32)[:, None]
     masked_rows = WORDS + mask_positions
     masked_low = ents[mask_positions.reshape(-1)].astype(jnp.bfloat16)
@@ -1289,56 +1748,73 @@
     grad_masked = lax.dot_general(
         grad_head_pre, head_low, (((1,), (1,)), ((), ())), preferred_element_type=jnp.float32
     )
-    grad_hidden = jnp.concatenate(
-        [
-            word_cotangent.astype(jnp.float32).reshape(SEQ_DEV, WORDS, D),
-            jnp.zeros((SEQ_DEV, ENT_LEN, D), jnp.float32),
-        ],
-        axis=1,
-    )
-    grad_hidden = grad_hidden.at[seq_index, masked_rows].add(
-        grad_masked.reshape(SEQ_DEV, MASK_ENT, D)
-    )
-    kept_grads = []
-    for layer_index in reversed(range(LAYERS)):
-        grad_hidden, layer_grads = (saved_backward if fused else layer_backward)(
-            grad_hidden[0] if fused else grad_hidden,
-            saved_layers[layer_index],
-            attn_low[layer_index],
-            out_low[layer_index],
-            up_low[layer_index],
-            down_low[layer_index],
-            gain_all[layer_index],
+    if fused:
+        hits = (
+            jnp.arange(slot_total, dtype=jnp.int32)[:, None] == mask_positions.reshape(-1)[None, :]
+        ).astype(jnp.float32)
+        grad_ents = jnp.dot(hits, grad_masked, precision=lax.Precision.HIGHEST)
+        word_grads, row_grads, totals = run_backward(
+            dims,
+            word_cotangent,
+            grad_ents,
+            grad_head.astype(jnp.bfloat16).reshape(*dims, -1, grad_head.shape[-1]),
+            gain_rows,
+            entity_rows,
+            wholes,
+            saved_layers,
+            8,
         )
-        if fused:
-            grad_hidden = grad_hidden[None]
-        if layer_index == 0:
-            word_grads = grad_hidden[:, :WORDS].reshape(SEQ_DEV * WORDS, D)
-            grad_entity = grad_hidden[:, WORDS:].reshape(slot_total, D).astype(jnp.bfloat16)
-            grad_proj = lax.dot_general(
-                entity_rows,
-                grad_entity,
-                (((0,), (0,)), ((), ())),
-                preferred_element_type=jnp.float32,
+        row_gradient_block = row_grads * keep_weight[:, None]
+        reduced = fused_sums(totals, norm_params.shape[-1])
+    else:
+        grad_hidden = jnp.concatenate(
+            [
+                word_cotangent.astype(jnp.float32).reshape(SEQ_DEV, WORDS, D),
+                jnp.zeros((SEQ_DEV, ENT_LEN, D), jnp.float32),
+            ],
+            axis=1,
+        )
+        grad_hidden = grad_hidden.at[seq_index, masked_rows].add(
+            grad_masked.reshape(SEQ_DEV, MASK_ENT, D)
+        )
+        kept_grads = []
+        for layer_index in reversed(range(LAYERS)):
+            grad_hidden, layer_grads = layer_backward(
+                grad_hidden,
+                saved_layers[layer_index],
+                attn_low[layer_index],
+                out_low[layer_index],
+                up_low[layer_index],
+                down_low[layer_index],
+                gain_all[layer_index],
             )
-            row_gradient_block = (
-                lax.dot_general(
+            if layer_index == 0:
+                word_grads = grad_hidden[:, :WORDS].reshape(SEQ_DEV * WORDS, D)
+                grad_entity = grad_hidden[:, WORDS:].reshape(slot_total, D).astype(jnp.bfloat16)
+                grad_proj = lax.dot_general(
+                    entity_rows,
                     grad_entity,
-                    proj_low,
-                    (((1,), (1,)), ((), ())),
+                    (((0,), (0,)), ((), ())),
                     preferred_element_type=jnp.float32,
                 )
-                * keep_weight[:, None]
-            )
-            outgoing = jnp.where(filled[:, :, None], row_gradient_block[safe_slot], 0.0)
-            incoming = lax.all_to_all(
-                outgoing.astype(jnp.bfloat16), "dp", split_axis=0, concat_axis=0, tiled=True
-            ).astype(outgoing.dtype)
-            grad_table = grad_table.at[safe_row].add(
-                jnp.where(owned_mask[:, :, None], incoming, 0.0)
-            )
-        kept_grads.insert(0, layer_grads)
-    reduced = sum_all(dims, kept_grads, grad_proj, grad_head)
+                row_gradient_block = (
+                    lax.dot_general(
+                        grad_entity,
+                        proj_low,
+                        (((1,), (1,)), ((), ())),
+                        preferred_element_type=jnp.float32,
+                    )
+                    * keep_weight[:, None]
+                )
+            kept_grads.insert(0, layer_grads)
+        reduced = sum_all(dims, kept_grads, grad_proj, grad_head)
+    outgoing = jnp.where(filled[:, :, None], row_gradient_block[safe_slot], 0.0)
+    incoming = lax.all_to_all(
+        outgoing.astype(jnp.bfloat16), "dp", split_axis=0, concat_axis=0, tiled=True
+    ).astype(outgoing.dtype)
+    grad_table = grad_table.at[safe_row].add(
+        jnp.where(owned_mask[:, :, None], incoming, 0.0)
+    )
     reduced_proj, reduced_head = reduced[5:]
     attn_new = adam_update(
         attention_in, attention_in_first, attention_in_second, reduced[0], kind_rates[0]

time: 855 us -> 589 us (0.69)
  matrix products: 175 us -> 13.6 us
  other arithmetic: 149 us -> 51.4 us
  local copies, waits for them, and re-layouts: 79.1 us -> 24.3 us
  Pallas kernels: 413 us -> 463 us
    dot_general x48 -> x1, matrix products: 164 us -> 1.18 us  [on_device(): grad_ents = jnp.dot(hits, grad_masked, precision=lax.Precision.HIGHEST)]
    sub x2 -> x0, other arithmetic: 75.7 us -> none  [attend_backward(): grad_probs - inner_sum]
    pallas_call x1, Pallas kernels: 177 us -> 226 us  [run_backward(): pl.pallas_call(functools.partial(backward_body, dims, names, half, hidden...]
    slice x25 -> x1, local copies, waits for them, and re-layouts: 34.8 us -> 0.67 us  [fused_sums(): norms = totals['norms'][:LAYERS * 4, :width].reshape(LAYERS, 4, width)]
    reduce_sum x4 -> x0, other arithmetic: 12 us -> none  [norm_back(): return (back, jnp.sum(grad * hat, axis=0), jnp.sum(grad, axis=0))]
    pallas_call x6 -> x0, local copies, waits for them, and re-layouts: 10.1 us -> none  [run_forward(): pl.pallas_call(functools.partial(forward_body, dims, chunks, needs), out_...]
    unnamed x295 -> x105, local copies, waits for them, and re-layouts: 19.4 us -> 12.8 us
  transfers between devices with their start and end apart: 9 -> 5, of which waited for: 2 -> 2; matrix products, arithmetic and copies ran while one was open for 14% -> 6% of each run, Pallas kernels for 0% -> 0%
where the time goes in v3:
time: 589 us; the launch traced here: 581 us
  Pallas kernels  463 us (79%)
  other arithmetic  51.4 us (9%)
  local copies, waits for them, and re-layouts  24.3 us (4%)
  starting transfers between devices  17.9 us (3%)
  matrix products  13.6 us (2%)
  waiting for transfers between devices  9.59 us (2%)
    pallas_call x1, Pallas kernels, run_backward(): pl.pallas_call(functools.partial(backward_body, dims, names, half, hidden...  226 us
    pallas_call x1, Pallas kernels, run_forward(): pl.pallas_call(functools.partial(forward_body, dims, chunks, needs), out_...  205 us
    pallas_call x3, Pallas kernels, spread(): pl.pallas_call(functools.partial(spread_body, count, wide, swap), out_sha...  31.8 us
    sub x8, other arithmetic, adam_update(): master - kind_rate * (first_hat / (jnp.sqrt(second_hat) + adam_eps) + wei...  21.8 us
    unnamed x105, local copies, waits for them, and re-layouts  12.8 us
  transfers between devices with their start and end apart: 5, of which 2 were waited for; matrix products, arithmetic and copies ran while one was open for 6% of the time, Pallas kernels for 0%

profile of v3, /device:TPU:0, one launch (start us, length us, event | category | flops | bytes accessed | tf_op | source)
XLA Modules:
  0.0 581.5 jit_solution(4218076210459458418)
XLA Ops:
  3.7 8.3 %all-to-all-start = ((s32[16,1,8]{2,1,0:T(1,128)}), s32[16,1,8]{2,1,0:T(1,128)S(1)}, u32[]{:S(2)}, u32[]{:S(2)}) async-start(s32[16,1,8]{2,1,0:T(1,128)} %copy.92), calls=%async_computation | async-start | bytes 16384 | tf_op jit(solution)/shard_map/all_to_all | solution.py:1656
  14.7 2.4 convert_element_type.79
  17.2 2.1 all-to-all-done
  19.6 1.5 gather_fusion.1
  21.1 1.6 bitcast_select_fusion.1
  22.7 4.9 all-to-all-start.1
  27.6 7.5 %all-to-all-done.1 = bf16[16,8,256]{2,1,0:T(8,128)(2,1)} async-done(((bf16[16,8,256]{2,1,0:T(8,128)(2,1)}), bf16[16,8,256]{2,1,0:T(8,128)(2,1)}, u32[]{:S(2)}, u32[]{:S(2)}) %all-to-all-start.1) | async-done | bytes 65568 | tf_op jit(solution)/shard_map/all_to_all | solution.py:1662
  35.1 1.8 fusion.1
  40.4 1.6 multiply_convert_fusion.1.refs_2_.refs_4_
  41.9 204.8 %shard_map.494 = (bf16[12,4,2,2,48,384]{5,4,3,2,1,0:T(8,128)(2,1)}, bf16[2,4,2,2,48,384]{5,4,3,2,1,0:T(8,128)(2,1)}, bf16[2,4,2,2,48,1536]{5,4,3,2,1,0:T(8,128)(...) custom-call(bf16[896,768]{1,0:T(8,128)(2,1)} %refs_0_.2, ...), custom_call_target="tpu_custom_call" | custom-call | tf_op jit(solution)/shard_map/pallas_call | solution.py:960
  246.8 1.6 gather_fusion.2
  250.3 10.4 %shard_map.495 = bf16[16,16,256]{2,1,0:T(8,128)(2,1)} custom-call(bf16[1,16,256]{2,1,0:T(8,128)(2,1)} %get-tuple-element.166.data), custom_call_target="tpu_custom_call" | custom-call | tf_op jit(solution)/shard_map/pallas_call | solution.py:309
  260.7 2.5 fusion.47
  263.1 1.8 exponential_reduce_fusion
  265.5 10.1 %shard_map.496 = f32[32,3,256]{2,1,0:T(4,128)} custom-call(f32[1,3,256]{2,1,0:T(4,128)} %maximum_bitcast_fusion.4.data), custom_call_target="tpu_custom_call" | custom-call | tf_op jit(solution)/shard_map/pallas_call | solution.py:309
  275.6 1.3 slice_reduce_fusion
  277.5 2.0 multiply_convert_fusion
  280.8 1.4 fusion.48
  282.2 11.3 %shard_map.497 = f32[16,16,256]{2,1,0:T(8,128)} custom-call(f32[16,16,256]{2,1,0:T(8,128)} %bitcast.127), custom_call_target="tpu_custom_call" | custom-call | tf_op jit(solution)/shard_map/pallas_call | solution.py:309
  294.6 4.3 fusion.50
  301.4 226.4 %shard_map.498 = (f32[896,768]{1,0:T(8,128)}, f32[128,256]{1,0:T(8,128)}, f32[48,256]{1,0:T(8,128)}, f32[48,768]{1,0:T(8,128)}, f32[48,768]{1,0:T(8,128)}, /*ind...) custom-call(bf16[896,768]{1,0:T(8,128)(2,1)} %refs_0_.3, ...), custom_call_target="tpu_custom_call" | custom-call | tf_op jit(solution)/shard_map/pallas_call | solution.py:1442
  538.5 4.6 all-to-all-start.2
  544.9 1.5 bitcast_dynamic-update-slice_fusion.7
  546.4 1.5 bitcast_dynamic-update-slice_fusion.6
  552.1 1.6 multiply_subtract_fusion.5
  553.7 1.5 multiply_subtract_fusion.4
  555.2 3.0 multiply_subtract_fusion.1
  559.1 1.5 multiply_subtract_fusion.3
  560.6 1.5 multiply_subtract_fusion.2
  562.8 5.5 scatter_custom_fusion
  568.3 11.2 %multiply_subtract_fusion = (f32[3968,256]{1,0:T(8,128)}, f32[3968,256]{1,0:T(8,128)}, f32[3968,256]{1,0:T(8,128)}) fusion(f32[3968,256]{1,0:T(8,128)} %param.59, f32[3968,256]{1,0:T(8,128)} %scatter_custom_fusion, f32[3968,256]{1,0:T(8,128)} %param.61, f32[3968,256]{1,0:T(8,128)} %param.60), kind=kLoop, calls=%fused_computation.7 | loop fusion | flops 15237120 | bytes 28442624 | tf_op jit(solution)/shard_map/sub | solution.py:340
  579.5 1.5 copy.127
  (161 shorter events, 35.4 us)
Async XLA Ops:
  1.6 10.5 %copy-start.17 = (f32[2,384,48]{1,2,0:T(8,128)S(1)}, f32[2,384,48]{1,2,0:T(8,128)}, u32[]{:S(2)}) copy-start(f32[2,384,48]{1,2,0:T(8,128)} %param.41) | copy-start | bytes 442372
  1.6 11.1 %copy-start.10 = (f32[2,1536,48]{1,2,0:T(8,128)S(1)}, f32[2,1536,48]{1,2,0:T(8,128)}, u32[]{:S(2)}) copy-start(f32[2,1536,48]{1,2,0:T(8,128)} %param.47) | copy-start | bytes 1769476
  1.6 11.9 %copy-start.23 = (f32[16,768]{1,0:T(8,128)S(1)}, f32[16,768]{1,0:T(8,128)}, u32[]{:S(2)}) copy-start(f32[16,768]{1,0:T(8,128)} %param.53) | copy-start | bytes 147460
  1.6 12.5 %copy-start.25 = (f32[48,256]{1,0:T(8,128)S(1)}, f32[48,256]{1,0:T(8,128)}, u32[]{:S(2)}) copy-start(f32[48,256]{1,0:T(8,128)} %param.56) | copy-start | bytes 147460
  1.6 13.1 %copy-start.39 = (s32[16,16]{1,0:T(8,128)S(1)}, s32[16,16]{1,0:T(8,128)}, u32[]{:S(2)}) copy-start(s32[16,16]{1,0:T(8,128)} %param.36) | copy-start | bytes 3076
  1.6 13.1 %copy-start.45 = (s32[1,16]{1,0:T(1,128)S(1)}, s32[1,16]{1,0:T(1,128)}, u32[]{:S(2)}) copy-start(s32[1,16]{1,0:T(1,128)} %param.35) | copy-start | bytes 196
  3.7 15.5 %all-to-all-start = ((s32[16,1,8]{2,1,0:T(1,128)}), s32[16,1,8]{2,1,0:T(1,128)S(1)}, u32[]{:S(2)}, u32[]{:S(2)}) async-start(s32[16,1,8]{2,1,0:T(1,128)} %copy.92), calls=%async_computation | async-start | bytes 16384 | tf_op jit(solution)/shard_map/all_to_all | solution.py:1656
  12.7 24.1 %copy-start.5 = (f32[2,6,48,384]{3,2,1,0:T(8,128)S(1)}, f32[2,6,48,384]{3,2,1,0:T(8,128)}, u32[]{:S(2)}) copy-start(f32[2,6,48,384]{3,2,1,0:T(8,128)} %param.38) | copy-start | bytes 2654212
  14.7 23.0 %copy-start.8 = (f32[2,48,1536]{2,1,0:T(8,128)S(1)}, f32[2,48,1536]{2,1,0:T(8,128)}, u32[]{:S(2)}) copy-start(f32[2,48,1536]{2,1,0:T(8,128)} %param.44) | copy-start | bytes 1769476
  14.7 23.7 %copy-start.36 = (f32[2,4,48]{2,1,0:T(4,128)S(1)}, f32[2,4,48]{2,1,0:T(4,128)}, u32[]{:S(2)}) copy-start(f32[2,4,48]{2,1,0:T(4,128)} %param.50) | copy-start | bytes 4612
  17.2 243.5 %copy-start.3 = (bf16[3968,256]{1,0:T(8,128)(2,1)}, bf16[3968,256]{1,0:T(8,128)(2,1)S(1)}, u32[]{:S(2)}) copy-start(bf16[3968,256]{1,0:T(8,128)(2,1)S(1)} %convert_element_type.79) | copy-start | bytes 6094852
  19.6 228.8 %copy-start.34 = (pred[16,8]{1,0:T(8,128)(4,1)}, pred[16,8]{1,0:T(8,128)(4,1)S(1)}, u32[]{:S(2)}) copy-start(pred[16,8]{1,0:T(8,128)(4,1)S(1)} %copy.94) | copy-start | bytes 388
  22.7 12.5 %all-to-all-start.1 = ((bf16[16,8,256]{2,1,0:T(8,128)(2,1)}), bf16[16,8,256]{2,1,0:T(8,128)(2,1)}, u32[]{:S(2)}, u32[]{:S(2)}) async-start(bf16[16,8,256]{2,1,0:T(8,128)(2,1)} %bitcast_select_fusion.1), calls=%async_computation.1 | async-start | bytes 131072 | tf_op jit(solution)/shard_map/all_to_all | solution.py:1662
  36.9 3.5 collective-permute-start
  36.9 209.9 %copy-start.42 = (f32[128]{0:T(128)}, f32[128]{0:T(128)S(1)}, u32[]{:S(2)}) copy-start(f32[128]{0:T(128)S(1)} %convert_subtract_fusion) | copy-start | bytes 1540
  280.8 13.8 %copy-start.13 = (bf16[16,16,256]{2,1,0:T(8,128)(2,1)S(1)}, bf16[16,16,256]{2,1,0:T(8,128)(2,1)}, u32[]{:S(2)}) copy-start(bf16[16,16,256]{2,1,0:T(8,128)(2,1)} %shard_map.495) | copy-start | bytes 393220
  294.5 4.4 collective-permute-start.1
  301.4 234.5 %copy-start.43 = (f32[128]{0:T(128)S(1)}, f32[128]{0:T(128)}, u32[]{:S(2)}) copy-start(f32[128]{0:T(128)} %copy-done.42) | copy-start | bytes 1540
  301.4 236.3 %copy-start.38 = (pred[16,8]{1,0:T(8,128)(4,1)S(1)}, pred[16,8]{1,0:T(8,128)(4,1)}, u32[]{:S(2)}) copy-start(pred[16,8]{1,0:T(8,128)(4,1)} %copy.99) | copy-start | bytes 388
  527.8 23.3 %copy-start.29 = (f32[48,768]{1,0:T(8,128)S(1)}, f32[48,768]{1,0:T(8,128)}, u32[]{:S(2)}) copy-start(f32[48,768]{1,0:T(8,128)} %get-tuple-element.128) | copy-start | bytes 442372
  527.8 24.3 %copy-start.24 = (f32[16,768]{1,0:T(8,128)S(1)}, f32[16,768]{1,0:T(8,128)}, u32[]{:S(2)}) copy-start(f32[16,768]{1,0:T(8,128)} %param.53) | copy-start | bytes 147460
  527.8 24.2 %copy-start.33 = (f32[16,768]{1,0:T(8,128)S(1)}, f32[16,768]{1,0:T(8,128)}, u32[]{:S(2)}) copy-start(f32[16,768]{1,0:T(8,128)} %param.55) | copy-start | bytes 147460
  527.8 25.9 %copy-start.26 = (f32[48,256]{1,0:T(8,128)S(1)}, f32[48,256]{1,0:T(8,128)}, u32[]{:S(2)}) copy-start(f32[48,256]{1,0:T(8,128)} %param.56) | copy-start | bytes 147460
  527.9 27.4 %copy-start.6 = (f32[2,6,48,384]{3,2,1,0:T(8,128)S(1)}, f32[2,6,48,384]{3,2,1,0:T(8,128)}, u32[]{:S(2)}) copy-start(f32[2,6,48,384]{3,2,1,0:T(8,128)} %param.38) | copy-start | bytes 2654212
  527.9 27.4 %copy-start.14 = (f32[2,6,48,384]{3,2,1,0:T(8,128)S(1)}, f32[2,6,48,384]{3,2,1,0:T(8,128)}, u32[]{:S(2)}) copy-start(f32[2,6,48,384]{3,2,1,0:T(8,128)} %param.40) | copy-start | bytes 2654212
  527.9 27.4 %copy-start.15 = (f32[2,6,48,384]{3,2,1,0:T(8,128)S(1)}, f32[2,6,48,384]{3,2,1,0:T(8,128)}, u32[]{:S(2)}) copy-start(f32[2,6,48,384]{3,2,1,0:T(8,128)} %param.39) | copy-start | bytes 2654212
  538.5 24.3 %all-to-all-start.2 = ((bf16[16,8,256]{2,1,0:T(8,128)(2,1)}), bf16[16,8,256]{2,1,0:T(8,128)(2,1)S(1)}, u32[]{:S(2)}, u32[]{:S(2)}) async-start(bf16[16,8,256]{2,1,0:T(8,128)(2,1)} %fusion.8), calls=%async_computation.2 | async-start | bytes 131072 | tf_op jit(solution)/shard_map/all_to_all | solution.py:1812
  549.9 8.3 %copy-start.18 = (f32[2,384,48]{1,2,0:T(8,128)S(1)}, f32[2,384,48]{1,2,0:T(8,128)}, u32[]{:S(2)}) copy-start(f32[2,384,48]{1,2,0:T(8,128)} %param.41) | copy-start | bytes 442372
  550.0 8.3 %copy-start.27 = (f32[2,384,48]{1,2,0:T(8,128)S(1)}, f32[2,384,48]{1,2,0:T(8,128)}, u32[]{:S(2)}) copy-start(f32[2,384,48]{1,2,0:T(8,128)} %param.43) | copy-start | bytes 442372
  550.0 8.3 %copy-start.28 = (f32[2,384,48]{1,2,0:T(8,128)S(1)}, f32[2,384,48]{1,2,0:T(8,128)}, u32[]{:S(2)}) copy-start(f32[2,384,48]{1,2,0:T(8,128)} %param.42) | copy-start | bytes 442372
  568.3 11.2 %copy-start.7 = (f32[896,768]{1,0:T(8,128)S(1)}, f32[896,768]{1,0:T(8,128)}, u32[]{:S(2)}) copy-start(f32[896,768]{1,0:T(8,128)} %get-tuple-element.201) | copy-start | bytes 8257540
  568.3 12.7 %copy-start.1 = (s32[128]{0:T(128)S(1)}, s32[128]{0:T(128)}, u32[]{:S(2)}) copy-start(s32[128]{0:T(128)} %param.33) | copy-start | bytes 1540
  (20 other events, 80.8 us)

commit v4 on v3

--- a/solution.py
+++ b/solution.py
@@ -791,22 +791,53 @@
         del refs[:count]
         return part
 
-    words, base, rows_in = take(3)
+    words, base, requests, place_mat, table = take(5)
     shards = take(len(needs["kinds"]))
     kept = take(len(needs["kinds"]))
     saved = [dict(zip(SAVED, take(len(SAVED)))) for _ in range(LAYERS)]
-    ents_out, gains_out = take(2)
+    ents_out, gains_out, rows_in, got_out = take(4)
     wholes = take(len(needs["kinds"]))
     act = dict(zip(SAVED, take(len(SAVED))))
     x, h1, gains, mine, theirs = take(5)
     gather_sems = take(4)
     pair_sems = take(2)
     (save_sem,) = take(1)
+    got, replies, answers, look_mine, look_theirs = take(5)
+    look_send, look_recv, look_pair = take(3)
 
     gather = Gather(dims, chunks, shards, wholes, kept, gather_sems)
     pair = Pair(mine, theirs, pair_sems)
-    greet(gather.targets() + [pair.other])
+    count = dims[0] * dims[1] * dims[2]
+    greet_line(count, [pair.other])
+    asking = Fan(
+        count, (look_send.at[0], look_recv.at[0]), lambda me, to: (requests.at[to], got.at[me])
+    )
+    asking.start()
     gather.begin()
+    here = lax.axis_index("dp")
+    got[here] = requests[here]
+    asking.wait()
+    wanted = flat(got)
+    got_out[...] = wanted
+
+    def look(j, found):
+        lane = lax.broadcasted_iota(jnp.int32, wanted.shape, 1) + j * 128
+        hot = jnp.where(wanted == lane, 1.0, 0.0).astype(jnp.bfloat16)
+        return found + mm(hot, table[pl.ds(pl.multiple_of(j * 128, 128), 128), :])
+
+    found = jnp.zeros((wanted.shape[0], table.shape[1]), jnp.float32)
+    found = lax.fori_loop(0, table.shape[0] // 128, look, found)
+    replies[...] = found.reshape(replies.shape)
+    answering = Fan(
+        count, (look_send.at[1], look_recv.at[1]), lambda me, to: (replies.at[to], answers.at[me])
+    )
+    answering.start()
+    answers[here] = replies[here]
+    gather.tick()
+    gather.tick()
+    answering.wait()
+    look_mine[...] = mm(place_mat[...], flat(answers).astype(jnp.bfloat16)).astype(jnp.bfloat16)
+    swap = send(look_mine, look_theirs, look_pair.at[0], look_pair.at[1], pair.other)
     attn, outs, ups, downs, proj, _, norms = wholes
     saving = {}
 
@@ -823,7 +854,6 @@
     x[:WORDS] = words[...].astype(jnp.float32)
     gather.need(needs["norms"])
     width = D // (dims[0] * dims[1] * dims[2])
-    count = dims[0] * dims[1] * dims[2]
     gains[...] = jnp.zeros_like(gains)
     for d in range(count):
         z, rest = d // (dims[1] * dims[2]), d % (dims[1] * dims[2])
@@ -833,6 +863,9 @@
         hot = jnp.where((pick == lane) & inside, 1.0, 0.0).astype(jnp.bfloat16)
         gains[...] += mm(norms[0, z, rest // dims[2], rest % dims[2]], hot)
     gather.need(needs["proj"])
+    swap.wait()
+    both = look_mine[...].astype(jnp.float32) + look_theirs[...].astype(jnp.float32)
+    rows_in[...] = both.astype(jnp.bfloat16)
     x[WORDS:] = base[...].astype(jnp.float32) + mm(rows_in[...], flat(proj, 0))
 
     for layer in range(LAYERS):
@@ -949,11 +982,12 @@
     return chunks, needs
 
 
-def run_forward(dims, words, base, entity_rows, shards, collective_id):
+def run_forward(dims, words, base, requests, place_mat, table_low, shards, collective_id):
     half, hidden = shards[0].shape[-1], shards[2].shape[-1]
     chunks, needs = gather_plan(hidden)
     shapes = saved_shapes(half, hidden)
     low, full = jnp.bfloat16, jnp.float32
+    width, slots = table_low.shape[1], requests.shape[0] * requests.shape[1]
     wholes = [(s.shape[0], *dims, *s.shape[1:]) for s in shards]
     copies = dims[0] + 2 * max(dims[1:])
     saved_out = [jax.ShapeDtypeStruct(*shapes[name]) for _ in range(LAYERS) for name in SAVED]
@@ -961,9 +995,14 @@
         functools.partial(forward_body, dims, chunks, needs),
         out_shape=[jax.ShapeDtypeStruct(shape, low) for shape in wholes]
         + saved_out
-        + [jax.ShapeDtypeStruct((ENT_LEN, D), full), jax.ShapeDtypeStruct((16, D), full)],
-        in_specs=[VMEM] * 3 + [ANY] * len(shards),
-        out_specs=[ANY] * (len(wholes) + len(saved_out)) + [VMEM] * 2,
+        + [
+            jax.ShapeDtypeStruct((ENT_LEN, D), full),
+            jax.ShapeDtypeStruct((16, D), full),
+            jax.ShapeDtypeStruct((ENT_LEN, width), low),
+            jax.ShapeDtypeStruct((slots, 128), jnp.int32),
+        ],
+        in_specs=[VMEM] * 5 + [ANY] * len(shards),
+        out_specs=[ANY] * (len(wholes) + len(saved_out)) + [VMEM] * 4,
         scratch_shapes=[pltpu.VMEM(shape, low) for shape in wholes]
         + [pltpu.VMEM(*shapes[name]) for name in SAVED]
         + [
@@ -979,17 +1018,356 @@
             pltpu.SemaphoreType.DMA((2 * LAYERS, BLOCKS)),
             pltpu.SemaphoreType.DMA((2 * LAYERS, BLOCKS)),
             pltpu.SemaphoreType.DMA((LAYERS * len(SAVED),)),
+            pltpu.VMEM(requests.shape, jnp.int32),
+            pltpu.VMEM((*requests.shape[:2], width), full),
+            pltpu.VMEM((*requests.shape[:2], width), full),
+            pltpu.VMEM((ENT_LEN, width), low),
+            pltpu.VMEM((ENT_LEN, width), low),
+            pltpu.SemaphoreType.DMA((2, requests.shape[0])),
+            pltpu.SemaphoreType.DMA((2, requests.shape[0])),
+            pltpu.SemaphoreType.DMA((2,)),
         ],
         compiler_params=pltpu.CompilerParams(
             collective_id=collective_id, has_side_effects=True, vmem_limit_bytes=VMEM_BYTES
         ),
-    )(words, base, entity_rows, *shards)
+    )(words, base, requests, place_mat, table_low, *shards)
     kept = result[: len(wholes)]
     saved = [
         dict(zip(SAVED, result[len(wholes) + layer * len(SAVED) :][: len(SAVED)]))
         for layer in range(LAYERS)
     ]
-    return kept, saved, *result[-2:]
+    return kept, saved, *result[-4:]
+
+
+class Fan:
+    def __init__(self, count, sems, copy_args):
+        self.count, self.sems, self.copy_args = count, sems, copy_args
+        self.index = lax.axis_index("dp")
+
+    def copy(self, step):
+        other = lax.rem(self.index + step, self.count)
+        src, dst = self.copy_args(self.index, other)
+        send_sem, recv_sem = self.sems
+        return pltpu.make_async_remote_copy(
+            src_ref=src,
+            dst_ref=dst,
+            send_sem=send_sem.at[step],
+            recv_sem=recv_sem.at[step],
+            device_id=(other, lax.axis_index("mp")),
+            device_id_type=MESH,
+        )
+
+    def start(self):
+        def go(step, carry):
+            self.copy(step).start()
+            return carry
+
+        lax.fori_loop(1, self.count, go, 0)
+
+    def wait(self):
+        def done(step, carry):
+            self.copy(step).wait()
+            return carry
+
+        lax.fori_loop(1, self.count, done, 0)
+
+
+def greet_line(count, extra):
+    barrier = pltpu.get_barrier_semaphore()
+    index, core = lax.axis_index("dp"), lax.axis_index("mp")
+
+    def hello(step, carry):
+        other = lax.rem(index + step, count)
+        pl.semaphore_signal(barrier, inc=1, device_id=(other, core), device_id_type=MESH)
+        return carry
+
+    lax.fori_loop(1, count, hello, 0)
+    for target in extra:
+        pl.semaphore_signal(barrier, inc=1, device_id=target, device_id_type=MESH)
+    pl.semaphore_wait(barrier, count - 1 + len(extra))
+
+
+TABLE_CUTS = 8
+
+
+def head_body(count, *refs):
+    ents, hits, head, table, local_targets = refs[:5]
+    losses, grad_logits, states, grad_head, grad_ents = refs[5:10]
+    logits, own_states, all_states, stat_mine, stat_theirs, stat_both, stat_all = refs[10:17]
+    grad_part, grad_all, share_mine, share_theirs = refs[17:21]
+    send_sem, recv_sem, pair_send, pair_recv = refs[21:]
+    index = lax.axis_index("dp")
+    other = (index, 1 - lax.axis_index("mp"))
+    greet_line(count, [other])
+    total_rows = count * MASK_ENT
+    span = table.shape[0] // TABLE_CUTS
+
+    masked = mm(hits[...], ents[...].astype(jnp.bfloat16)).astype(jnp.bfloat16)
+    head_low = flat(head)
+    value, slope = gelu_parts(mm(masked, head_low))
+    own_states[...] = value.astype(jnp.bfloat16)
+    fan = Fan(count, (send_sem.at[0], recv_sem.at[0]), lambda me, to: (own_states, all_states.at[me]))
+    fan.start()
+    all_states[index] = own_states[...]
+    fan.wait()
+    states[...] = flat(all_states)
+    target = local_targets[0:1, :]
+
+    def hit_of(c):
+        row = lax.broadcasted_iota(jnp.int32, (span, total_rows), 0) + c * span
+        return row == target
+
+    def rows_of(c):
+        return pl.ds(pl.multiple_of(c * span, 16), span)
+
+    def score(c, carry):
+        peak, picked = carry
+        part = mm_rt(table[rows_of(c), :], states[...])
+        logits[rows_of(c), :] = part
+        peak = jnp.maximum(peak, jnp.max(part, axis=0, keepdims=True))
+        picked += jnp.sum(jnp.where(hit_of(c), part, 0.0), axis=0, keepdims=True)
+        return peak, picked
+
+    empty = jnp.zeros((1, total_rows), jnp.float32)
+    peak, picked = lax.fori_loop(0, TABLE_CUTS, score, (empty - 3e38, empty))
+
+    def weigh(c, weight):
+        return weight + jnp.sum(jnp.exp(logits[rows_of(c), :] - peak), axis=0, keepdims=True)
+
+    weight = lax.fori_loop(0, TABLE_CUTS, weigh, empty)
+    stat_mine[0:1, :] = peak
+    stat_mine[1:2, :] = weight
+    stat_mine[2:3, :] = picked
+    swap = send(stat_mine, stat_theirs, pair_send.at[0], pair_recv.at[0], other)
+    swap.wait()
+    peak_both = jnp.maximum(stat_mine[0:1, :], stat_theirs[0:1, :])
+    stat_both[0:1, :] = peak_both
+    stat_both[1:2, :] = stat_mine[1:2, :] * jnp.exp(stat_mine[0:1, :] - peak_both) + stat_theirs[
+        1:2, :
+    ] * jnp.exp(stat_theirs[0:1, :] - peak_both)
+    stat_both[2:3, :] = stat_mine[2:3, :] + stat_theirs[2:3, :]
+    fan = Fan(count, (send_sem.at[1], recv_sem.at[1]), lambda me, to: (stat_both, stat_all.at[me]))
+    fan.start()
+    stat_all[index] = stat_both[...]
+    fan.wait()
+    peak_all = stat_all[0, 0:1, :]
+    for d in range(1, count):
+        peak_all = jnp.maximum(peak_all, stat_all[d, 0:1, :])
+    weight_all = picked_all = empty
+    for d in range(count):
+        weight_all += stat_all[d, 1:2, :] * jnp.exp(stat_all[d, 0:1, :] - peak_all)
+        picked_all += stat_all[d, 2:3, :]
+    log_norm = peak_all + jnp.log(weight_all)
+    losses[...] = jnp.broadcast_to(log_norm - picked_all, losses.shape)
+    grad_part[...] = jnp.zeros_like(grad_part)
+
+    def grads(c, carry):
+        prob = jnp.exp(logits[rows_of(c), :] - log_norm)
+        part = (prob - jnp.where(hit_of(c), 1.0, 0.0)) * (1.0 / total_rows)
+        low = part.astype(jnp.bfloat16)
+        grad_logits[rows_of(c), :] = low
+        grad_part[...] += mm_lt(low, table[rows_of(c), :]).reshape(grad_part.shape)
+        return carry
+
+    lax.fori_loop(0, TABLE_CUTS, grads, 0)
+    fan = Fan(
+        count, (send_sem.at[2], recv_sem.at[2]), lambda me, to: (grad_part.at[to], grad_all.at[me])
+    )
+    fan.start()
+    grad_all[index] = grad_part[index]
+    fan.wait()
+    share_mine[...] = jnp.sum(grad_all[...], axis=0)
+    swap = send(share_mine, share_theirs, pair_send.at[1], pair_recv.at[1], other)
+    swap.wait()
+    grad_pre = ((share_mine[...] + share_theirs[...]) * slope).astype(jnp.bfloat16)
+    grad_head[...] = mm_lt(masked, grad_pre).astype(jnp.bfloat16).reshape(grad_head.shape)
+    grad_masked = mm_rt(grad_pre, head_low)
+    grad_ents[...] = lax.dot_general(
+        hits[...].astype(jnp.float32),
+        grad_masked,
+        (((0,), (0,)), ((), ())),
+        precision=lax.Precision.HIGHEST,
+        preferred_element_type=jnp.float32,
+    )
+
+
+def run_head(dims, ents, hits, head, table_low, local_targets, collective_id):
+    count = dims[0] * dims[1] * dims[2]
+    width = table_low.shape[1]
+    rows = count * MASK_ENT
+    low, full = jnp.bfloat16, jnp.float32
+    return pl.pallas_call(
+        functools.partial(head_body, count),
+        out_shape=[
+            jax.ShapeDtypeStruct((8, rows), full),
+            jax.ShapeDtypeStruct((table_low.shape[0], rows), low),
+            jax.ShapeDtypeStruct((rows, width), low),
+            jax.ShapeDtypeStruct(head.shape, low),
+            jax.ShapeDtypeStruct((ENT_LEN, D), full),
+        ],
+        in_specs=[VMEM] * 5,
+        out_specs=[VMEM] * 5,
+        scratch_shapes=[
+            pltpu.VMEM((table_low.shape[0], rows), full),
+            pltpu.VMEM((MASK_ENT, width), low),
+            pltpu.VMEM((count, MASK_ENT, width), low),
+            pltpu.VMEM((8, rows), full),
+            pltpu.VMEM((8, rows), full),
+            pltpu.VMEM((8, rows), full),
+            pltpu.VMEM((count, 8, rows), full),
+            pltpu.VMEM((count, MASK_ENT, width), full),
+            pltpu.VMEM((count, MASK_ENT, width), full),
+            pltpu.VMEM((MASK_ENT, width), full),
+            pltpu.VMEM((MASK_ENT, width), full),
+            pltpu.SemaphoreType.DMA((3, count)),
+            pltpu.SemaphoreType.DMA((3, count)),
+            pltpu.SemaphoreType.DMA((2,)),
+            pltpu.SemaphoreType.DMA((2,)),
+        ],
+        compiler_params=pltpu.CompilerParams(
+            collective_id=collective_id, has_side_effects=True, vmem_limit_bytes=VMEM_BYTES
+        ),
+    )(ents, hits, head, table_low, local_targets)
+
+
+def update_body(names, width, *refs):
+    refs = list(refs)
+
+    def take(count):
+        part = refs[:count]
+        del refs[:count]
+        return part
+
+    kinds = len(kind_rates)
+    state_in = [take(3) for _ in range(kinds)]
+    totals_in = take(len(names))
+    incoming, requests, grad_logits, states = take(4)
+    state_out = [take(3) for _ in range(kinds)]
+    held = [take(3) for _ in range(kinds)]
+    totals_held = take(len(names))
+    in_sem, total_sem, out_sem = take(3)
+    table = kinds - 1
+    height = held[table][0].shape[0] // TABLE_CUTS
+
+    def piece(ref, c):
+        return ref if c is None else ref.at[pl.ds(c * height, height)]
+
+    def copies(kind, c, inward):
+        base = 3 * (kind + (0 if c is None else c))
+        pairs = []
+        for i in range(3):
+            if inward:
+                src, dst, sem = state_in[kind][i], held[kind][i], in_sem.at[base + i]
+            else:
+                src, dst, sem = held[kind][i], state_out[kind][i], out_sem.at[base + i]
+            pairs.append(pltpu.make_async_copy(piece(src, c), piece(dst, c), sem))
+        return pairs
+
+    leaving = []
+    total_copies = [
+        pltpu.make_async_copy(src, dst, total_sem.at[i])
+        for i, (src, dst) in enumerate(zip(totals_in, totals_held))
+    ]
+    for c in range(2):
+        for copy in copies(table, c, True):
+            copy.start()
+    for copy in total_copies:
+        copy.start()
+    for kind in range(table):
+        for copy in copies(kind, None, True):
+            copy.start()
+    for c in range(2, TABLE_CUTS):
+        for copy in copies(table, c, True):
+            copy.start()
+    total_of = dict(zip(names, totals_held))
+
+    def update(kind, at, gradient):
+        master, first, second = held[kind]
+        first_new = beta_first * first[at] + (1.0 - beta_first) * gradient
+        second_new = beta_second * second[at] + (1.0 - beta_second) * gradient * gradient
+        first_hat = first_new * (1.0 / (1.0 - beta_first**STEP))
+        second_hat = second_new * (1.0 / (1.0 - beta_second**STEP))
+        value = master[at]
+        value -= kind_rates[kind] * (
+            first_hat / (jnp.sqrt(second_hat) + adam_eps) + weight_decay * value
+        )
+        master[at], first[at], second[at] = value, first_new, second_new
+
+    def finish(kind, c=None):
+        for copy in copies(kind, c, False):
+            copy.start()
+            leaving.append(copy)
+
+    def table_part(c):
+        for copy in copies(table, c, True):
+            copy.wait()
+        rows = slice(c * height, (c + 1) * height)
+        gradient = mm(grad_logits[rows, :], states[...])
+        row = lax.broadcasted_iota(jnp.int32, (height, requests.shape[1]), 0) + c * height
+        hot = jnp.where(row == requests[0:1, :], 1.0, 0.0).astype(jnp.bfloat16)
+        gradient += mm(hot, incoming[...].astype(jnp.bfloat16))
+        update(table, (rows, slice(None)), gradient)
+        finish(table, c)
+
+    table_part(0)
+    table_part(1)
+    for copy in total_copies:
+        copy.wait()
+    for kind in range(table):
+        for copy in copies(kind, None, True):
+            copy.wait()
+        for layer in range(LAYERS):
+            if kind == 0:
+                blocks = []
+                for name in ("words", "ents"):
+                    total = total_of[layer, name]
+                    half = total.shape[1] // 2
+                    blocks += [total[:, :half], total[:, half:]]
+                blocks += [total_of[layer, "key"][...], total_of[layer, "value"][...]]
+                for mat, block in enumerate(blocks):
+                    update(kind, (layer, mat), block)
+            elif kind == 1:
+                update(kind, (layer,), total_of[layer, "out"][...])
+            elif kind in (2, 3):
+                for i in range(2):
+                    total = total_of[layer, ("up%d", "down%d")[kind - 2] % i]
+                    half = total.shape[1]
+                    cols = slice(i * half, (i + 1) * half)
+                    update(kind, (layer, slice(None), cols), total[...])
+            elif kind == 4:
+                update(kind, (layer,), total_of["norms"][4 * layer : 4 * layer + 4, :width])
+        if kind == 5:
+            update(kind, (slice(None),), total_of["proj"][...])
+        if kind == 6:
+            update(kind, (slice(None),), total_of["head"][...])
+        finish(kind)
+    for c in range(2, TABLE_CUTS):
+        table_part(c)
+    for copy in leaving:
+        copy.wait()
+
+
+def run_update(states_of, totals, incoming, requests, grad_logits, states):
+    names = list(totals)
+    full = jnp.float32
+    flat_states = [array for group in states_of for array in group]
+    width = states_of[4][0].shape[-1]
+    kinds = len(kind_rates)
+    result = pl.pallas_call(
+        functools.partial(update_body, names, width),
+        out_shape=[jax.ShapeDtypeStruct(a.shape, full) for a in flat_states],
+        in_specs=[ANY] * (len(flat_states) + len(names)) + [VMEM] * 4,
+        out_specs=[ANY] * len(flat_states),
+        scratch_shapes=[pltpu.VMEM(a.shape, full) for a in flat_states]
+        + [pltpu.VMEM(totals[name].shape, full) for name in names]
+        + [
+            pltpu.SemaphoreType.DMA((3 * (kinds + TABLE_CUTS),)),
+            pltpu.SemaphoreType.DMA((len(names),)),
+            pltpu.SemaphoreType.DMA((3 * (kinds + TABLE_CUTS),)),
+        ],
+        compiler_params=pltpu.CompilerParams(vmem_limit_bytes=VMEM_BYTES),
+    )(*flat_states, *totals.values(), incoming, requests, grad_logits, states)
+    return [result[3 * i : 3 * i + 3] for i in range(kinds)]
 
 
 def norm_back(grad, hat, scale, gain_row):
@@ -1130,10 +1508,10 @@
         del refs[:count]
         return part
 
-    cotangent, grad_ents, grad_head, gains, entity_rows = take(5)
+    cotangent, grad_ents, grad_head, gains, entity_rows, place_mat = take(6)
     w_attn, w_out, w_up, w_down, w_proj = take(5)
     saved = [dict(zip(SAVED, take(len(SAVED)))) for _ in range(LAYERS)]
-    word_grads, row_grads = take(2)
+    word_grads, incoming = take(2)
     totals = take(len(names))
     slots = list(UNITS + EXTRA)
     buffers = [take(4) for _ in slots]
@@ -1145,6 +1523,7 @@
     (free_sem,) = take(1)
     pair_sems = take(2)
     (load_sem,) = take(1)
+    out_rows, in_rows, row_send, row_recv = take(4)
 
     units = []
     for name in names:
@@ -1153,7 +1532,8 @@
         units.append((slots.index(kind), UNIT_FIRST[kind], turn))
     sums = Sums(dims, units, buffers, totals, sum_sems, free_sem)
     pair = Pair(mine, theirs, pair_sems)
-    greet([target for group in sums.peers for _, target in group] + [pair.other])
+    count = dims[0] * dims[1] * dims[2]
+    greet_line(count, [pair.other])
     part_of = {slot: buffers[i][0] for i, slot in enumerate(slots)}
     loads, counter = {}, [0]
 
@@ -1395,10 +1775,15 @@
     leaving = pltpu.make_async_copy(gacc.at[pl.ds(0, WORDS)], word_grads, load_sem.at[counter[0]])
     leaving.start()
     grad_entity = gacc[WORDS:].astype(jnp.bfloat16)
+    row_grads = mm_rt(grad_entity, flat(mat_proj)).astype(jnp.bfloat16)
+    out_rows[...] = mm_lt(place_mat[...], row_grads).reshape(out_rows.shape)
+    returning = Fan(count, (row_send, row_recv), lambda me, to: (out_rows.at[to], in_rows.at[me]))
+    returning.start()
+    here = lax.axis_index("dp")
+    in_rows[here] = out_rows[here]
     proj_part = part_of["proj"]
     proj_part[...] = mm_lt(entity_rows[...], grad_entity).astype(jnp.bfloat16).reshape(proj_part.shape)
     sums.start(0, names.index("proj"))
-    count = dims[0] * dims[1] * dims[2]
     width = D // count
     norm_low = gnorm[...].astype(jnp.bfloat16)
     for d in range(count):
@@ -1409,12 +1794,15 @@
         block = mm_rt(norm_low, hot).astype(jnp.bfloat16)
         part_of["norms"][z, rest // dims[2], rest % dims[2]] = block
     sums.start(0, names.index("norms"))
-    row_grads[...] = mm_rt(grad_entity, flat(mat_proj))
     sums.close()
+    returning.wait()
+    incoming[...] = flat(in_rows)
     leaving.wait()
 
 
-def run_backward(dims, cotangent, grad_ents, grad_head, gains, entity_rows, kept, saved, collective_id):
+def run_backward(
+    dims, cotangent, grad_ents, grad_head, gains, entity_rows, place_mat, kept, saved, collective_id
+):
     names = sum_plan()
     half, hidden = kept[0].shape[-1], kept[2].shape[-1]
     low, full = jnp.bfloat16, jnp.float32
@@ -1437,16 +1825,18 @@
         ]
     copies = dims[0] + 2 * max(dims[1:])
     kinds = [name if isinstance(name, str) else name[1] for name in names]
-    inputs = [cotangent, grad_ents, grad_head, gains, entity_rows, *kept[:5]]
+    count = dims[0] * dims[1] * dims[2]
+    width, slots = kept[5].shape[-1], place_mat.shape[1]
+    inputs = [cotangent, grad_ents, grad_head, gains, entity_rows, place_mat, *kept[:5]]
     inputs += [saved[layer][name] for layer in range(LAYERS) for name in SAVED]
     result = pl.pallas_call(
         functools.partial(backward_body, dims, names, half, hidden),
         out_shape=[
             jax.ShapeDtypeStruct((WORDS, D), full),
-            jax.ShapeDtypeStruct((ENT_LEN, kept[5].shape[-1]), full),
+            jax.ShapeDtypeStruct((slots, width), full),
         ]
         + [jax.ShapeDtypeStruct(blocks[kind], full) for kind in kinds],
-        in_specs=[VMEM] * 5 + [ANY] * (len(inputs) - 5),
+        in_specs=[VMEM] * 6 + [ANY] * (len(inputs) - 6),
         out_specs=[ANY] + [VMEM] * (1 + len(names)),
         scratch_shapes=scratch
         + [
@@ -1476,6 +1866,10 @@
             pltpu.SemaphoreType.DMA((2 * LAYERS, BLOCKS)),
             pltpu.SemaphoreType.DMA((2 * LAYERS, BLOCKS)),
             pltpu.SemaphoreType.DMA((64,)),
+            pltpu.VMEM((count, slots // count, width), full),
+            pltpu.VMEM((count, slots // count, width), full),
+            pltpu.SemaphoreType.DMA((count,)),
+            pltpu.SemaphoreType.DMA((count,)),
         ],
         compiler_params=pltpu.CompilerParams(
             collective_id=collective_id, has_side_effects=True, vmem_limit_bytes=VMEM_BYTES
@@ -1585,31 +1979,7 @@
     )
 
 
-def fused_sums(totals, width):
-    layers = range(LAYERS)
-
-    def halves(name):
-        parts = [totals[layer, name] for layer in layers]
-        cut = parts[0].shape[1] // 2
-        return [[part[:, :cut], part[:, cut:]] for part in parts]
-
-    words, ents = halves("words"), halves("ents")
-    attn = jnp.stack(
-        [
-            jnp.stack(words[layer] + ents[layer] + [totals[layer, "key"], totals[layer, "value"]])
-            for layer in layers
-        ]
-    )
-    ups = jnp.stack([jnp.concatenate([totals[i, "up0"], totals[i, "up1"]], axis=1) for i in layers])
-    downs = jnp.stack(
-        [jnp.concatenate([totals[i, "down0"], totals[i, "down1"]], axis=1).T for i in layers]
-    )
-    outs = jnp.stack([totals[i, "out"].T for i in layers])
-    norms = totals["norms"][: LAYERS * 4, :width].reshape(LAYERS, 4, width)
-    return attn, outs, ups, downs, norms, totals["proj"], totals["head"]
-
-
-def on_device(
+def apart_device(
     word_inputs,
     entity_base,
     entity_ids,
@@ -1646,7 +2016,11 @@
     shards, heights = weight_shards(
         attention_in, attention_out, feed_up, feed_down, norm_params, entity_proj, head_proj
     )
-    fused = heights[0] % 16 == 0 and heights[4] % 16 == 0
+    wholes = gather_apart(dims, shards)
+    attn_low, out_low, up_low, down_low, norm_low, proj_low, head_low = unpack_weights(
+        wholes, heights, norm_params.shape[-1]
+    )
+    gain_all = norm_low.astype(jnp.float32)
     slot_total = entity_ids.shape[0]
     shard_rows = entity_table.shape[0]
     bucket_rows = buckets.reshape(buckets.shape[2], buckets.shape[3])
@@ -1674,43 +2048,30 @@
         jnp.arange(slot_total, dtype=jnp.int32)[:, None] == masked_slots[None, :], axis=1
     ).astype(jnp.float32)
     entity_rows = (paired * keep_weight[:, None]).astype(jnp.bfloat16)
-    if fused:
-        wholes, saved_layers, ents, gain_rows = run_forward(
-            dims, word_inputs, entity_base, entity_rows, shards, 6
+    entity_inputs = entity_base.astype(jnp.float32) + jnp.dot(
+        entity_rows, proj_low, preferred_element_type=jnp.float32
+    )
+    hidden = jnp.concatenate(
+        [
+            word_inputs.astype(jnp.float32).reshape(SEQ_DEV, WORDS, D),
+            entity_inputs.reshape(SEQ_DEV, ENT_LEN, D),
+        ],
+        axis=1,
+    )
+    saved_layers = []
+    for layer_index in range(LAYERS):
+        hidden, saved_acts = layer_forward(
+            hidden,
+            attn_low[layer_index],
+            out_low[layer_index],
+            up_low[layer_index],
+            down_low[layer_index],
+            gain_all[layer_index],
         )
-    else:
-        wholes = gather_apart(dims, shards)
-        attn_low, out_low, up_low, down_low, norm_low, proj_low, head_low = unpack_weights(
-            wholes, heights, norm_params.shape[-1]
-        )
-        gain_all = norm_low.astype(jnp.float32)
-        entity_inputs = entity_base.astype(jnp.float32) + jnp.dot(
-            entity_rows, proj_low, preferred_element_type=jnp.float32
-        )
-        hidden = jnp.concatenate(
-            [
-                word_inputs.astype(jnp.float32).reshape(SEQ_DEV, WORDS, D),
-                entity_inputs.reshape(SEQ_DEV, ENT_LEN, D),
-            ],
-            axis=1,
-        )
-        saved_layers = []
-        for layer_index in range(LAYERS):
-            hidden, saved_acts = layer_forward(
-                hidden,
-                attn_low[layer_index],
-                out_low[layer_index],
-                up_low[layer_index],
-                down_low[layer_index],
-                gain_all[layer_index],
-            )
-            saved_layers.append(saved_acts)
-        ents = hidden[0, WORDS:]
-    if fused:
-        head_low = wholes[5].reshape(-1, wholes[5].shape[-1])
+        saved_layers.append(saved_acts)
     seq_index = jnp.arange(SEQ_DEV, dtype=jnp.int32)[:, None]
     masked_rows = WORDS + mask_positions
-    masked_low = ents[mask_positions.reshape(-1)].astype(jnp.bfloat16)
+    masked_low = hidden[seq_index, masked_rows].reshape(SEQ_DEV * MASK_ENT, D).astype(jnp.bfloat16)
     head_pre = jnp.dot(masked_low, head_low, preferred_element_type=jnp.float32)
     states_low = gelu_exact(head_pre).astype(jnp.bfloat16)
     all_states = spread(states_low, False, False, 3).reshape(-1, states_low.shape[1])
@@ -1748,73 +2109,54 @@
     grad_masked = lax.dot_general(
         grad_head_pre, head_low, (((1,), (1,)), ((), ())), preferred_element_type=jnp.float32
     )
-    if fused:
-        hits = (
-            jnp.arange(slot_total, dtype=jnp.int32)[:, None] == mask_positions.reshape(-1)[None, :]
-        ).astype(jnp.float32)
-        grad_ents = jnp.dot(hits, grad_masked, precision=lax.Precision.HIGHEST)
-        word_grads, row_grads, totals = run_backward(
-            dims,
-            word_cotangent,
-            grad_ents,
-            grad_head.astype(jnp.bfloat16).reshape(*dims, -1, grad_head.shape[-1]),
-            gain_rows,
-            entity_rows,
-            wholes,
-            saved_layers,
-            8,
+    grad_hidden = jnp.concatenate(
+        [
+            word_cotangent.astype(jnp.float32).reshape(SEQ_DEV, WORDS, D),
+            jnp.zeros((SEQ_DEV, ENT_LEN, D), jnp.float32),
+        ],
+        axis=1,
+    )
+    grad_hidden = grad_hidden.at[seq_index, masked_rows].add(
+        grad_masked.reshape(SEQ_DEV, MASK_ENT, D)
+    )
+    kept_grads = []
+    for layer_index in reversed(range(LAYERS)):
+        grad_hidden, layer_grads = layer_backward(
+            grad_hidden,
+            saved_layers[layer_index],
+            attn_low[layer_index],
+            out_low[layer_index],
+            up_low[layer_index],
+            down_low[layer_index],
+            gain_all[layer_index],
         )
-        row_gradient_block = row_grads * keep_weight[:, None]
-        reduced = fused_sums(totals, norm_params.shape[-1])
-    else:
-        grad_hidden = jnp.concatenate(
-            [
-                word_cotangent.astype(jnp.float32).reshape(SEQ_DEV, WORDS, D),
-                jnp.zeros((SEQ_DEV, ENT_LEN, D), jnp.float32),
-            ],
-            axis=1,
-        )
-        grad_hidden = grad_hidden.at[seq_index, masked_rows].add(
-            grad_masked.reshape(SEQ_DEV, MASK_ENT, D)
-        )
-        kept_grads = []
-        for layer_index in reversed(range(LAYERS)):
-            grad_hidden, layer_grads = layer_backward(
-                grad_hidden,
-                saved_layers[layer_index],
-                attn_low[layer_index],
-                out_low[layer_index],
-                up_low[layer_index],
-                down_low[layer_index],
-                gain_all[layer_index],
+        if layer_index == 0:
+            word_grads = grad_hidden[:, :WORDS].reshape(SEQ_DEV * WORDS, D)
+            grad_entity = grad_hidden[:, WORDS:].reshape(slot_total, D).astype(jnp.bfloat16)
+            grad_proj = lax.dot_general(
+                entity_rows,
+                grad_entity,
+                (((0,), (0,)), ((), ())),
+                preferred_element_type=jnp.float32,
             )
-            if layer_index == 0:
-                word_grads = grad_hidden[:, :WORDS].reshape(SEQ_DEV * WORDS, D)
-                grad_entity = grad_hidden[:, WORDS:].reshape(slot_total, D).astype(jnp.bfloat16)
-                grad_proj = lax.dot_general(
-                    entity_rows,
+            row_gradient_block = (
+                lax.dot_general(
                     grad_entity,
-                    (((0,), (0,)), ((), ())),
+                    proj_low,
+                    (((1,), (1,)), ((), ())),
                     preferred_element_type=jnp.float32,
                 )
-                row_gradient_block = (
-                    lax.dot_general(
-                        grad_entity,
-                        proj_low,
-                        (((1,), (1,)), ((), ())),
-                        preferred_element_type=jnp.float32,
-                    )
-                    * keep_weight[:, None]
-                )
-            kept_grads.insert(0, layer_grads)
-        reduced = sum_all(dims, kept_grads, grad_proj, grad_head)
-    outgoing = jnp.where(filled[:, :, None], row_gradient_block[safe_slot], 0.0)
-    incoming = lax.all_to_all(
-        outgoing.astype(jnp.bfloat16), "dp", split_axis=0, concat_axis=0, tiled=True
-    ).astype(outgoing.dtype)
-    grad_table = grad_table.at[safe_row].add(
-        jnp.where(owned_mask[:, :, None], incoming, 0.0)
-    )
+                * keep_weight[:, None]
+            )
+            outgoing = jnp.where(filled[:, :, None], row_gradient_block[safe_slot], 0.0)
+            incoming = lax.all_to_all(
+                outgoing.astype(jnp.bfloat16), "dp", split_axis=0, concat_axis=0, tiled=True
+            ).astype(outgoing.dtype)
+            grad_table = grad_table.at[safe_row].add(
+                jnp.where(owned_mask[:, :, None], incoming, 0.0)
+            )
+        kept_grads.insert(0, layer_grads)
+    reduced = sum_all(dims, kept_grads, grad_proj, grad_head)
     reduced_proj, reduced_head = reduced[5:]
     attn_new = adam_update(
         attention_in, attention_in_first, attention_in_second, reduced[0], kind_rates[0]
@@ -1864,6 +2206,112 @@
         table_new[1],
         table_new[2],
     )
+
+
+def turned(*arrays):
+    return tuple(jnp.swapaxes(array, 1, 2) for array in arrays)
+
+
+def fused_device(
+    word_inputs,
+    entity_base,
+    entity_ids,
+    buckets,
+    mask_positions,
+    targets,
+    word_cotangent,
+    attention_in,
+    attention_in_first,
+    attention_in_second,
+    attention_out,
+    attention_out_first,
+    attention_out_second,
+    feed_up,
+    feed_up_first,
+    feed_up_second,
+    feed_down,
+    feed_down_first,
+    feed_down_second,
+    norm_params,
+    norm_params_first,
+    norm_params_second,
+    entity_proj,
+    entity_proj_first,
+    entity_proj_second,
+    head_proj,
+    head_proj_first,
+    head_proj_second,
+    entity_table,
+    entity_table_first,
+    entity_table_second,
+):
+    dims = chip_grid(lax.axis_size("dp"))
+    shards, heights = weight_shards(
+        attention_in, attention_out, feed_up, feed_down, norm_params, entity_proj, head_proj
+    )
+    slot_total, shard_rows = entity_ids.shape[0], entity_table.shape[0]
+    bucket_rows = buckets.reshape(buckets.shape[2], buckets.shape[3])
+    request = jnp.where(
+        bucket_rows >= 0, entity_ids[jnp.maximum(bucket_rows, 0)] % shard_rows, -1
+    ).astype(jnp.int32)
+    requests = jnp.broadcast_to(request[:, :, None], (*request.shape, 128))
+    slots = jnp.arange(slot_total, dtype=jnp.int32)
+    marks = mask_positions.reshape(-1)[:, None] == slots[None, :]
+    keep = jnp.logical_not(jnp.any(marks, axis=0))
+    place_mat = (slots[:, None] == bucket_rows.reshape(-1)[None, :]) & keep[:, None]
+    place_mat = place_mat.astype(jnp.bfloat16)
+    hits = marks.astype(jnp.bfloat16)
+    table_low = entity_table.astype(jnp.bfloat16)
+    flat_targets = targets.reshape(-1)
+    local_targets = flat_targets - lax.axis_index(("dp", "mp")) * shard_rows
+    local_targets = jnp.broadcast_to(local_targets[None, :], (8, flat_targets.shape[0]))
+    wholes, saved_layers, ents, gain_rows, entity_rows, got = run_forward(
+        dims, word_inputs, entity_base, requests, place_mat, table_low, shards, 6
+    )
+    losses, grad_logits, states, grad_head, grad_ents = run_head(
+        dims, ents, hits, wholes[5][0], table_low, local_targets, 7
+    )
+    word_grads, incoming, totals = run_backward(
+        dims,
+        word_cotangent,
+        grad_ents,
+        grad_head,
+        gain_rows,
+        entity_rows,
+        place_mat,
+        wholes,
+        saved_layers,
+        8,
+    )
+    wanted = jnp.broadcast_to(got[:, 0][None, :], (8, got.shape[0]))
+    updated = run_update(
+        (
+            (attention_in, attention_in_first, attention_in_second),
+            turned(attention_out, attention_out_first, attention_out_second),
+            (feed_up, feed_up_first, feed_up_second),
+            turned(feed_down, feed_down_first, feed_down_second),
+            (norm_params, norm_params_first, norm_params_second),
+            (entity_proj, entity_proj_first, entity_proj_second),
+            (head_proj, head_proj_first, head_proj_second),
+            (entity_table, entity_table_first, entity_table_second),
+        ),
+        totals,
+        incoming,
+        wanted,
+        grad_logits,
+        states,
+    )
+    updated[1], updated[3] = turned(*updated[1]), turned(*updated[3])
+    results = [losses[0], word_grads]
+    for master, first, second in updated:
+        results += [first, second, master]
+    return tuple(results)
+
+
+def on_device(*arrays):
+    n_dp = lax.axis_size("dp")
+    whole_tiles = D % (16 * n_dp) == 0
+    return (fused_device if whole_tiles else apart_device)(*arrays)
 
 
 def solution(mesh):

time: 589 us -> 523 us (0.89)
  other arithmetic: 51.4 us -> 10.6 us
  Pallas kernels: 463 us -> 497 us
  starting transfers between devices: 17.9 us -> 0 us
  local copies, waits for them, and re-layouts: 24.3 us -> 8.21 us
  matrix products: 13.6 us -> 0 us
  waiting for transfers between devices: 9.59 us -> 0 us
    sub x11 -> x1, other arithmetic: 22.3 us -> 0.01 us  [fused_device(): local_targets = flat_targets - lax.axis_index(('dp', 'mp')) * shard_rows]
    pallas_call x3 -> x2, Pallas kernels: 31.8 us -> 53.3 us  [the longest x1 35.6 us: run_head(): pl.pallas_call(functools.partial(head_body, count), out_shape=[jax.ShapeD...]
    all_to_all x3 -> x0, starting transfers between devices: 17.8 us -> none  [the longest x1 8.31 us: on_device(): lax.all_to_all(request, 'dp', split_axis=0, concat_axis=0, tiled=True)]
    dot_general x8 -> x0, matrix products: 13.6 us -> none  [the longest x1 4.32 us: on_device(): lax.dot_general(grad_logits, all_states, (((0,), (0,)), ((), ())), prefer...]
    unnamed x105 -> x26, local copies, waits for them, and re-layouts: 12.8 us -> 1.69 us
    pallas_call x1, Pallas kernels: 205 us -> 215 us  [run_forward(): pl.pallas_call(functools.partial(forward_body, dims, chunks, needs), out_...]
    all_to_all x3 -> x0, waiting for transfers between devices: 9.58 us -> none  [the longest x1 7.48 us: on_device(): lax.all_to_all(replies, 'dp', split_axis=0, concat_axis=0, tiled=True)]
  transfers between devices with their start and end apart: 5 -> 0, of which waited for: 2 -> 0; matrix products, arithmetic and copies ran while one was open for 6% -> 0% of each run, Pallas kernels for 0% -> 0%
where the time goes in v4:
time: 523 us; the launch traced here: 517 us
  Pallas kernels  497 us (95%)
  other arithmetic  10.6 us (2%)
  local copies, waits for them, and re-layouts  8.21 us (2%)
    pallas_call x1, Pallas kernels, run_backward(): pl.pallas_call(functools.partial(backward_body, dims, names, half, hidden...  228 us
    pallas_call x1, Pallas kernels, run_forward(): pl.pallas_call(functools.partial(forward_body, dims, chunks, needs), out_...  215 us
    pallas_call x1, Pallas kernels, run_head(): pl.pallas_call(functools.partial(head_body, count), out_shape=[jax.ShapeD...  35.6 us
    pallas_call x1, Pallas kernels, run_update(): pl.pallas_call(functools.partial(update_body, names, width), out_shape=[j...  17.6 us

profile of v4, /device:TPU:0, one launch (start us, length us, event | category | flops | bytes accessed | tf_op | source)
XLA Modules:
  0.0 517.1 jit_solution(5660577102894441592)
XLA Ops:
  0.7 0.0 copy-start
  0.7 0.7 convert.5
  1.4 0.6 pad.5.refs_11_
  2.0 0.7 broadcast_maximum_fusion
  2.7 0.1 copy.64
  2.7 0.1 reshape.106
  3.0 1.2 gather_fusion
  4.2 0.7 fusion.2
  4.9 0.1 reshape.115
  5.0 0.1 copy.65
  5.1 0.1 copy.69
  5.2 0.1 sub.15
  5.2 0.6 broadcast_in_dim.14.refs_4_
  5.9 0.1 copy.70
  5.9 0.1 eq.33
  6.0 0.6 convert_bitcast_fusion.1.refs_9_
  6.6 0.6 convert_bitcast_fusion.refs_10_
  7.2 0.7 fusion.1.refs_3_.refs_5_
  8.0 0.7 broadcast_in_dim.13.refs_2_
  8.7 0.6 bitcast_convert_fusion.1.refs_6_
  9.3 0.7 convert_element_type.41.refs_7_
  10.1 0.7 bitcast_convert_fusion.refs_8_
  10.8 0.8 convert_element_type.38
  11.6 3.6 convert_element_type.37.refs_4_.refs_3_
  15.3 215.4 %shard_map.494 = (bf16[12,4,2,2,48,384]{5,4,3,2,1,0:T(8,128)(2,1)}, bf16[2,4,2,2,48,384]{5,4,3,2,1,0:T(8,128)(2,1)}, bf16[2,4,2,2,48,1536]{5,4,3,2,1,0:T(8,128)(...) custom-call(bf16[896,768]{1,0:T(8,128)(2,1)} %refs_0_.3, ...), custom_call_target="tpu_custom_call" | custom-call | tf_op jit(solution)/shard_map/pallas_call | solution.py:994
  230.7 0.9 slice_reduce_fusion
  231.7 0.6 broadcast_in_dim.16.refs_46_
  232.3 35.6 %shard_map.495 = (f32[8,256]{1,0:T(8,128)}, bf16[3968,256]{1,0:T(8,128)(2,1)}, bf16[256,256]{1,0:T(8,128)(2,1)}, bf16[4,2,2,48,256]{4,3,2,1,0:T(8,128)(2,1)}, f32[128,768]{1,0:T(8,128)}) custom-call(f32[128,768]{1,0:T(8,128)} %get-tuple-element.112.refs_0_, bf16[16,128]{1,0:T(8,128)(2,1)} %get-tuple-element.198.refs_1_, ...), custom_call_target="tpu_custom_call" | custom-call | tf_op jit(solution)/shard_map/pallas_call | solution.py:1199
  267.9 228.5 %shard_map.496 = (f32[896,768]{1,0:T(8,128)}, f32[128,256]{1,0:T(8,128)}, f32[48,256]{1,0:T(8,128)}, f32[48,768]{1,0:T(8,128)}, f32[48,768]{1,0:T(8,128)}, /*ind...) custom-call(bf16[896,768]{1,0:T(8,128)(2,1)} %refs_0_.4, ...), custom_call_target="tpu_custom_call" | custom-call | tf_op jit(solution)/shard_map/pallas_call | solution.py:1832
  496.4 1.3 slice.6
  497.6 17.6 %shard_map.497 = (f32[2,6,48,384]{3,2,1,0:T(8,128)}, f32[2,6,48,384]{3,2,1,0:T(8,128)}, f32[2,6,48,384]{3,2,1,0:T(8,128)}, f32[2,48,384]{2,1,0:T(8,128)}, f32[2,...) custom-call(f32[2,6,48,384]{3,2,1,0:T(8,128)} %refs_0_.5, ...), custom_call_target="tpu_custom_call" | custom-call | tf_op jit(solution)/shard_map/pallas_call | solution.py:1356
  515.3 1.5 copy.72
  (28 shorter events, 0.1 us)
Async XLA Ops:
  0.7 2.2 copy-start
  2.9 1.4 copy-start.11
  2.9 2.2 copy-start.9
  2.9 2.3 copy-start.10
  2.9 3.1 copy-start.7
  2.9 3.7 copy-start.8
  2.9 5.7 %copy-start.6 = (f32[2,384,48]{1,2,0:T(8,128)S(1)}, f32[2,384,48]{1,2,0:T(8,128)}, u32[]{:S(2)}) copy-start(f32[2,384,48]{1,2,0:T(8,128)} %param.41) | copy-start | bytes 442372
  2.9 6.4 %copy-start.4 = (f32[2,48,1536]{2,1,0:T(8,128)S(1)}, f32[2,48,1536]{2,1,0:T(8,128)}, u32[]{:S(2)}) copy-start(f32[2,48,1536]{2,1,0:T(8,128)} %refs_6_.1) | copy-start | bytes 1769476
  2.9 7.1 %copy-start.5 = (f32[2,1536,48]{1,2,0:T(8,128)S(1)}, f32[2,1536,48]{1,2,0:T(8,128)}, u32[]{:S(2)}) copy-start(f32[2,1536,48]{1,2,0:T(8,128)} %param.47) | copy-start | bytes 1769476
  4.2 6.6 %copy-start.2 = (f32[2,6,48,384]{3,2,1,0:T(8,128)S(1)}, f32[2,6,48,384]{3,2,1,0:T(8,128)}, u32[]{:S(2)}) copy-start(f32[2,6,48,384]{3,2,1,0:T(8,128)} %refs_0_.5) | copy-start | bytes 2654212
  497.6 17.6 %copy-start.3 = (f32[896,768]{1,0:T(8,128)S(1)}, f32[896,768]{1,0:T(8,128)}, u32[]{:S(2)}) copy-start(f32[896,768]{1,0:T(8,128)} %get-tuple-element.227) | copy-start | bytes 8257540
  515.3 1.6 copy-start.1

commit v5 on v4

--- a/solution.py
+++ b/solution.py
@@ -605,85 +605,134 @@
     return values * cdf, cdf + values * bell
 
 
-class Gather:
-    def __init__(self, dims, chunks, shards, wholes, kept, sems, lags=(3, 2, 2)):
-        self.dims, self.chunks, self.shards, self.wholes, self.kept = dims, chunks, shards, wholes, kept
+LINK_BYTES_US = 45000.0
+HOP_US = 1.5
+ORDERS = ((0, 1, 2), (0, 2, 1), (2, 0, 1), (1, 0, 2))
+
+
+def cut_load(size):
+    return (size // 2) * (size - size // 2)
+
+
+def gather_loads(dims, order, shard_bytes):
+    loads, held = [0.0, 0.0, 0.0], shard_bytes
+    for axis in order:
+        loads[axis] += held * cut_load(dims[axis])
+        held *= dims[axis]
+    return loads
+
+
+def balanced_orders(dims, sizes):
+    total, chosen = [0.0, 0.0, 0.0], []
+    for size in sizes:
+        options = []
+        for rank, order in enumerate(ORDERS):
+            loads = gather_loads(dims, order, size)
+            after = [a + b for a, b in zip(total, loads)]
+            options.append((max(after), sum(after), rank, order, after))
+        best = min(options)
+        chosen.append(best[3])
+        total = best[4]
+    return chosen
+
+
+class Links:
+    def __init__(self, dims):
+        self.dims = dims
+        self.clock, self.free, self.serial = 0.0, [0.0, 0.0, 0.0], 0
+        self.active = []
+
+    def issue(self, axis, message_bytes, what):
+        if self.dims[axis] > 1:
+            begin = max(self.clock, self.free[axis])
+            self.free[axis] = begin + message_bytes * cut_load(self.dims[axis]) / LINK_BYTES_US
+            finish = self.free[axis] + HOP_US
+        else:
+            finish = self.clock
+        self.serial += 1
+        self.active.append((finish, self.serial, what))
+
+    def finish_first(self):
+        first = min(self.active, key=lambda item: item[:2])
+        self.active.remove(first)
+        self.clock = max(self.clock, first[0])
+        self.complete(first[2])
+
+    def spend(self, micros):
+        self.clock += micros
+        while self.active and min(item[0] for item in self.active) <= self.clock:
+            self.finish_first()
+
+
+class Gather(Links):
+    def __init__(self, dims, chunks, shards, wholes, kept, sems):
+        super().__init__(dims)
+        self.chunks, self.shards, self.wholes, self.kept = chunks, shards, wholes, kept
         self.send_sem, self.recv_sem, self.local_sem, self.keep_sem = sems
         self.spot = place(dims)
         self.peers = [axis_peers(dims, axis) for axis in range(3)]
-        self.pending, self.step = {}, 0
-        self.ahead, self.lag1, self.lag2 = lags
-
-    def targets(self):
-        return [target for group in self.peers for _, target in group]
+        self.copies, self.done, self.keeping = {}, set(), []
+        self.next, self.window = 0, 6
+
+    def slab(self, whole, order, stage):
+        held = order[:stage]
+        return whole.at[
+            (slice(None), *[slice(None) if d in held else self.spot[d] for d in range(3)])
+        ]
 
     def start(self, stage, c):
-        which, rows, cols, y_first = self.chunks[c]
-        z, y, x = self.spot
+        which, rows, cols, order = self.chunks[c]
         whole = self.wholes[which].at[rows, :, :, :, :, cols]
         shard = self.shards[which].at[rows, :, cols]
-        copies = []
+        copies, base = [], sum(self.dims[order[i]] for i in range(stage))
+        dst = self.slab(whole, order, stage)
+        src = dst
         if stage == 0:
-            own = pltpu.make_async_copy(shard, whole.at[:, z, y, x], self.local_sem.at[c])
+            own = pltpu.make_async_copy(shard, dst, self.local_sem.at[c])
             own.start()
             copies.append(own)
-            src, dst, group = shard, whole.at[:, z, y, x], self.peers[0]
-        elif stage == 1:
-            src = whole.at[:, :, y, x]
-            dst, group = src, self.peers[1 if y_first else 2]
-        else:
-            src = whole.at[:, :, :, x] if y_first else whole.at[:, :, y]
-            dst, group = src, self.peers[2 if y_first else 1]
-        base = (0, self.dims[0], self.dims[0] + max(self.dims[1:]))[stage]
-        for slot, (_, target) in enumerate(group):
+            src = shard
+        for slot, (_, target) in enumerate(self.peers[order[stage]]):
             sems = self.send_sem.at[c, base + slot], self.recv_sem.at[c, base + slot]
             copies.append(send(src, dst, *sems, target))
-        self.pending[stage, c] = copies
-
-    def finish(self, stage, c):
-        for copy in self.pending.pop((stage, c)):
+        self.copies[stage, c] = copies
+        held = 1
+        for axis in order[:stage]:
+            held *= self.dims[axis]
+        shape = shard.shape
+        self.issue(order[stage], held * 2 * shape[0] * shape[1] * shape[2], (stage, c))
+
+    def complete(self, what):
+        stage, c = what
+        for copy in self.copies.pop(what):
             copy.wait()
-        if stage == 2:
+        if stage < 2:
+            self.start(stage + 1, c)
+        else:
             which, rows, cols, _ = self.chunks[c]
+            at = (rows, slice(None), slice(None), slice(None), slice(None), cols)
             keep = pltpu.make_async_copy(
-                self.wholes[which].at[rows, :, :, :, :, cols],
-                self.kept[which].at[rows, :, :, :, :, cols],
-                self.keep_sem.at[c],
+                self.wholes[which].at[at], self.kept[which].at[at], self.keep_sem.at[c]
             )
             keep.start()
-            self.pending[3, c] = [keep]
-
-    def begin(self):
-        for c in range(min(self.ahead, len(self.chunks))):
-            self.start(0, c)
-
-    def tick(self):
-        total, step = len(self.chunks), self.step
-        if step >= total + self.lag1 + self.lag2:
-            return
-        self.step += 1
-        if step + self.ahead < total:
-            self.start(0, step + self.ahead)
-        if step < total:
-            self.finish(0, step)
-            self.start(1, step)
-        late = step - self.lag1
-        if 0 <= late < total:
-            self.finish(1, late)
-            self.start(2, late)
-        late -= self.lag2
-        if 0 <= late < total:
-            self.finish(2, late)
+            self.keeping.append(keep)
+            self.done.add(c)
+        self.refill()
+
+    def refill(self):
+        while self.next < len(self.chunks) and self.next - len(self.done) < self.window:
+            self.next += 1
+            self.start(0, self.next - 1)
 
     def need(self, c):
-        while self.step < c + self.lag1 + self.lag2 + 1:
-            self.tick()
+        while c not in self.done:
+            self.finish_first()
 
     def close(self):
-        self.need(len(self.chunks) - 1)
-        for key in sorted(self.pending):
-            for copy in self.pending[key]:
-                copy.wait()
+        while self.active:
+            self.finish_first()
+        for keep in self.keeping:
+            keep.wait()
 
 
 class Pair:
@@ -703,7 +752,7 @@
             device_id_type=MESH,
         )
 
-    def run(self, compute, consume, between=None):
+    def run(self, compute, consume, between):
         phase = self.phase
         self.phase += 1
 
@@ -715,10 +764,9 @@
         for c in range(BLOCKS):
             self.mine[c] = compute(c, pl.ds(c * BLOCK, BLOCK)).astype(jnp.bfloat16)
             self.copy(phase, c).start()
-            if between is not None:
-                between()
             if c:
                 take(c - 1)
+            between()
         take(BLOCKS - 1)
 
 
@@ -813,7 +861,7 @@
         count, (look_send.at[0], look_recv.at[0]), lambda me, to: (requests.at[to], got.at[me])
     )
     asking.start()
-    gather.begin()
+    gather.refill()
     here = lax.axis_index("dp")
     got[here] = requests[here]
     asking.wait()
@@ -833,8 +881,7 @@
     )
     answering.start()
     answers[here] = replies[here]
-    gather.tick()
-    gather.tick()
+    gather.spend(7.0)
     answering.wait()
     look_mine[...] = mm(place_mat[...], flat(answers).astype(jnp.bfloat16)).astype(jnp.bfloat16)
     swap = send(look_mine, look_theirs, look_pair.at[0], look_pair.at[1], pair.other)
@@ -888,12 +935,12 @@
                 project_rows(act[name], act["xb"], 0, WORDS, 448, attn, 6 * layer + word_mat)
                 project_rows(act[name], act["xb"], WORDS, ENT_LEN, ENT_LEN, attn, 6 * layer + ent_mat)
             save(layer, name)
-            gather.tick()
+            gather.spend(2.5)
         free("o")
         free("stats")
         for head_pair in range(act["o"].shape[1] // (2 * HEAD_DIM)):
             attend(act, head_pair)
-            gather.tick()
+            gather.spend(4.3)
         save(layer, "o")
         gather.need(needs["out", layer])
         for name in ("n1", "h1b"):
@@ -910,7 +957,7 @@
             h1[rows, :] = value
             act["h1b"][rows, :] = value.astype(jnp.bfloat16)
 
-        pair.run(out_part, first_norm, gather.tick)
+        pair.run(out_part, first_norm, lambda: gather.spend(1.3))
         save(layer, "n1")
         save(layer, "h1b")
         gather.need(needs["up", layer, 1])
@@ -930,7 +977,7 @@
 
         for c in range(BLOCKS):
             up_block(c)
-            gather.tick()
+            gather.spend(2.6)
         save(layer, "g")
         save(layer, "slope")
         gather.need(needs["down", layer, 1])
@@ -944,7 +991,7 @@
             act["stats"][rows, 9:10] = scale
             x[rows, :] = hat * gain[2] + gain[3]
 
-        pair.run(down_part, second_norm, gather.tick)
+        pair.run(down_part, second_norm, lambda: gather.spend(1.8))
         save(layer, "n2")
         save(layer, "stats")
     ents_out[...] = x[WORDS:]
@@ -960,36 +1007,40 @@
 MAT_ORDER = (4, 5, 0, 2, 1, 3)
 
 
-def gather_plan(hidden):
+def gather_plan(dims, shards):
     every = slice(None)
-    chunks = [(6, pl.ds(0, 1), every, True), (4, pl.ds(0, 1), every, False)]
-    needs = {"kinds": KINDS, "norms": 0, "proj": 1}
-    y_first = [True]
-
-    def add(name, which, row, cols):
-        chunks.append((which, pl.ds(row, 1), cols, y_first[0]))
-        y_first[0] = not y_first[0]
+    chunks, needs, sizes = [], {"kinds": KINDS}, []
+    hidden = shards[2].shape[-1]
+
+    def add(name, which, row, cols=every, part=1):
+        chunks.append((which, pl.ds(row, 1), cols))
+        sizes.append(2 * shards[which].shape[1] * shards[which].shape[2] // part)
         needs[name] = len(chunks) - 1
 
+    add("norms", 6, 0)
+    add("proj", 4, 0)
     for layer in range(LAYERS):
         for mat in MAT_ORDER:
-            add(("mat", layer, mat), 0, 6 * layer + mat, every)
-        add(("out", layer), 1, layer, every)
+            add(("mat", layer, mat), 0, 6 * layer + mat)
+        add(("out", layer), 1, layer)
+        if layer == LAYERS - 1:
+            add("head", 5, 0)
         for which, name in ((2, "up"), (3, "down")):
             for part in range(2):
-                add((name, layer, part), which, layer, pl.ds(part * (hidden // 2), hidden // 2))
-    add("head", 5, 0, every)
-    return chunks, needs
+                cols = pl.ds(part * (hidden // 2), hidden // 2)
+                add((name, layer, part), which, layer, cols, 2)
+    orders = balanced_orders(dims, sizes)
+    return [chunk + (order,) for chunk, order in zip(chunks, orders)], needs
 
 
 def run_forward(dims, words, base, requests, place_mat, table_low, shards, collective_id):
     half, hidden = shards[0].shape[-1], shards[2].shape[-1]
-    chunks, needs = gather_plan(hidden)
+    chunks, needs = gather_plan(dims, shards)
     shapes = saved_shapes(half, hidden)
     low, full = jnp.bfloat16, jnp.float32
     width, slots = table_low.shape[1], requests.shape[0] * requests.shape[1]
     wholes = [(s.shape[0], *dims, *s.shape[1:]) for s in shards]
-    copies = dims[0] + 2 * max(dims[1:])
+    copies = sum(dims)
     saved_out = [jax.ShapeDtypeStruct(*shapes[name]) for _ in range(LAYERS) for name in SAVED]
     result = pl.pallas_call(
         functools.partial(forward_body, dims, chunks, needs),
@@ -1379,79 +1430,70 @@
     return back, gain_part, jnp.sum(grad, axis=0, keepdims=True)
 
 
-class Sums:
+class Sums(Links):
     def __init__(self, dims, units, buffers, totals, sems, free_sem):
-        self.dims, self.units, self.totals = dims, units, totals
-        self.buffers = buffers
+        super().__init__(dims)
+        self.units, self.totals, self.buffers = units, totals, buffers
         self.send_sem, self.recv_sem = sems
         self.free_sem = free_sem
         self.spot = place(dims)
         self.peers = [axis_peers(dims, axis) for axis in range(3)]
-        self.queue, self.done = [], set()
-        self.least = 2
-
-    def group(self, stage, y_first):
-        return self.peers[((1, 2, 0) if y_first else (2, 1, 0))[stage]]
+        self.copies, self.done = {}, set()
 
     def start(self, stage, u):
-        slot, y_first, turn = self.units[u]
-        part, first, second, third = self.buffers[slot]
-        z, y, x = self.spot
-        group = self.group(stage, y_first)
+        slot, order, turn = self.units[u]
+        part, arrived = self.buffers[slot][0], self.buffers[slot][1 + stage]
+        axis = order[stage]
+        group = self.peers[axis]
         if turn and group:
             pl.semaphore_wait(self.free_sem.at[slot, stage], len(group))
-        copies = []
-        base = (0, max(self.dims[1:]), 2 * max(self.dims[1:]))[stage]
+        copies, base = [], sum(self.dims[order[i]] for i in range(stage))
         for k, (spot, target) in enumerate(group):
-            if stage == 0:
-                src = part.at[:, spot] if y_first else part.at[:, :, spot]
-                dst = first.at[k]
-            elif stage == 1:
-                src = part.at[:, y, spot] if y_first else part.at[:, spot, x]
-                dst = second.at[k]
-            else:
-                src, dst = part.at[spot, y, x], third.at[k]
+            at = [slice(None)] * 3
+            for d in order[:stage]:
+                at[d] = self.spot[d]
+            at[axis] = spot
             sems = self.send_sem.at[u, base + k], self.recv_sem.at[u, base + k]
-            copies.append(send(src, dst, *sems, target))
-        self.queue.append((stage, u, copies))
-
-    def advance(self):
-        stage, u, copies = self.queue.pop(0)
-        slot, y_first, turn = self.units[u]
-        part, first, second, third = self.buffers[slot]
-        z, y, x = self.spot
-        for copy in copies:
+            copies.append(send(part.at[tuple(at)], arrived.at[k], *sems, target))
+        self.copies[stage, u] = copies
+        held = 1
+        for d in order[stage + 1 :]:
+            held *= self.dims[d]
+        self.issue(axis, held * 2 * part.shape[3] * part.shape[4], (stage, u))
+
+    def complete(self, what):
+        stage, u = what
+        slot, order, turn = self.units[u]
+        part, arrived = self.buffers[slot][0], self.buffers[slot][1 + stage]
+        for copy in self.copies.pop(what):
             copy.wait()
-        group = self.group(stage, y_first)
-        across = self.dims[2] if y_first else self.dims[1]
-        if stage == 0 and group:
-
-            def add_first(i, carry):
-                a, b = i // across, i % across
-                at = (a, y, b) if y_first else (a, b, x)
-                value = part[at].astype(jnp.float32)
-                for k in range(len(group)):
-                    value += first[k, a, b].astype(jnp.float32)
+        axis = order[stage]
+        group = self.peers[axis]
+        rest = [d for d in range(3) if d not in order[: stage + 1]]
+
+        def total_at(spots):
+            at = tuple(spots.get(d, self.spot[d]) for d in range(3))
+            value = part[at].astype(jnp.float32)
+            for k in range(len(group)):
+                value += arrived[(k, *[spots[d] for d in rest])].astype(jnp.float32)
+            return at, value
+
+        if stage == 2:
+            self.totals[u][...] = total_at({})[1]
+            self.done.add(u)
+        elif group:
+            inner = self.dims[rest[-1]]
+
+            def add(i, carry):
+                spots = {rest[-1]: i % inner}
+                if len(rest) == 2:
+                    spots[rest[0]] = i // inner
+                at, value = total_at(spots)
                 part[at] = value.astype(part.dtype)
                 return carry
 
-            lax.fori_loop(0, self.dims[0] * across, add_first, 0)
-        if stage == 1 and group:
-
-            def add_second(i, carry):
-                value = part[i, y, x].astype(jnp.float32)
-                for k in range(len(group)):
-                    value += second[k, i].astype(jnp.float32)
-                part[i, y, x] = value.astype(part.dtype)
-                return carry
-
-            lax.fori_loop(0, self.dims[0], add_second, 0)
-        if stage == 2:
-            value = part[z, y, x].astype(jnp.float32)
-            for k in range(len(group)):
-                value += third[k].astype(jnp.float32)
-            self.totals[u][...] = value
-            self.done.add(u)
+            count = inner * (self.dims[rest[0]] if len(rest) == 2 else 1)
+            lax.fori_loop(0, count, add, 0)
         if self.reused(u):
             for _, target in group:
                 pl.semaphore_signal(
@@ -1464,25 +1506,23 @@
         slot, _, turn = self.units[u]
         return not turn and sum(unit[0] == slot for unit in self.units) > 1
 
-    def tick(self):
-        if len(self.queue) > self.least:
-            self.advance()
-
     def need(self, u):
         while u not in self.done:
-            self.advance()
+            self.finish_first()
 
     def close(self):
-        while self.queue:
-            self.advance()
+        while self.active:
+            self.finish_first()
 
 
 UNITS = ("down0", "down1", "up0", "up1", "out", "words", "ents", "key", "value")
 EXTRA = ("head", "proj", "norms")
-UNIT_FIRST = dict(
-    down0=True, down1=False, up0=True, up1=False, out=True, words=True, ents=False, key=True,
-    value=False, head=True, proj=False, norms=True,
-)
+
+
+def unit_orders(dims, blocks):
+    names = list(blocks)
+    sizes = [2 * rows * cols for rows, cols in blocks.values()]
+    return {name: order[::-1] for name, order in zip(names, balanced_orders(dims, sizes))}
 
 
 def sum_plan():
@@ -1500,7 +1540,7 @@
     }[name]
 
 
-def backward_body(dims, names, half, hidden, *refs):
+def backward_body(dims, names, orders, half, hidden, *refs):
     refs = list(refs)
 
     def take(count):
@@ -1529,7 +1569,7 @@
     for name in names:
         kind = name if isinstance(name, str) else name[1]
         turn = not isinstance(name, str) and name[0] < LAYERS - 1
-        units.append((slots.index(kind), UNIT_FIRST[kind], turn))
+        units.append((slots.index(kind), orders[kind], turn))
     sums = Sums(dims, units, buffers, totals, sum_sems, free_sem)
     pair = Pair(mine, theirs, pair_sems)
     count = dims[0] * dims[1] * dims[2]
@@ -1547,9 +1587,7 @@
         for copy in loads.pop(key, []):
             copy.wait()
 
-    def tick(times=1):
-        for _ in range(times):
-            sums.tick()
+    tick = sums.spend
 
     def begin_layer(layer):
         s = saved[layer]
@@ -1612,6 +1650,7 @@
             return carry
 
         lax.fori_loop(0, BLOCKS, late_norm, 0)
+        tick(3.0)
         load("n1", saved[layer]["n1"], hat)
         ready("g")
         for i in range(2):
@@ -1620,7 +1659,7 @@
             cols = slice(i * (hidden // 2), (i + 1) * (hidden // 2))
             fill("down%d" % i, glow, left, cols)
             submit(layer, "down%d" % i)
-            tick()
+            tick(2.2)
         ahead = saved[layer]
         for i, name in enumerate(("k", "qw", "qe", "v")):
             load("qkv", ahead[name], left.at[:, pl.ds(i * half, half)])
@@ -1637,7 +1676,7 @@
             return carry
 
         lax.fori_loop(0, BLOCKS, inner, 0)
-        tick()
+        tick(3.5)
         load("up", w_up.at[layer], mat_wide)
         ready("h1b")
         for i in range(2):
@@ -1646,7 +1685,7 @@
             cols = slice(i * (hidden // 2), (i + 1) * (hidden // 2))
             fill("up%d" % i, xh, right, cols)
             submit(layer, "up%d" % i)
-            tick()
+            tick(2.2)
         load("xb", saved[layer]["xb"], xh)
         ready("up")
         ready("n1")
@@ -1663,7 +1702,7 @@
             add_norm(4 * layer, gain_part)
             add_norm(4 * layer + 1, shift_part)
 
-        pair.run(up_part, early_norm, tick)
+        pair.run(up_part, early_norm, lambda: tick(2.0))
         ready("o")
         ready("out")
         if not last:
@@ -1678,7 +1717,7 @@
             return carry
 
         lax.fori_loop(0, BLOCKS, mixed, 0)
-        tick()
+        tick(3.7)
         ready("qkv")
         for head_pair in range(half // (2 * HEAD_DIM)):
             lo = head_pair * 2 * HEAD_DIM
@@ -1731,7 +1770,7 @@
 
             for first in range(0, BLOCKS, 2):
                 lax.fori_loop(first, first + 2, block, 0)
-                tick()
+                tick(4.7)
             at = 2 * half + lo
             right[:, at : at + 2 * HEAD_DIM] = (dk_acc[...] * 0.125).astype(jnp.bfloat16)
             at = 3 * half + lo
@@ -1748,7 +1787,7 @@
                 sums.need(names.index((layer + 1, name)))
             fill(name, xh, right, cols, rows)
             submit(layer, name)
-            tick()
+            tick(1.4)
         ready("attn")
         mats = [slice(j * half, (j + 1) * half) for j in range(4)]
 
@@ -1768,7 +1807,7 @@
         def to_input(c, rows, total):
             gacc[rows, :] += total
 
-        pair.run(input_part, to_input, tick)
+        pair.run(input_part, to_input, lambda: tick(2.0))
         if layer:
             begin_layer(layer - 1)
     ready("proj")
@@ -1812,25 +1851,22 @@
     blocks["proj"] = (kept[4].shape[4], D)
     blocks["norms"] = (16, 128)
     scratch = []
+    orders = unit_orders(dims, blocks)
     for name in UNITS + EXTRA:
-        y_first = UNIT_FIRST[name]
-        own = (dims[0], dims[2] if y_first else dims[1])
-        turns = (dims[1], dims[2]) if y_first else (dims[2], dims[1])
-        block = blocks[name]
-        scratch += [
-            pltpu.VMEM((*dims, *block), low),
-            pltpu.VMEM((max(turns[0] - 1, 1), *own, *block), low),
-            pltpu.VMEM((max(turns[1] - 1, 1), dims[0], *block), low),
-            pltpu.VMEM((max(dims[0] - 1, 1), *block), low),
-        ]
-    copies = dims[0] + 2 * max(dims[1:])
+        order, block = orders[name], blocks[name]
+        scratch.append(pltpu.VMEM((*dims, *block), low))
+        for stage in range(3):
+            rest = [dims[d] for d in range(3) if d not in order[: stage + 1]]
+            peers = max(dims[order[stage]] - 1, 1)
+            scratch.append(pltpu.VMEM((peers, *rest, *block), low))
+    copies = sum(dims)
     kinds = [name if isinstance(name, str) else name[1] for name in names]
     count = dims[0] * dims[1] * dims[2]
     width, slots = kept[5].shape[-1], place_mat.shape[1]
     inputs = [cotangent, grad_ents, grad_head, gains, entity_rows, place_mat, *kept[:5]]
     inputs += [saved[layer][name] for layer in range(LAYERS) for name in SAVED]
     result = pl.pallas_call(
-        functools.partial(backward_body, dims, names, half, hidden),
+        functools.partial(backward_body, dims, names, orders, half, hidden),
         out_shape=[
             jax.ShapeDtypeStruct((WORDS, D), full),
             jax.ShapeDtypeStruct((slots, width), full),

time: 523 us -> 474 us (0.906)
  Pallas kernels: 497 us -> 448 us
    pallas_call x1, Pallas kernels: 228 us -> 195 us  [run_backward(): pl.pallas_call(functools.partial(backward_body, dims, names, orders, half...]
    pallas_call x1, Pallas kernels: 215 us -> 197 us  [run_forward(): pl.pallas_call(functools.partial(forward_body, dims, chunks, needs), out_...]
where the time goes in v5:
time: 474 us; the launch traced here: 468 us
  Pallas kernels  448 us (95%)
  other arithmetic  10.6 us (2%)
  local copies, waits for them, and re-layouts  8.21 us (2%)
    pallas_call x1, Pallas kernels, run_forward(): pl.pallas_call(functools.partial(forward_body, dims, chunks, needs), out_...  197 us
    pallas_call x1, Pallas kernels, run_backward(): pl.pallas_call(functools.partial(backward_body, dims, names, orders, half...  195 us
    pallas_call x1, Pallas kernels, run_head(): pl.pallas_call(functools.partial(head_body, count), out_shape=[jax.ShapeD...  39.1 us
    pallas_call x1, Pallas kernels, run_update(): pl.pallas_call(functools.partial(update_body, names, width), out_shape=[j...  17.6 us

profile of v5, /device:TPU:0, one launch (start us, length us, event | category | flops | bytes accessed | tf_op | source)
XLA Modules:
  0.0 468.0 jit_solution(4615720296920238698)
XLA Ops:
  0.7 0.0 copy-start
  0.7 0.7 convert.5
  1.4 0.6 pad.5.refs_11_
  2.0 0.7 broadcast_maximum_fusion
  2.7 0.1 copy.64
  2.7 0.1 reshape.106
  3.0 1.2 gather_fusion
  4.2 0.7 fusion.2
  4.9 0.1 reshape.115
  5.0 0.1 copy.65
  5.1 0.1 copy.69
  5.2 0.1 sub.15
  5.2 0.6 broadcast_in_dim.14.refs_4_
  5.9 0.1 copy.70
  5.9 0.1 eq.33
  6.0 0.6 convert_bitcast_fusion.1.refs_9_
  6.6 0.6 convert_bitcast_fusion.refs_10_
  7.2 0.7 fusion.1.refs_3_.refs_5_
  8.0 0.7 broadcast_in_dim.13.refs_2_
  8.7 0.6 bitcast_convert_fusion.1.refs_6_
  9.3 0.7 convert_element_type.41.refs_7_
  10.1 0.7 bitcast_convert_fusion.refs_8_
  10.8 0.8 convert_element_type.38
  11.6 3.6 convert_element_type.37.refs_4_.refs_3_
  15.3 196.7 %shard_map.494 = (bf16[12,4,2,2,48,384]{5,4,3,2,1,0:T(8,128)(2,1)}, bf16[2,4,2,2,48,384]{5,4,3,2,1,0:T(8,128)(2,1)}, bf16[2,4,2,2,48,1536]{5,4,3,2,1,0:T(8,128)(...) custom-call(bf16[896,768]{1,0:T(8,128)(2,1)} %refs_0_.3, ...), custom_call_target="tpu_custom_call" | custom-call | tf_op jit(solution)/shard_map/pallas_call | solution.py:1045
  211.9 0.9 slice_reduce_fusion
  212.9 0.6 broadcast_in_dim.16.refs_46_
  213.5 39.1 %shard_map.495 = (f32[8,256]{1,0:T(8,128)}, bf16[3968,256]{1,0:T(8,128)(2,1)}, bf16[256,256]{1,0:T(8,128)(2,1)}, bf16[4,2,2,48,256]{4,3,2,1,0:T(8,128)(2,1)}, f32[128,768]{1,0:T(8,128)}) custom-call(f32[128,768]{1,0:T(8,128)} %get-tuple-element.112.refs_0_, bf16[16,128]{1,0:T(8,128)(2,1)} %get-tuple-element.198.refs_1_, ...), custom_call_target="tpu_custom_call" | custom-call | tf_op jit(solution)/shard_map/pallas_call | solution.py:1250
  252.6 194.6 %shard_map.496 = (f32[896,768]{1,0:T(8,128)}, f32[128,256]{1,0:T(8,128)}, f32[48,256]{1,0:T(8,128)}, f32[48,768]{1,0:T(8,128)}, f32[48,768]{1,0:T(8,128)}, /*ind...) custom-call(bf16[896,768]{1,0:T(8,128)(2,1)} %refs_0_.4, ...), custom_call_target="tpu_custom_call" | custom-call | tf_op jit(solution)/shard_map/pallas_call | solution.py:1868
  447.3 1.3 slice.6
  448.5 17.6 %shard_map.497 = (f32[2,6,48,384]{3,2,1,0:T(8,128)}, f32[2,6,48,384]{3,2,1,0:T(8,128)}, f32[2,6,48,384]{3,2,1,0:T(8,128)}, f32[2,48,384]{2,1,0:T(8,128)}, f32[2,...) custom-call(f32[2,6,48,384]{3,2,1,0:T(8,128)} %refs_0_.5, ...), custom_call_target="tpu_custom_call" | custom-call | tf_op jit(solution)/shard_map/pallas_call | solution.py:1407
  466.2 1.5 copy.72
  (28 shorter events, 0.1 us)
Async XLA Ops:
  0.7 2.2 copy-start
  2.9 1.4 copy-start.11
  2.9 2.2 copy-start.9
  2.9 2.3 copy-start.10
  2.9 3.1 copy-start.7
  2.9 3.7 copy-start.8
  2.9 5.7 %copy-start.6 = (f32[2,384,48]{1,2,0:T(8,128)S(1)}, f32[2,384,48]{1,2,0:T(8,128)}, u32[]{:S(2)}) copy-start(f32[2,384,48]{1,2,0:T(8,128)} %param.41) | copy-start | bytes 442372
  2.9 6.4 %copy-start.4 = (f32[2,48,1536]{2,1,0:T(8,128)S(1)}, f32[2,48,1536]{2,1,0:T(8,128)}, u32[]{:S(2)}) copy-start(f32[2,48,1536]{2,1,0:T(8,128)} %refs_6_.1) | copy-start | bytes 1769476
  2.9 7.1 %copy-start.5 = (f32[2,1536,48]{1,2,0:T(8,128)S(1)}, f32[2,1536,48]{1,2,0:T(8,128)}, u32[]{:S(2)}) copy-start(f32[2,1536,48]{1,2,0:T(8,128)} %param.47) | copy-start | bytes 1769476
  4.2 6.6 %copy-start.2 = (f32[2,6,48,384]{3,2,1,0:T(8,128)S(1)}, f32[2,6,48,384]{3,2,1,0:T(8,128)}, u32[]{:S(2)}) copy-start(f32[2,6,48,384]{3,2,1,0:T(8,128)} %refs_0_.5) | copy-start | bytes 2654212
  448.5 17.6 %copy-start.3 = (f32[896,768]{1,0:T(8,128)S(1)}, f32[896,768]{1,0:T(8,128)}, u32[]{:S(2)}) copy-start(f32[896,768]{1,0:T(8,128)} %get-tuple-element.227) | copy-start | bytes 8257540
  466.2 1.6 copy-start.1

commit v6 on v5

--- a/solution.py
+++ b/solution.py
@@ -605,7 +605,8 @@
     return values * cdf, cdf + values * bell
 
 
-LINK_BYTES_US = 45000.0
+GATHER_RATE = 52000.0
+SUM_RATE = 45000.0
 HOP_US = 1.5
 ORDERS = ((0, 1, 2), (0, 2, 1), (2, 0, 1), (1, 0, 2))
 
@@ -637,15 +638,15 @@
 
 
 class Links:
-    def __init__(self, dims):
-        self.dims = dims
+    def __init__(self, dims, rate):
+        self.dims, self.rate = dims, rate
         self.clock, self.free, self.serial = 0.0, [0.0, 0.0, 0.0], 0
         self.active = []
 
     def issue(self, axis, message_bytes, what):
         if self.dims[axis] > 1:
             begin = max(self.clock, self.free[axis])
-            self.free[axis] = begin + message_bytes * cut_load(self.dims[axis]) / LINK_BYTES_US
+            self.free[axis] = begin + message_bytes * cut_load(self.dims[axis]) / self.rate
             finish = self.free[axis] + HOP_US
         else:
             finish = self.clock
@@ -666,7 +667,7 @@
 
 class Gather(Links):
     def __init__(self, dims, chunks, shards, wholes, kept, sems):
-        super().__init__(dims)
+        super().__init__(dims, GATHER_RATE)
         self.chunks, self.shards, self.wholes, self.kept = chunks, shards, wholes, kept
         self.send_sem, self.recv_sem, self.local_sem, self.keep_sem = sems
         self.spot = place(dims)
@@ -843,7 +844,7 @@
     shards = take(len(needs["kinds"]))
     kept = take(len(needs["kinds"]))
     saved = [dict(zip(SAVED, take(len(SAVED)))) for _ in range(LAYERS)]
-    ents_out, gains_out, rows_in, got_out = take(4)
+    ents_out, gains_out, rows_in, got_out, table_out = take(5)
     wholes = take(len(needs["kinds"]))
     act = dict(zip(SAVED, take(len(SAVED))))
     x, h1, gains, mine, theirs = take(5)
@@ -851,7 +852,9 @@
     pair_sems = take(2)
     (save_sem,) = take(1)
     got, replies, answers, look_mine, look_theirs = take(5)
-    look_send, look_recv, look_pair = take(3)
+    look_send, look_recv, look_pair, table_full, table_sem = take(5)
+    reading = pltpu.make_async_copy(table, table_full, table_sem)
+    reading.start()
 
     gather = Gather(dims, chunks, shards, wholes, kept, gather_sems)
     pair = Pair(mine, theirs, pair_sems)
@@ -865,13 +868,17 @@
     here = lax.axis_index("dp")
     got[here] = requests[here]
     asking.wait()
+    reading.wait()
     wanted = flat(got)
     got_out[...] = wanted
 
     def look(j, found):
         lane = lax.broadcasted_iota(jnp.int32, wanted.shape, 1) + j * 128
         hot = jnp.where(wanted == lane, 1.0, 0.0).astype(jnp.bfloat16)
-        return found + mm(hot, table[pl.ds(pl.multiple_of(j * 128, 128), 128), :])
+        rows = pl.ds(pl.multiple_of(j * 128, 128), 128)
+        low = table_full[rows, :].astype(jnp.bfloat16)
+        table_out[rows, :] = low
+        return found + mm(hot, low)
 
     found = jnp.zeros((wanted.shape[0], table.shape[1]), jnp.float32)
     found = lax.fori_loop(0, table.shape[0] // 128, look, found)
@@ -1033,12 +1040,12 @@
     return [chunk + (order,) for chunk, order in zip(chunks, orders)], needs
 
 
-def run_forward(dims, words, base, requests, place_mat, table_low, shards, collective_id):
+def run_forward(dims, words, base, requests, place_mat, table, shards, collective_id):
     half, hidden = shards[0].shape[-1], shards[2].shape[-1]
     chunks, needs = gather_plan(dims, shards)
     shapes = saved_shapes(half, hidden)
     low, full = jnp.bfloat16, jnp.float32
-    width, slots = table_low.shape[1], requests.shape[0] * requests.shape[1]
+    width, slots = table.shape[1], requests.shape[0] * requests.shape[1]
     wholes = [(s.shape[0], *dims, *s.shape[1:]) for s in shards]
     copies = sum(dims)
     saved_out = [jax.ShapeDtypeStruct(*shapes[name]) for _ in range(LAYERS) for name in SAVED]
@@ -1051,9 +1058,10 @@
             jax.ShapeDtypeStruct((16, D), full),
             jax.ShapeDtypeStruct((ENT_LEN, width), low),
             jax.ShapeDtypeStruct((slots, 128), jnp.int32),
+            jax.ShapeDtypeStruct(table.shape, low),
         ],
-        in_specs=[VMEM] * 5 + [ANY] * len(shards),
-        out_specs=[ANY] * (len(wholes) + len(saved_out)) + [VMEM] * 4,
+        in_specs=[VMEM] * 4 + [ANY] * (1 + len(shards)),
+        out_specs=[ANY] * (len(wholes) + len(saved_out)) + [VMEM] * 5,
         scratch_shapes=[pltpu.VMEM(shape, low) for shape in wholes]
         + [pltpu.VMEM(*shapes[name]) for name in SAVED]
         + [
@@ -1077,17 +1085,19 @@
             pltpu.SemaphoreType.DMA((2, requests.shape[0])),
             pltpu.SemaphoreType.DMA((2, requests.shape[0])),
             pltpu.SemaphoreType.DMA((2,)),
+            pltpu.VMEM(table.shape, full),
+            pltpu.SemaphoreType.DMA,
         ],
         compiler_params=pltpu.CompilerParams(
             collective_id=collective_id, has_side_effects=True, vmem_limit_bytes=VMEM_BYTES
         ),
-    )(words, base, requests, place_mat, table_low, *shards)
+    )(words, base, requests, place_mat, table, *shards)
     kept = result[: len(wholes)]
     saved = [
         dict(zip(SAVED, result[len(wholes) + layer * len(SAVED) :][: len(SAVED)]))
         for layer in range(LAYERS)
     ]
-    return kept, saved, *result[-4:]
+    return kept, saved, *result[-5:]
 
 
 class Fan:
@@ -1145,8 +1155,8 @@
     ents, hits, head, table, local_targets = refs[:5]
     losses, grad_logits, states, grad_head, grad_ents = refs[5:10]
     logits, own_states, all_states, stat_mine, stat_theirs, stat_both, stat_all = refs[10:17]
-    grad_part, grad_all, share_mine, share_theirs = refs[17:21]
-    send_sem, recv_sem, pair_send, pair_recv = refs[21:]
+    grad_part, hit_part, grad_send, grad_all, share_mine, share_theirs = refs[17:23]
+    factors, turned_factors, send_sem, recv_sem, pair_send, pair_recv = refs[23:]
     index = lax.axis_index("dp")
     other = (index, 1 - lax.axis_index("mp"))
     greet_line(count, [other])
@@ -1182,53 +1192,70 @@
     empty = jnp.zeros((1, total_rows), jnp.float32)
     peak, picked = lax.fori_loop(0, TABLE_CUTS, score, (empty - 3e38, empty))
 
+    grad_part[...] = jnp.zeros_like(grad_part)
+    hit_part[...] = jnp.zeros_like(hit_part)
+
     def weigh(c, weight):
-        return weight + jnp.sum(jnp.exp(logits[rows_of(c), :] - peak), axis=0, keepdims=True)
+        raised = jnp.exp(logits[rows_of(c), :] - peak)
+        hot = jnp.where(hit_of(c), 1.0, 0.0).astype(jnp.bfloat16)
+        grad_part[...] += mm_lt(raised.astype(jnp.bfloat16), table[rows_of(c), :])
+        hit_part[...] += mm_lt(hot, table[rows_of(c), :])
+        return weight + jnp.sum(raised, axis=0, keepdims=True)
 
     weight = lax.fori_loop(0, TABLE_CUTS, weigh, empty)
     stat_mine[0:1, :] = peak
     stat_mine[1:2, :] = weight
     stat_mine[2:3, :] = picked
-    swap = send(stat_mine, stat_theirs, pair_send.at[0], pair_recv.at[0], other)
+    block = (count, MASK_ENT, table.shape[1])
+    grad_send[:, :MASK_ENT, :] = grad_part[...].astype(jnp.bfloat16).reshape(block)
+    grad_send[:, MASK_ENT:, :] = hit_part[...].astype(jnp.bfloat16).reshape(block)
+    fan = Fan(count, (send_sem.at[1], recv_sem.at[1]), lambda me, to: (stat_mine, stat_all.at[me]))
+    fan.start()
+    back = Fan(
+        count, (send_sem.at[2], recv_sem.at[2]), lambda me, to: (grad_send.at[to], grad_all.at[me])
+    )
+    back.start()
+    stat_all[index] = stat_mine[...]
+    grad_all[index] = grad_send[index]
+    fan.wait()
+    peak_line = stat_all[0, 0:1, :]
+    for d in range(1, count):
+        peak_line = jnp.maximum(peak_line, stat_all[d, 0:1, :])
+    weight_line = picked_line = empty
+    for d in range(count):
+        weight_line += stat_all[d, 1:2, :] * jnp.exp(stat_all[d, 0:1, :] - peak_line)
+        picked_line += stat_all[d, 2:3, :]
+    stat_both[0:1, :] = peak_line
+    stat_both[1:2, :] = weight_line
+    stat_both[2:3, :] = picked_line
+    swap = send(stat_both, stat_theirs, pair_send.at[0], pair_recv.at[0], other)
     swap.wait()
-    peak_both = jnp.maximum(stat_mine[0:1, :], stat_theirs[0:1, :])
-    stat_both[0:1, :] = peak_both
-    stat_both[1:2, :] = stat_mine[1:2, :] * jnp.exp(stat_mine[0:1, :] - peak_both) + stat_theirs[
-        1:2, :
-    ] * jnp.exp(stat_theirs[0:1, :] - peak_both)
-    stat_both[2:3, :] = stat_mine[2:3, :] + stat_theirs[2:3, :]
-    fan = Fan(count, (send_sem.at[1], recv_sem.at[1]), lambda me, to: (stat_both, stat_all.at[me]))
-    fan.start()
-    stat_all[index] = stat_both[...]
-    fan.wait()
-    peak_all = stat_all[0, 0:1, :]
-    for d in range(1, count):
-        peak_all = jnp.maximum(peak_all, stat_all[d, 0:1, :])
-    weight_all = picked_all = empty
+    peak_all = jnp.maximum(peak_line, stat_theirs[0:1, :])
+    weight_all = weight_line * jnp.exp(peak_line - peak_all) + stat_theirs[1:2, :] * jnp.exp(
+        stat_theirs[0:1, :] - peak_all
+    )
+    log_norm = peak_all + jnp.log(weight_all)
+    losses[...] = jnp.broadcast_to(log_norm - picked_line - stat_theirs[2:3, :], losses.shape)
+    factors[...] = jnp.zeros_like(factors)
     for d in range(count):
-        weight_all += stat_all[d, 1:2, :] * jnp.exp(stat_all[d, 0:1, :] - peak_all)
-        picked_all += stat_all[d, 2:3, :]
-    log_norm = peak_all + jnp.log(weight_all)
-    losses[...] = jnp.broadcast_to(log_norm - picked_all, losses.shape)
-    grad_part[...] = jnp.zeros_like(grad_part)
+        factors[d : d + 1, :] = jnp.exp(stat_all[d, 0:1, :] - log_norm)
+    turned_factors[...] = factors[...].T
+    own = turned_factors[pl.ds(pl.multiple_of(index * MASK_ENT, MASK_ENT), MASK_ENT), :]
+    back.wait()
+    share = jnp.zeros((MASK_ENT, table.shape[1]), jnp.float32)
+    for d in range(count):
+        share += grad_all[d, :MASK_ENT, :].astype(jnp.float32) * own[:, d : d + 1]
+        share -= grad_all[d, MASK_ENT:, :].astype(jnp.float32)
+    share_mine[...] = share * (1.0 / total_rows)
+    swap = send(share_mine, share_theirs, pair_send.at[1], pair_recv.at[1], other)
 
     def grads(c, carry):
         prob = jnp.exp(logits[rows_of(c), :] - log_norm)
         part = (prob - jnp.where(hit_of(c), 1.0, 0.0)) * (1.0 / total_rows)
-        low = part.astype(jnp.bfloat16)
-        grad_logits[rows_of(c), :] = low
-        grad_part[...] += mm_lt(low, table[rows_of(c), :]).reshape(grad_part.shape)
+        grad_logits[rows_of(c), :] = part.astype(jnp.bfloat16)
         return carry
 
     lax.fori_loop(0, TABLE_CUTS, grads, 0)
-    fan = Fan(
-        count, (send_sem.at[2], recv_sem.at[2]), lambda me, to: (grad_part.at[to], grad_all.at[me])
-    )
-    fan.start()
-    grad_all[index] = grad_part[index]
-    fan.wait()
-    share_mine[...] = jnp.sum(grad_all[...], axis=0)
-    swap = send(share_mine, share_theirs, pair_send.at[1], pair_recv.at[1], other)
     swap.wait()
     grad_pre = ((share_mine[...] + share_theirs[...]) * slope).astype(jnp.bfloat16)
     grad_head[...] = mm_lt(masked, grad_pre).astype(jnp.bfloat16).reshape(grad_head.shape)
@@ -1266,10 +1293,14 @@
             pltpu.VMEM((8, rows), full),
             pltpu.VMEM((8, rows), full),
             pltpu.VMEM((count, 8, rows), full),
-            pltpu.VMEM((count, MASK_ENT, width), full),
-            pltpu.VMEM((count, MASK_ENT, width), full),
+            pltpu.VMEM((rows, width), full),
+            pltpu.VMEM((rows, width), full),
+            pltpu.VMEM((count, 2 * MASK_ENT, width), low),
+            pltpu.VMEM((count, 2 * MASK_ENT, width), low),
             pltpu.VMEM((MASK_ENT, width), full),
             pltpu.VMEM((MASK_ENT, width), full),
+            pltpu.VMEM((128, rows), full),
+            pltpu.VMEM((rows, 128), full),
             pltpu.SemaphoreType.DMA((3, count)),
             pltpu.SemaphoreType.DMA((3, count)),
             pltpu.SemaphoreType.DMA((2,)),
@@ -1432,7 +1463,7 @@
 
 class Sums(Links):
     def __init__(self, dims, units, buffers, totals, sems, free_sem):
-        super().__init__(dims)
+        super().__init__(dims, SUM_RATE)
         self.units, self.totals, self.buffers = units, totals, buffers
         self.send_sem, self.recv_sem = sems
         self.free_sem = free_sem
@@ -2297,12 +2328,11 @@
     place_mat = (slots[:, None] == bucket_rows.reshape(-1)[None, :]) & keep[:, None]
     place_mat = place_mat.astype(jnp.bfloat16)
     hits = marks.astype(jnp.bfloat16)
-    table_low = entity_table.astype(jnp.bfloat16)
     flat_targets = targets.reshape(-1)
     local_targets = flat_targets - lax.axis_index(("dp", "mp")) * shard_rows
     local_targets = jnp.broadcast_to(local_targets[None, :], (8, flat_targets.shape[0]))
-    wholes, saved_layers, ents, gain_rows, entity_rows, got = run_forward(
-        dims, word_inputs, entity_base, requests, place_mat, table_low, shards, 6
+    wholes, saved_layers, ents, gain_rows, entity_rows, got, table_low = run_forward(
+        dims, word_inputs, entity_base, requests, place_mat, entity_table, shards, 6
     )
     losses, grad_logits, states, grad_head, grad_ents = run_head(
         dims, ents, hits, wholes[5][0], table_low, local_targets, 7

time: 474 us -> 459 us (0.968)
  Pallas kernels: 448 us -> 438 us
    pallas_call x1, Pallas kernels: 39.1 us -> 32.3 us  [run_head(): pl.pallas_call(functools.partial(head_body, count), out_shape=[jax.ShapeD...]
where the time goes in v6:
time: 459 us; the launch traced here: 454 us
  Pallas kernels  438 us (95%)
  local copies, waits for them, and re-layouts  8.2 us (2%)
  other arithmetic  6.96 us (2%)
    pallas_call x1, Pallas kernels, run_forward(): pl.pallas_call(functools.partial(forward_body, dims, chunks, needs), out_...  195 us
    pallas_call x1, Pallas kernels, run_backward(): pl.pallas_call(functools.partial(backward_body, dims, names, orders, half...  193 us
    pallas_call x1, Pallas kernels, run_head(): pl.pallas_call(functools.partial(head_body, count), out_shape=[jax.ShapeD...  32.3 us
    pallas_call x1, Pallas kernels, run_update(): pl.pallas_call(functools.partial(update_body, names, width), out_shape=[j...  17.6 us

profile of v6, /device:TPU:0, one launch (start us, length us, event | category | flops | bytes accessed | tf_op | source)
XLA Modules:
  0.0 453.9 jit_solution(8130470483457941670)
XLA Ops:
  0.7 0.0 copy-start
  0.7 0.7 convert.5
  1.4 0.6 pad.5.refs_11_
  2.0 0.7 broadcast_maximum_fusion
  2.7 0.1 copy.64
  2.7 0.1 reshape.106
  2.9 0.0 copy-start.11
  3.0 1.2 gather_fusion
  4.2 0.7 fusion.2
  4.9 0.1 reshape.115
  5.0 0.1 copy.65
  5.1 0.1 copy.69
  5.2 0.1 sub.15
  5.2 0.6 broadcast_in_dim.14.refs_4_
  5.9 0.1 copy.70
  5.9 0.1 eq.33
  6.0 0.6 convert_bitcast_fusion.1.refs_9_
  6.6 0.6 convert_bitcast_fusion.refs_10_
  7.2 0.7 fusion.1.refs_3_.refs_5_
  8.0 0.7 broadcast_in_dim.13.refs_2_
  8.7 0.6 bitcast_convert_fusion.1.refs_6_
  9.3 0.7 convert_element_type.37.refs_7_
  10.1 0.7 bitcast_convert_fusion.refs_8_
  10.8 0.8 convert_element_type.34
  11.6 194.7 %shard_map.494 = (bf16[12,4,2,2,48,384]{5,4,3,2,1,0:T(8,128)(2,1)}, bf16[2,4,2,2,48,384]{5,4,3,2,1,0:T(8,128)(2,1)}, bf16[2,4,2,2,48,1536]{5,4,3,2,1,0:T(8,128)(...) custom-call(bf16[896,768]{1,0:T(8,128)(2,1)} %refs_0_.3, ...), custom_call_target="tpu_custom_call" | custom-call | tf_op jit(solution)/shard_map/pallas_call | solution.py:1052
  206.3 0.9 slice_reduce_fusion
  207.3 0.6 broadcast_in_dim.16.refs_46_
  207.9 32.3 %shard_map.495 = (f32[8,256]{1,0:T(8,128)}, bf16[3968,256]{1,0:T(8,128)(2,1)}, bf16[256,256]{1,0:T(8,128)(2,1)}, bf16[4,2,2,48,256]{4,3,2,1,0:T(8,128)(2,1)}, f32[128,768]{1,0:T(8,128)}) custom-call(f32[128,768]{1,0:T(8,128)} %get-tuple-element.113.refs_0_, bf16[16,128]{1,0:T(8,128)(2,1)} %get-tuple-element.200.refs_1_, ...), custom_call_target="tpu_custom_call" | custom-call | tf_op jit(solution)/shard_map/pallas_call | solution.py:1277
  240.3 192.9 %shard_map.496 = (f32[896,768]{1,0:T(8,128)}, f32[128,256]{1,0:T(8,128)}, f32[48,256]{1,0:T(8,128)}, f32[48,768]{1,0:T(8,128)}, f32[48,768]{1,0:T(8,128)}, /*ind...) custom-call(bf16[896,768]{1,0:T(8,128)(2,1)} %refs_0_.4, ...), custom_call_target="tpu_custom_call" | custom-call | tf_op jit(solution)/shard_map/pallas_call | solution.py:1899
  433.2 1.3 slice.6
  434.5 17.6 %shard_map.497 = (f32[2,6,48,384]{3,2,1,0:T(8,128)}, f32[2,6,48,384]{3,2,1,0:T(8,128)}, f32[2,6,48,384]{3,2,1,0:T(8,128)}, f32[2,48,384]{2,1,0:T(8,128)}, f32[2,...) custom-call(f32[2,6,48,384]{3,2,1,0:T(8,128)} %refs_0_.5, ...), custom_call_target="tpu_custom_call" | custom-call | tf_op jit(solution)/shard_map/pallas_call | solution.py:1438
  452.1 1.5 copy.72
  (27 shorter events, 0.1 us)
Async XLA Ops:
  0.7 2.2 copy-start
  2.9 1.4 copy-start.11
  2.9 2.2 copy-start.9
  2.9 2.3 copy-start.10
  2.9 3.1 copy-start.7
  2.9 3.7 copy-start.8
  2.9 5.7 %copy-start.6 = (f32[2,384,48]{1,2,0:T(8,128)S(1)}, f32[2,384,48]{1,2,0:T(8,128)}, u32[]{:S(2)}) copy-start(f32[2,384,48]{1,2,0:T(8,128)} %param.41) | copy-start | bytes 442372
  2.9 6.4 %copy-start.4 = (f32[2,48,1536]{2,1,0:T(8,128)S(1)}, f32[2,48,1536]{2,1,0:T(8,128)}, u32[]{:S(2)}) copy-start(f32[2,48,1536]{2,1,0:T(8,128)} %refs_6_.1) | copy-start | bytes 1769476
  2.9 7.1 %copy-start.5 = (f32[2,1536,48]{1,2,0:T(8,128)S(1)}, f32[2,1536,48]{1,2,0:T(8,128)}, u32[]{:S(2)}) copy-start(f32[2,1536,48]{1,2,0:T(8,128)} %param.47) | copy-start | bytes 1769476
  4.2 6.6 %copy-start.2 = (f32[2,6,48,384]{3,2,1,0:T(8,128)S(1)}, f32[2,6,48,384]{3,2,1,0:T(8,128)}, u32[]{:S(2)}) copy-start(f32[2,6,48,384]{3,2,1,0:T(8,128)} %refs_0_.5) | copy-start | bytes 2654212
  434.5 17.7 %copy-start.3 = (f32[896,768]{1,0:T(8,128)S(1)}, f32[896,768]{1,0:T(8,128)}, u32[]{:S(2)}) copy-start(f32[896,768]{1,0:T(8,128)} %get-tuple-element.229) | copy-start | bytes 8257540
  452.1 1.6 copy-start.1

commit v7 on v6

--- a/solution.py
+++ b/solution.py
@@ -606,7 +606,7 @@
 
 
 GATHER_RATE = 52000.0
-SUM_RATE = 45000.0
+SUM_RATE = 40000.0
 HOP_US = 1.5
 ORDERS = ((0, 1, 2), (0, 2, 1), (2, 0, 1), (1, 0, 2))
 

time: 459 us -> 462 us (level)
  no operation moved by 1% of the time
where the time goes in v7:
time: 462 us; the launch traced here: 456 us
  Pallas kernels  440 us (95%)
  local copies, waits for them, and re-layouts  8.2 us (2%)
  other arithmetic  6.96 us (2%)
    pallas_call x1, Pallas kernels, run_backward(): pl.pallas_call(functools.partial(backward_body, dims, names, orders, half...  195 us
    pallas_call x1, Pallas kernels, run_forward(): pl.pallas_call(functools.partial(forward_body, dims, chunks, needs), out_...  195 us
    pallas_call x1, Pallas kernels, run_head(): pl.pallas_call(functools.partial(head_body, count), out_shape=[jax.ShapeD...  32.3 us
    pallas_call x1, Pallas kernels, run_update(): pl.pallas_call(functools.partial(update_body, names, width), out_shape=[j...  17.6 us

profile of v7, /device:TPU:0, one launch (start us, length us, event | category | flops | bytes accessed | tf_op | source)
XLA Modules:
  0.0 456.1 jit_solution(13758627975724953890)
XLA Ops:
  0.7 0.0 copy-start
  0.7 0.7 convert.5
  1.4 0.6 pad.5.refs_11_
  2.0 0.7 broadcast_maximum_fusion
  2.7 0.1 copy.64
  2.7 0.1 reshape.106
  2.9 0.0 copy-start.11
  3.0 1.2 gather_fusion
  4.2 0.7 fusion.2
  4.9 0.1 reshape.115
  5.0 0.1 copy.65
  5.1 0.1 copy.69
  5.2 0.1 sub.15
  5.2 0.6 broadcast_in_dim.14.refs_4_
  5.9 0.1 copy.70
  5.9 0.1 eq.33
  6.0 0.6 convert_bitcast_fusion.1.refs_9_
  6.6 0.6 convert_bitcast_fusion.refs_10_
  7.2 0.7 fusion.1.refs_3_.refs_5_
  8.0 0.7 broadcast_in_dim.13.refs_2_
  8.7 0.6 bitcast_convert_fusion.1.refs_6_
  9.3 0.7 convert_element_type.37.refs_7_
  10.1 0.7 bitcast_convert_fusion.refs_8_
  10.8 0.8 convert_element_type.34
  11.6 194.7 %shard_map.494 = (bf16[12,4,2,2,48,384]{5,4,3,2,1,0:T(8,128)(2,1)}, bf16[2,4,2,2,48,384]{5,4,3,2,1,0:T(8,128)(2,1)}, bf16[2,4,2,2,48,1536]{5,4,3,2,1,0:T(8,128)(...) custom-call(bf16[896,768]{1,0:T(8,128)(2,1)} %refs_0_.3, ...), custom_call_target="tpu_custom_call" | custom-call | tf_op jit(solution)/shard_map/pallas_call | solution.py:1052
  206.3 0.9 slice_reduce_fusion
  207.3 0.6 broadcast_in_dim.16.refs_46_
  207.9 32.3 %shard_map.495 = (f32[8,256]{1,0:T(8,128)}, bf16[3968,256]{1,0:T(8,128)(2,1)}, bf16[256,256]{1,0:T(8,128)(2,1)}, bf16[4,2,2,48,256]{4,3,2,1,0:T(8,128)(2,1)}, f32[128,768]{1,0:T(8,128)}) custom-call(f32[128,768]{1,0:T(8,128)} %get-tuple-element.113.refs_0_, bf16[16,128]{1,0:T(8,128)(2,1)} %get-tuple-element.200.refs_1_, ...), custom_call_target="tpu_custom_call" | custom-call | tf_op jit(solution)/shard_map/pallas_call | solution.py:1277
  240.3 195.1 %shard_map.496 = (f32[896,768]{1,0:T(8,128)}, f32[128,256]{1,0:T(8,128)}, f32[48,256]{1,0:T(8,128)}, f32[48,768]{1,0:T(8,128)}, f32[48,768]{1,0:T(8,128)}, /*ind...) custom-call(bf16[896,768]{1,0:T(8,128)(2,1)} %refs_0_.4, ...), custom_call_target="tpu_custom_call" | custom-call | tf_op jit(solution)/shard_map/pallas_call | solution.py:1899
  435.4 1.3 slice.6
  436.6 17.6 %shard_map.497 = (f32[2,6,48,384]{3,2,1,0:T(8,128)}, f32[2,6,48,384]{3,2,1,0:T(8,128)}, f32[2,6,48,384]{3,2,1,0:T(8,128)}, f32[2,48,384]{2,1,0:T(8,128)}, f32[2,...) custom-call(f32[2,6,48,384]{3,2,1,0:T(8,128)} %refs_0_.5, ...), custom_call_target="tpu_custom_call" | custom-call | tf_op jit(solution)/shard_map/pallas_call | solution.py:1438
  454.3 1.5 copy.72
  (27 shorter events, 0.1 us)
Async XLA Ops:
  0.7 2.2 copy-start
  2.9 1.4 copy-start.11
  2.9 2.2 copy-start.9
  2.9 2.3 copy-start.10
  2.9 3.1 copy-start.7
  2.9 3.7 copy-start.8
  2.9 5.7 %copy-start.6 = (f32[2,384,48]{1,2,0:T(8,128)S(1)}, f32[2,384,48]{1,2,0:T(8,128)}, u32[]{:S(2)}) copy-start(f32[2,384,48]{1,2,0:T(8,128)} %param.41) | copy-start | bytes 442372
  2.9 6.4 %copy-start.4 = (f32[2,48,1536]{2,1,0:T(8,128)S(1)}, f32[2,48,1536]{2,1,0:T(8,128)}, u32[]{:S(2)}) copy-start(f32[2,48,1536]{2,1,0:T(8,128)} %refs_6_.1) | copy-start | bytes 1769476
  2.9 7.1 %copy-start.5 = (f32[2,1536,48]{1,2,0:T(8,128)S(1)}, f32[2,1536,48]{1,2,0:T(8,128)}, u32[]{:S(2)}) copy-start(f32[2,1536,48]{1,2,0:T(8,128)} %param.47) | copy-start | bytes 1769476
  4.2 6.6 %copy-start.2 = (f32[2,6,48,384]{3,2,1,0:T(8,128)S(1)}, f32[2,6,48,384]{3,2,1,0:T(8,128)}, u32[]{:S(2)}) copy-start(f32[2,6,48,384]{3,2,1,0:T(8,128)} %refs_0_.5) | copy-start | bytes 2654212
  436.6 17.7 %copy-start.3 = (f32[896,768]{1,0:T(8,128)S(1)}, f32[896,768]{1,0:T(8,128)}, u32[]{:S(2)}) copy-start(f32[896,768]{1,0:T(8,128)} %get-tuple-element.229) | copy-start | bytes 8257540
  454.3 1.6 copy-start.1
